TPU v7x, 32 devices: a whole 2x2x4 slice. The times are simulated.
32 devices in a mesh: group: 4 (over y, x), member: 8 (over z, core).
Axes of the slice: x: 2, y: 2, z: 4, core: 2. Of those that a mesh axis runs over, the one named last changes fastest.
Arguments:
- tokens: bfloat16 [4096, 2048], P(('group', 'member')), may hold values from -6 to 6
- cotangent: bfloat16 [4096, 2048], P(('group', 'member')), may hold values from -6 to 6
- w_gate: bfloat16 [2048, 512], P('member'), may hold values from -0.125 to 0.125
- w_up: bfloat16 [2048, 512], P('member'), may hold values from -0.125 to 0.125
- w_down: bfloat16 [2048, 512], P('member'), may hold values from -0.125 to 0.125
- basis: float32 [2048, 256], P('member'), may hold values from -0.088388348 to 0.088388348
- first_moment: float32 [3, 256, 512], P(None, 'member'), may hold values from -3 to 3
- second_moment: float32 [3, 256, 512], P(None, 'member'), may hold values from 0.1 to 2
Outputs:
- input_grad: bfloat16 [4096, 2048], P(('group', 'member'))
- new_first: float32 [3, 256, 512], P(None, 'member')
- new_second: float32 [3, 256, 512], P(None, 'member')
- updates: float32 [3, 2048, 512], P(None, 'member')
All inputs are finite; a program needn't handle non-finite values.
Results may differ from a plain program's by a relative error of at most 0.008.
Values may be sent and summed in bfloat16 or wider, within the bound.
No kernel may reach another device: no remote copies, remote signals or barrier semaphores. Data moves between devices by JAX's collectives and lax.ppermute only.
A program may use at most 64 MiB of HBM per device.

v0:
```python
import math

import jax
import jax.numpy as jnp
from jax import lax
from jax.sharding import PartitionSpec as P

FF = 512
RANK = 256


def contract_rows(left, right):
    return lax.dot_general(
        left, right, (((0,), (0,)), ((), ())), preferred_element_type=jnp.float32
    )


def contract_cols(left, right):
    return lax.dot_general(
        left, right, (((1,), (1,)), ((), ())), preferred_element_type=jnp.float32
    )


def split_parts(values):
    high_part = values.astype(jnp.bfloat16)
    low_part = (values - high_part.astype(jnp.float32)).astype(jnp.bfloat16)
    return (high_part, low_part)


def local(tokens, cotangent, w_gate, w_up, w_down, basis, first_moment, second_moment):
    pieces = (
        lax.all_gather(w_gate, "member", axis=0, tiled=True),
        lax.all_gather(w_up, "member", axis=0, tiled=True),
        lax.all_gather(w_down, "member", axis=0, tiled=True),
    )
    gate = jnp.dot(tokens, pieces[0], preferred_element_type=jnp.float32)
    up = jnp.dot(tokens, pieces[1], preferred_element_type=jnp.float32)
    dhid = jnp.dot(cotangent, pieces[2], preferred_element_type=jnp.float32)
    sig = jax.nn.sigmoid(gate)
    silu = gate * sig
    hidden = (silu * up).astype(jnp.bfloat16)
    dgate = (dhid * up * sig * (1.0 + gate * (1.0 - sig))).astype(jnp.bfloat16)
    dup = (dhid * silu).astype(jnp.bfloat16)
    pieces = lax.all_gather((w_gate, w_up), "member", axis=0, tiled=True)
    dx_full = contract_cols(dgate, pieces[0]) + contract_cols(dup, pieces[1])
    input_grad = dx_full.astype(jnp.bfloat16)
    full_basis = lax.all_gather(basis, "member", axis=0, tiled=True)
    highest = lax.Precision.HIGHEST
    basis_high, basis_low = split_parts(full_basis)
    x_proj = jnp.dot(tokens, basis_high, preferred_element_type=jnp.float32) + jnp.dot(
        tokens, basis_low, preferred_element_type=jnp.float32
    )
    y_proj = jnp.dot(cotangent, basis_high, preferred_element_type=jnp.float32) + jnp.dot(
        cotangent, basis_low, preferred_element_type=jnp.float32
    )
    x_high, x_low = split_parts(x_proj)
    y_high, y_low = split_parts(y_proj)
    low_gate = contract_rows(x_high, dgate) + contract_rows(x_low, dgate)
    low_up = contract_rows(x_high, dup) + contract_rows(x_low, dup)
    low_down = contract_rows(y_high, hidden) + contract_rows(y_low, hidden)
    local_low = jnp.stack([low_gate, low_up, low_down])
    partial_rows = lax.psum_scatter(local_low, "member", scatter_dimension=1, tiled=True)
    share = lax.psum(partial_rows, "group")
    squares = lax.psum(jnp.sum(share * share), "member")
    limit = math.sqrt(3.0 * RANK * FF)
    factor = jnp.minimum(1.0, limit / jnp.sqrt(squares + 1e-06))
    grad_low = factor * share
    new_first = 0.5 * first_moment + 0.5 * grad_low
    new_second = 0.9 * second_moment + 0.1 * grad_low * grad_low
    step = (new_first / (jnp.sqrt(new_second) + 1e-08)).astype(jnp.bfloat16)
    updates = jnp.einsum(
        "dr,krf->kdf",
        basis,
        lax.all_gather(step, "member", axis=1, tiled=True).astype(jnp.float32),
        precision=highest,
    )
    return (input_grad, new_first, new_second, updates)


def solution(mesh):
    placed = (
        P(("group", "member"), None),
        P(("group", "member"), None),
        P("member", None),
        P("member", None),
        P("member", None),
        P("member", None),
        P(None, "member", None),
        P(None, "member", None),
    )
    return jax.shard_map(
        local,
        mesh=mesh,
        in_specs=placed,
        out_specs=(
            P(("group", "member"), None),
            P(None, "member", None),
            P(None, "member", None),
            P(None, "member", None),
        ),
        check_vma=False,
    )
```

profile of v0, /device:TPU:0, one launch (start us, length us, event | category | flops | bytes accessed | tf_op | source)
XLA Modules:
  0.0 263.1 jit_solution(16964054385228106456)
XLA Ops:
  7.2 0.7 all-gather.11.cloned.1.call-update
  8.0 0.7 all-gather.5.cloned.1.call-update
  8.7 0.7 all-gather.9.cloned.1.call-update
  9.5 0.5 all-gather.7.cloned.1.call-update
  10.0 31.4 %all-gather.11.cloned.1.call-done = f32[2048,256]{1,0:T(8,128)} async-done(((f32[256,256]{1,0:T(8,128)}), f32[2048,256]{1,0:T(8,128)}) %all-gather.11.cloned.1.call-update) | async-done | bytes 2097168 | tf_op jit(solution)/shard_map/all_gather | solution.py:47
  41.5 2.1 fusion.16
  43.6 28.1 %all-gather.5.cloned.1.call-done = bf16[2048,512]{1,0:T(8,128)(2,1)} async-done(((bf16[256,512]{1,0:T(8,128)(2,1)}), bf16[2048,512]{1,0:T(8,128)(2,1)}) %all-gather.5.cloned.1.call-update) | async-done | bytes 2097168 | tf_op jit(solution)/shard_map/all_gather | solution.py:34
  71.7 2.7 %fusion.21 = f32[128,512]{1,0:T(8,128)} fusion(bf16[128,2048]{1,0:T(8,128)(2,1)S(1)} %copy-done.3, bf16[2048,512]{1,0:T(8,128)(2,1)} %all-gather.5.cloned.1.call-done), kind=kOutput, calls=%fused_computation.39 | convolution fusion | flops 268435456 | bytes 2883584 | tf_op jit(solution)/shard_map/dot_general | solution.py:38
  74.4 0.3 fusion.4
  74.8 27.2 %all-gather.9.cloned.1.call-done = bf16[2048,512]{1,0:T(8,128)(2,1)} async-done(((bf16[256,512]{1,0:T(8,128)(2,1)}), bf16[2048,512]{1,0:T(8,128)(2,1)}) %all-gather.9.cloned.1.call-update) | async-done | bytes 2097168 | tf_op jit(solution)/shard_map/all_gather | solution.py:32
  101.9 2.0 fusion.22
  104.0 28.0 %all-gather.7.cloned.1.call-done = bf16[2048,512]{1,0:T(8,128)(2,1)} async-done(((bf16[256,512]{1,0:T(8,128)(2,1)}), bf16[2048,512]{1,0:T(8,128)(2,1)}) %all-gather.7.cloned.1.call-update) | async-done | bytes 2097168 | tf_op jit(solution)/shard_map/all_gather | solution.py:33
  132.0 2.1 multiply_convert_fusion
  134.1 0.2 fusion.10
  134.3 0.3 fusion.1
  134.6 0.3 fusion.18
  134.9 0.3 fusion.5
  135.2 0.2 fusion.12
  135.5 0.3 fusion.2
  135.7 0.2 fusion.14
  136.0 0.3 fusion.3
  136.3 1.3 pad_maximum_fusion
  137.6 33.6 %reduce-scatter.2.cloned.1.call-done = f32[3,32,512]{2,1,0:T(8,128)} async-done(((f32[3,256,512]{2,1,0:T(8,128)}), f32[3,32,512]{2,1,0:T(8,128)}) %reduce-scatter.2.cloned.1.call-update) | async-done | bytes 196624 | tf_op jit(solution)/shard_map/reduce_scatter | solution.py:62
  171.3 1.8 fusion.23
  173.0 41.6 %all-reduce.2.cloned.1.call-done = f32[3,32,512]{2,1,0:T(8,128)} async-done(((f32[3,32,512]{2,1,0:T(8,128)}), f32[3,32,512]{2,1,0:T(8,128)}) %all-reduce.2.cloned.1.call-update) | async-done | bytes 196624 | tf_op jit(solution)/shard_map/psum | solution.py:63
  214.7 1.7 multiply_reduce_fusion
  216.3 3.5 %fusion = bf16[128,2048]{1,0:T(8,128)(2,1)} fusion(f32[128,2048]{1,0:T(8,128)} %fusion.23, bf16[128,512]{1,0:T(8,128)(2,1)S(1)} %get-tuple-element.13, bf16[2048,512]{1,0:T(8,128)(2,1)} %all-gather.7.cloned.1.call-done), kind=kOutput, calls=%fused_computation.1 | convolution fusion | flops 268959744 | bytes 3801088 | tf_op jit(solution)/shard_map/dot_general | solution.py:19
  219.8 16.6 %psum.15 = f32[]{:T(128)} all-reduce(f32[]{:T(128)} %multiply_reduce_fusion), channel_id=1, replica_groups=mesh['group'=4,'member'=8] {'member'}, use_global_device_ids=true, to_apply=%region_3.0 | all-reduce | flops 1 | bytes 8 | tf_op jit(solution)/shard_map/psum | solution.py:64
  237.1 0.9 divide_convert_fusion
  237.9 15.8 %all_gather.21 = bf16[3,256,512]{2,1,0:T(8,128)(2,1)S(1)} all-gather(bf16[3,32,512]{2,1,0:T(8,128)(2,1)S(1)} %get-tuple-element.8), channel_id=1, replica_groups=mesh['group'=4,'member'=8] {'member'}, dimensions={1}, use_global_device_ids=true | all-gather | bytes 884736 | tf_op jit(solution)/shard_map/all_gather | solution.py:74
  253.7 0.9 convolution_bitcast_fusion
  254.7 1.6 copy.14
  (26 shorter events, 0.3 us)
Async XLA Ops:
  7.2 94.8 %copy-start = (bf16[128,2048]{1,0:T(8,128)(2,1)S(1)}, bf16[128,2048]{1,0:T(8,128)(2,1)}, u32[]{:S(2)}) copy-start(bf16[128,2048]{1,0:T(8,128)(2,1)} %param.8) | copy-start | bytes 1572868
  7.2 64.5 %copy-start.3 = (bf16[128,2048]{1,0:T(8,128)(2,1)S(1)}, bf16[128,2048]{1,0:T(8,128)(2,1)}, u32[]{:S(2)}) copy-start(bf16[128,2048]{1,0:T(8,128)(2,1)} %param.9) | copy-start | bytes 1572868
  7.2 34.3 %all-gather.11.cloned.1.call-start = ((), (), s32[]{:S(2)}) async-start(), calls=%async_computation.4 | async-start | bytes 2359296 | tf_op jit(solution)/shard_map/all_gather | solution.py:47
  7.9 63.8 %all-gather.5.cloned.1.call-start = ((), (), s32[]{:S(2)}) async-start(), calls=%async_computation.1 | async-start | bytes 2359296 | tf_op jit(solution)/shard_map/all_gather | solution.py:34
  8.7 93.2 %all-gather.9.cloned.1.call-start = ((), (), s32[]{:S(2)}) async-start(), calls=%async_computation.3 | async-start | bytes 2359296 | tf_op jit(solution)/shard_map/all_gather | solution.py:32
  9.4 122.6 %all-gather.7.cloned.1.call-start = ((), (), s32[]{:S(2)}) async-start(), calls=%async_computation.2 | async-start | bytes 2359296 | tf_op jit(solution)/shard_map/all_gather | solution.py:33
  10.0 161.2 %reduce-scatter.2.cloned.1.call-start = ((), (), s32[]{:S(2)}) async-start(), calls=%async_computation.5 | async-start | bytes 1769472 | tf_op jit(solution)/shard_map/reduce_scatter | solution.py:62
  43.5 30.9 %copy-start.1 = (f32[2048,256]{1,0:T(8,128)S(1)}, f32[2048,256]{1,0:T(8,128)}, u32[]{:S(2)}) copy-start(f32[2048,256]{1,0:T(8,128)} %all-gather.11.cloned.1.call-done) | copy-start | bytes 6291460
  74.8 57.3 %copy-start.6 = (f32[128,512]{1,0:T(8,128)S(1)}, f32[128,512]{1,0:T(8,128)}, u32[]{:S(2)}) copy-start(f32[128,512]{1,0:T(8,128)} %fusion.21) | copy-start | bytes 786436
  136.3 35.0 %copy-start.2 = (bf16[2048,512]{1,0:T(8,128)(2,1)S(1)}, bf16[2048,512]{1,0:T(8,128)(2,1)}, u32[]{:S(2)}) copy-start(bf16[2048,512]{1,0:T(8,128)(2,1)} %all-gather.9.cloned.1.call-done) | copy-start | bytes 6291460
  137.5 77.1 %all-reduce.2.cloned.1.call-start = ((), (), s32[]{:S(2)}) async-start(), calls=%async_computation.6 | async-start | bytes 393216 | tf_op jit(solution)/shard_map/psum | solution.py:63
  173.0 64.0 %copy-start.7 = (f32[3,32,512]{2,1,0:T(8,128)S(1)}, f32[3,32,512]{2,1,0:T(8,128)}, u32[]{:S(2)}) copy-start(f32[3,32,512]{2,1,0:T(8,128)} %param.15) | copy-start | bytes 589828
  173.0 64.0 %copy-start.8 = (f32[3,32,512]{2,1,0:T(8,128)S(1)}, f32[3,32,512]{2,1,0:T(8,128)}, u32[]{:S(2)}) copy-start(f32[3,32,512]{2,1,0:T(8,128)} %param.14) | copy-start | bytes 589828
  214.7 22.4 %copy-start.5 = (f32[3,32,512]{2,1,0:T(8,128)S(1)}, f32[3,32,512]{2,1,0:T(8,128)}, u32[]{:S(2)}) copy-start(f32[3,32,512]{2,1,0:T(8,128)} %all-reduce.2.cloned.1.call-done) | copy-start | bytes 589828
  216.3 37.4 %copy-start.4 = (f32[256,256]{1,0:T(8,128)S(1)}, f32[256,256]{1,0:T(8,128)}, u32[]{:S(2)}) copy-start(f32[256,256]{1,0:T(8,128)} %param.13) | copy-start | bytes 786436
Sparse Core Ops, SparseCore 0:
  9.6 31.7 all-gather.10
  43.1 28.5 all-gather.4
  73.3 28.5 all-gather.8
  103.4 28.5 all-gather.6
  137.7 33.5 reduce-scatter.1
  174.0 40.6 all-reduce.1
where the time goes:
time: 263 us
  waiting for transfers between devices  193 us (73%)
  blocking collectives  32.3 us (12%)
  matrix products  17.6 us (7%)
  between operations  15 us (6%)
  other arithmetic  3.77 us (1%)
    psum x1, waiting for transfers between devices, local(): share = lax.psum(partial_rows, 'group')  41.6 us
    reduce_scatter x1, waiting for transfers between devices, local(): lax.psum_scatter(local_low, 'member', scatter_dimension=1, tiled=True)  33.6 us
    all_gather x1, waiting for transfers between devices, local(): full_basis = lax.all_gather(basis, 'member', axis=0, tiled=True)  31.4 us
    all_gather x1, waiting for transfers between devices, local(): lax.all_gather(w_down, 'member', axis=0, tiled=True)  28.1 us
    all_gather x1, waiting for transfers between devices, local(): lax.all_gather(w_up, 'member', axis=0, tiled=True)  28 us
    all_gather x1, waiting for transfers between devices, local(): lax.all_gather(w_gate, 'member', axis=0, tiled=True)  27.2 us
    psum x1, blocking collectives, local(): squares = lax.psum(jnp.sum(share * share), 'member')  16.6 us
    all_gather x1, blocking collectives, local(): lax.all_gather(step, 'member', axis=1, tiled=True).astype(jnp.float32)  15.8 us
  transfers between devices with their start and end apart: 6, of which 6 were waited for; matrix products, arithmetic and copies ran while one was open for 3% of the time, Pallas kernels for 0%

commit v1 on v0

v1 whole, which is shorter than its diff:
```python
import functools
import math

import jax
import jax.numpy as jnp
from jax import lax
from jax.experimental import pallas as pl
from jax.experimental.pallas import tpu as pltpu
from jax.sharding import PartitionSpec as P

BF = jnp.bfloat16
F32 = jnp.float32
ROWS = (((0,), (0,)), ((), ()))
COLS = (((1,), (1,)), ((), ()))


def dot(left, right, dims=(((1,), (0,)), ((), ()))):
    return lax.dot_general(left, right, dims, preferred_element_type=F32)


def whole(count):
    return [pl.BlockSpec(memory_space=pltpu.VMEM)] * count


def call(body, outs, scratch, flops, *operands):
    moved = sum(o.size * o.dtype.itemsize for o in operands)
    moved += sum(math.prod(s) * jnp.dtype(d).itemsize for s, d in outs)
    return pl.pallas_call(
        body,
        out_shape=[jax.ShapeDtypeStruct(s, d) for s, d in outs],
        in_specs=whole(len(operands)),
        out_specs=whole(len(outs)),
        scratch_shapes=scratch,
        compiler_params=pltpu.CompilerParams(vmem_limit_bytes=40 * 1024 * 1024),
        cost_estimate=pl.CostEstimate(
            flops=flops, bytes_accessed=moved, transcendentals=0
        ),
    )(*operands)


def places():
    group, member = lax.axis_index("group"), lax.axis_index("member")
    return group % 2, (group // 2) % 2, member // 2, member % 2, member


def sources(count):
    _, high, _, _, member = places()
    order = [member, member ^ 1]
    for k in range(1, count // 2):
        near = member ^ (2 * k) ^ high
        order += [near, near ^ 1]
    return order


def joined(refs):
    return jnp.concatenate([ref[...] for ref in refs], axis=0)


def place_blocks(members, blocks, full):
    depth = blocks[0].shape[0]
    for src, block in zip(sources(members), blocks):
        full[pl.ds(pl.multiple_of(src * depth, depth), depth), :] = block[...]


def first_kernel(members, *refs):
    toks, cots, blocks = refs[:4], refs[4:8], refs[8 : 8 + members]
    dhid_ref, proj_ref, full = refs[8 + members :]
    unit = dhid_ref.shape[1]
    half = proj_ref.shape[1] // 2
    place_blocks(members, blocks, full)
    from_cot = dot(joined(cots), full[...])
    dhid_ref[...] = from_cot[:, :unit]
    proj_ref[:, :half] = dot(joined(toks), full[:, unit:]).astype(BF)
    proj_ref[:, half:] = from_cot[:, unit:].astype(BF)


def second_kernel(members, *refs):
    chips = members // 2
    tok_refs, blocks = refs[:4], refs[4 : 4 + members]
    dhid_ref, mine_ref, other_ref = refs[4 + members : 7 + members]
    dgu_ref, *low_refs, low, full = refs[7 + members :]
    unit = dhid_ref.shape[1]
    half = mine_ref.shape[1] // 2
    _, _, chip, core, _ = places()
    place_blocks(members, blocks, full)
    total = dot(joined(tok_refs), full[...])
    gate, up, dhid = total[:, :unit], total[:, unit:], dhid_ref[...]
    sig = 1.0 / (1.0 + jnp.exp(-gate))
    silu = gate * sig
    hidden = (silu * up).astype(BF)
    dgate = (dhid * up * sig * (1.0 + gate * (1.0 - sig))).astype(BF)
    dup = (dhid * silu).astype(BF)
    dgu = jnp.concatenate([dgate, dup], axis=1)
    dgu_ref[...] = dgu
    toks = mine_ref.shape[0] // 4
    other = jnp.concatenate(
        [other_ref[i * toks : (i + 1) * toks, :] for i in (1, 0, 3, 2)], axis=0
    )
    for away, proj in enumerate((mine_ref[...], other)):
        rows = pl.ds(away * half, half)
        tok_low = dot(proj[:, :half], dgu, ROWS)
        low[0, rows, :] = tok_low[:, :unit]
        low[1, rows, :] = tok_low[:, unit:]
        low[2, rows, :] = dot(proj[:, half:], hidden, ROWS)
    height = low_refs[0].shape[1]
    for k, ref in enumerate(low_refs):
        row = (chip ^ k) * height
        row = (row // half ^ core) * half + row % half
        rows = pl.ds(pl.multiple_of(row, height), height)
        for i in range(ref.shape[0]):
            ref[i] = low[i, rows, :].astype(ref.dtype)


def grad_kernel(members, *refs):
    dgu_ref, blocks, full = refs[0], refs[1 : 1 + members], refs[-1]
    keep_0, keep_1, send_0, send_1 = refs[1 + members : 5 + members]
    toks = keep_0.shape[0]
    place_blocks(members, blocks, full)
    for i, ref in enumerate((keep_0, send_0, keep_1, send_1)):
        part = dot(dgu_ref[i * toks : (i + 1) * toks, :], full[...], COLS)
        ref[...] = part.astype(ref.dtype)


def last_kernel(chips, limit, *refs):
    lows, (core_low, moms, core_moms) = refs[:2], refs[2:5]
    basis_ref, first_ref, second_ref, new_first_ref, new_second_ref, upd_ref = refs[5:11]
    full, stepped = refs[11:]
    side, _, chip, core, member = places()
    height, unit = lows[0].shape[2:]
    pieces = []
    squares = None
    for dc in range(2):
        for dx in range(2):
            column = ((side ^ dx) * 2 + (core ^ dc)) * unit
            columns = pl.ds(pl.multiple_of(column, unit), unit)
            for k in range(chips):
                low = (core_low[dx, k] if dc else lows[dx][k]).astype(F32)
                square = jnp.sum(low * low, axis=(0, 1), keepdims=True)
                squares = square if squares is None else squares + square
                pieces.append((dc, dx, k, columns, low))
                rows = pl.ds(pl.multiple_of((chip ^ k) * height, height), height)
                full[:, rows, columns] = low
    total = jnp.sum(squares, axis=2, keepdims=True)
    factor = jnp.minimum(1.0, limit / jnp.sqrt(total + 1e-06))
    own_rows = first_ref.shape[1]
    mine = factor * full[:, pl.ds(pl.multiple_of(member * own_rows, own_rows), own_rows), :]
    new_first_ref[...] = 0.5 * first_ref[...] + 0.5 * mine
    new_second_ref[...] = 0.9 * second_ref[...] + 0.1 * mine * mine
    for dc, dx, k, columns, low in pieces:
        for dr in range(2):
            mom = core_moms[dx, k, dr] if dc else moms[dx, k, dr]
            row = ((chip ^ k) * 2 + (core ^ dc ^ dr)) * own_rows
            rows = pl.ds(pl.multiple_of(row, own_rows), own_rows)
            grad = factor * full[:, rows, columns]
            first = 0.5 * mom[0].astype(F32) + 0.5 * grad
            second = 0.9 * mom[1].astype(F32) + 0.1 * grad * grad
            stepped[:, rows, columns] = first / (jnp.sqrt(second) + 1e-08)
    basis = basis_ref[...]
    high = basis.astype(BF)
    rest = (basis - high.astype(F32)).astype(BF)
    for i in range(upd_ref.shape[0]):
        step = stepped[i].astype(BF)
        upd_ref[i] = dot(high, step) + dot(rest, step)


def local(sizes, tokens, cotangent, w_gate, w_up, w_down, basis, first_moment, second_moment):
    groups, members = sizes
    chips = members // 2
    toks, width = tokens.shape
    depth, hidden_size = w_gate.shape
    rank = basis.shape[1]
    unit, half = hidden_size // 4, rank // 2
    own_rows = first_moment.shape[1]
    limit = math.sqrt(first_moment.shape[0] * rank * hidden_size)

    def by_member(value, bits):
        return lax.ppermute(value, "member", [(i, i ^ bits) for i in range(members)])

    def by_group(value, bits):
        return lax.ppermute(value, "group", [(i, i ^ bits) for i in range(groups)])

    def by_chip(value, bits):
        pairs = []
        for g in range(groups):
            for i in range(members):
                j = i ^ bits ^ ((g // 2) % 2)
                pairs.append((g * members + i, g * members + j))
        return lax.ppermute(value, ("group", "member"), pairs)

    side, high, chip, core, member = places()

    def cut(value, column, size):
        return lax.dynamic_slice_in_dim(value, column, size, axis=value.ndim - 1)

    low_basis = basis.astype(BF)

    def block_a(which):
        return jnp.concatenate(
            [cut(w_down, (2 * side + which) * unit, unit), cut(low_basis, which * half, half)],
            axis=1,
        )

    def block_b(which):
        column = (2 * side + which) * unit
        return jnp.concatenate([cut(w_gate, column, unit), cut(w_up, column, unit)], axis=1)

    def spread(block):
        sent = block(core ^ high)
        near = {}
        for k in range(1, chips):
            bit = k & -k
            near[k] = by_chip(sent, 2 * k) if k == bit else by_member(near[k ^ bit], 2 * bit)
        far = {k: by_group(near[k], 2) for k in near}
        out = [block(core), by_member(block(1 - core), 1)]
        for k in range(1, chips):
            out += [near[k], far[k]]
        return out

    cot_x = by_group(cotangent, 1)
    blocks_a = spread(block_a)
    tok_x = by_group(tokens, 1)
    blocks_b = spread(block_b)
    cot_c, tok_c = by_member(cotangent, 1), by_member(tokens, 1)
    cot_xc, tok_xc = by_member(cot_x, 1), by_member(tok_x, 1)
    token_blocks = (tokens, tok_c, tok_x, tok_xc)
    cot_blocks = (cotangent, cot_c, cot_x, cot_xc)

    moments = jnp.stack([first_moment, second_moment]).astype(BF)
    mom_mine = cut(moments, (2 * side + core) * unit, unit)
    mom_core = by_member(cut(moments, (2 * side + 1 - core) * unit, unit), 1)
    mom_chip = jnp.stack([mom_mine, mom_core])
    mom_half = jnp.stack([mom_chip] + [by_member(mom_chip, 2 * k) for k in range(1, chips)])
    moms = jnp.stack([mom_half, by_group(mom_half, 1)])
    core_moms = by_member(moms, 1)

    four = 4 * toks
    dhid, proj = call(
        functools.partial(first_kernel, members),
        [((four, unit), F32), ((four, 2 * half), BF)],
        [pltpu.VMEM((width, unit + half), BF)],
        2 * four * width * (2 * half + unit),
        *token_blocks,
        *cot_blocks,
        *blocks_a,
    )
    proj_core = by_member(proj, 1)
    height = rank // chips
    piece = (3, height, unit)
    dgu, *lows = call(
        functools.partial(second_kernel, members),
        [((four, 2 * unit), BF)] + [(piece, BF if k else F32) for k in range(chips)],
        [pltpu.VMEM((3, rank, unit), F32), pltpu.VMEM((width, 2 * unit), BF)],
        2 * four * (width * 2 * unit + 3 * rank * unit),
        *token_blocks,
        *blocks_b,
        dhid,
        proj,
        proj_core,
    )
    share = lows[0]
    for k in range(1, chips):
        share = share + by_member(lows[k], 2 * k).astype(F32)
    bit = 2
    while bit < groups:
        sent = share.astype(BF)
        share = sent.astype(F32) + by_group(sent, bit).astype(F32)
        bit *= 2
    share = share.astype(BF)

    keep_0, keep_1, send_0, send_1 = call(
        functools.partial(grad_kernel, members),
        [((toks, width), F32)] * 2 + [((toks, width), BF)] * 2,
        [pltpu.VMEM((width, 2 * unit), BF)],
        2 * four * width * 2 * unit,
        dgu,
        *blocks_b,
    )
    near_part = keep_1 + by_member(send_1, 1).astype(F32)
    mine_part = keep_0 + by_member(send_0, 1).astype(F32)
    input_grad = (mine_part + by_group(near_part.astype(BF), 1).astype(F32)).astype(BF)

    low_mine = jnp.stack([share] + [by_member(share, 2 * k) for k in range(1, chips)])
    low_side = by_group(low_mine, 1)
    low_core = by_member(jnp.stack([low_mine, low_side]), 1)
    new_first, new_second, updates = call(
        functools.partial(last_kernel, chips, limit),
        [(first_moment.shape, F32), (second_moment.shape, F32), ((3, depth, hidden_size), F32)],
        [pltpu.VMEM((3, rank, hidden_size), F32)] * 2,
        4 * 3 * depth * rank * hidden_size,
        low_mine,
        low_side,
        low_core,
        moms,
        core_moms,
        basis,
        first_moment,
        second_moment,
    )
    return (input_grad, new_first, new_second, updates)


def solution(mesh):
    sizes = (mesh.shape["group"], mesh.shape["member"])
    tokens = P(("group", "member"), None)
    rows = P("member", None)
    low = P(None, "member", None)
    return jax.shard_map(
        functools.partial(local, sizes),
        mesh=mesh,
        in_specs=(tokens, tokens, rows, rows, rows, rows, low, low),
        out_specs=(tokens, low, low, low),
        check_vma=False,
    )
```

time: 263 us -> 97.6 us (0.37)
  waiting for transfers between devices: 193 us -> 34 us
  starting transfers between devices: 0.23 us -> 44 us
  blocking collectives: 32.3 us -> 0 us
  matrix products: 17.6 us -> 0 us
  between operations: 15 us -> 0.9 us
  Pallas kernels: 0 us -> 8.9 us
  local copies, waits for them, and re-layouts: 1.66 us -> 7.08 us
    all_gather x4 -> x0, waiting for transfers between devices: 115 us -> none  [the longest x1 31.4 us: local(): full_basis = lax.all_gather(basis, 'member', axis=0, tiled=True)]
    ppermute x0 -> x39, starting transfers between devices: none -> 44 us  [the longest x23 18.5 us: by_member(): lax.ppermute(value, 'member', [(i, i ^ bits) for i in range(members)])]
    psum x1 -> x0, waiting for transfers between devices: 41.6 us -> none  [local(): share = lax.psum(partial_rows, 'group')]
    ppermute x0 -> x39, waiting for transfers between devices: none -> 34 us  [the longest x12 16.1 us: by_group(): return lax.ppermute(value, 'group', [(i, i ^ bits) for i in range(groups)])]
    reduce_scatter x1 -> x0, waiting for transfers between devices: 33.6 us -> none  [local(): lax.psum_scatter(local_low, 'member', scatter_dimension=1, tiled=True)]
    dot_general x16 -> x0, matrix products: 17.6 us -> none  [the longest x2 5.28 us: contract_cols(): lax.dot_general(left, right, (((1,), (1,)), ((), ())), preferred_element_...]
    psum x1 -> x0, blocking collectives: 16.6 us -> none  [local(): squares = lax.psum(jnp.sum(share * share), 'member')]
    all_gather x1 -> x0, blocking collectives: 15.8 us -> none  [local(): lax.all_gather(step, 'member', axis=1, tiled=True).astype(jnp.float32)]
  transfers between devices with their start and end apart: 6 -> 39, of which waited for: 6 -> 15; matrix products, arithmetic and copies ran while one was open for 3% -> 5% of each run, Pallas kernels for 0% -> 9%
where the time goes in v1:
time: 97.6 us; the launch traced here: 97.3 us
  starting transfers between devices  44 us (45%)
  waiting for transfers between devices  34 us (35%)
  Pallas kernels  8.9 us (9%)
  local copies, waits for them, and re-layouts  7.08 us (7%)
  other arithmetic  2.39 us (2%)
    ppermute x23, starting transfers between devices, by_member(): lax.ppermute(value, 'member', [(i, i ^ bits) for i in range(members)])  18.5 us
    ppermute x12, starting transfers between devices, by_group(): return lax.ppermute(value, 'group', [(i, i ^ bits) for i in range(groups)])  18.5 us
    ppermute x12, waiting for transfers between devices, by_group(): return lax.ppermute(value, 'group', [(i, i ^ bits) for i in range(groups)])  16.1 us
    ppermute x23, waiting for transfers between devices, by_member(): lax.ppermute(value, 'member', [(i, i ^ bits) for i in range(members)])  11.4 us
    pallas_call x4, Pallas kernels, call(): pl.pallas_call(body, out_shape=[jax.ShapeDtypeStruct(s, d) for s, d in ou...  8.9 us
    ppermute x4, starting transfers between devices, by_chip(): return lax.ppermute(value, ('group', 'member'), pairs)  6.94 us
    ppermute x4, waiting for transfers between devices, by_chip(): return lax.ppermute(value, ('group', 'member'), pairs)  6.52 us
    dynamic_slice x3, local copies, waits for them, and re-layouts, cut(): return lax.dynamic_slice_in_dim(value, column, size, axis=value.ndim - 1)  3.92 us
  transfers between devices with their start and end apart: 39, of which 15 were waited for; matrix products, arithmetic and copies ran while one was open for 5% of the time, Pallas kernels for 9%

profile of v1, /device:TPU:0, one launch (start us, length us, event | category | flops | bytes accessed | tf_op | source)
XLA Modules:
  0.0 97.3 jit_solution(1255985888593171987)
XLA Ops:
  0.7 3.0 %collective-permute-start.1 = (bf16[128,2048]{1,0:T(8,128)(2,1)}, bf16[128,2048]{1,0:T(8,128)(2,1)S(1)}, u32[]{:S(2)}, u32[]{:S(2)}) collective-permute-start(bf16[128,2048]{1,0:T(8,128)(2,1)} %refs_0_.3), channel_id=1, source_target_pairs={{0,8},{8,0},{16,24},{24,16},{1,9},{9,1},{17,25},{25,17},{2,10},{10... | collective-permute-start | bytes 1572872 | tf_op jit(solution)/shard_map/ppermute | solution.py:180
  3.8 1.6 %constant_dynamic-slice_fusion.7 = (bf16[256,128]{1,0:T(8,128)(2,1)S(1)}, bf16[256,128]{1,0:T(8,128)(2,1)}, bf16[256,128]{1,0:T(8,128)(2,1)}) fusion(bf16[256,512]{1,0:T(8,128)(2,1)} %param.10, s32[]{:T(128)S(6)} %select_n.53, s32[]{:T(128)S(6)} %select_n.49, s32[]{:T(128)S(6)} %select_n.50), kind=kLoop, calls=%fused_computation.31 | loop fusion | bytes 393228 | tf_op jit(solution)/shard_map/dynamic_slice | solution.py:193
  5.3 1.7 %constant_dynamic-slice_fusion.1 = (bf16[256,128]{1,0:T(8,128)(2,1)S(1)}, bf16[256,128]{1,0:T(8,128)(2,1)}, bf16[256,128]{1,0:T(8,128)(2,1)S(1)}, bf16[256,128]{...) fusion(bf16[256,512]{1,0:T(8,128)(2,1)} %param.12, s32[]{:T(128)S(6)} %select_n.53, ...), kind=kLoop, calls=%fused_computation.25 | loop fusion | bytes 786444 | tf_op jit(solution)/shard_map/dynamic_slice | solution.py:193
  7.0 3.1 %collective-permute-start.6 = (bf16[256,256]{1,0:T(8,128)(2,1)S(1)}, bf16[256,256]{1,0:T(8,128)(2,1)S(1)}, u32[]{:S(2)}, u32[]{:S(2)}) collective-permute-start(bf16[256,256]{1,0:T(8,128)(2,1)S(1)} %pad_maximum_fusion.6), channel_id=1, source_target_pairs={{0,4},{1,5},{2,6},{3,7},{4,0},{5,1},{6,2},{7,3},{8,12},{9,13},{10,... | collective-permute-start | bytes 393224 | tf_op jit(solution)/shard_map/ppermute | solution.py:188
  10.9 1.6 %collective-permute-start.14 = (bf16[256,256]{1,0:T(8,128)(2,1)S(1)}, bf16[256,256]{1,0:T(8,128)(2,1)S(1)}, u32[]{:S(2)}, u32[]{:S(2)}) collective-permute-start(bf16[256,256]{1,0:T(8,128)(2,1)S(1)} %pad_maximum_fusion.9), channel_id=1, source_target_pairs={{0,2},{1,3},{2,0},{3,1},{4,6},{5,7},{6,4},{7,5},{8,10},{9,11},{10,... | collective-permute-start | bytes 393224 | tf_op jit(solution)/shard_map/ppermute | solution.py:188
  12.9 4.6 %collective-permute-done.6.refs_8_.refs_5_ = bf16[256,256]{1,0:T(8,128)(2,1)S(1)} collective-permute-done((bf16[256,256]{1,0:T(8,128)(2,1)S(1)}, bf16[256,256]{1,0:T(8,128)(2,1)S(1)}, u32[]{:S(2)}, u32[]{:S(2)}) %collective-permute-start.6) | collective-permute-done | bytes 131104 | tf_op jit(solution)/shard_map/ppermute | solution.py:188
  17.5 2.2 %collective-permute-start.15 = (bf16[256,256]{1,0:T(8,128)(2,1)S(1)}, bf16[256,256]{1,0:T(8,128)(2,1)S(1)}, u32[]{:S(2)}, u32[]{:S(2)}) collective-permute-start(bf16[256,256]{1,0:T(8,128)(2,1)S(1)} %collective-permute-done.14.refs_10_), channel_id=1, source_target_pairs={{0,16},{8,24},{16,0},{24,8},{1,17},{9,25},{17,1},{25,9},{2,18},{10... | collective-permute-start | bytes 393224 | tf_op jit(solution)/shard_map/ppermute | solution.py:180
  19.8 1.9 %collective-permute-done.16.refs_12_ = bf16[256,256]{1,0:T(8,128)(2,1)} collective-permute-done((bf16[256,256]{1,0:T(8,128)(2,1)S(1)}, bf16[256,256]{1,0:T(8,128)(2,1)}, u32[]{:S(2)}, u32[]{:S(2)}) %collective-permute-start.16) | collective-permute-done | bytes 131104 | tf_op jit(solution)/shard_map/ppermute | solution.py:188
  21.6 2.5 %collective-permute-start.17 = (bf16[256,256]{1,0:T(8,128)(2,1)}, bf16[256,256]{1,0:T(8,128)(2,1)}, u32[]{:S(2)}, u32[]{:S(2)}) collective-permute-start(bf16[256,256]{1,0:T(8,128)(2,1)} %collective-permute-done.16.refs_12_), channel_id=1, source_target_pairs={{0,16},{8,24},{16,0},{24,8},{1,17},{9,25},{17,1},{25,9},{2,18},{10... | collective-permute-start | bytes 393224 | tf_op jit(solution)/shard_map/ppermute | solution.py:180
  29.0 4.4 %collective-permute-done.18.refs_14_ = bf16[256,256]{1,0:T(8,128)(2,1)S(1)} collective-permute-done((bf16[256,256]{1,0:T(8,128)(2,1)}, bf16[256,256]{1,0:T(8,128)(2,1)S(1)}, u32[]{:S(2)}, u32[]{:S(2)}) %collective-permute-start.18) | collective-permute-done | bytes 131104 | tf_op jit(solution)/shard_map/ppermute | solution.py:177
  33.4 1.7 %collective-permute-start.19 = (bf16[256,256]{1,0:T(8,128)(2,1)S(1)}, bf16[256,256]{1,0:T(8,128)(2,1)S(1)}, u32[]{:S(2)}, u32[]{:S(2)}) collective-permute-start(bf16[256,256]{1,0:T(8,128)(2,1)S(1)} %collective-permute-done.18.refs_14_), channel_id=1, source_target_pairs={{0,16},{8,24},{16,0},{24,8},{1,17},{9,25},{17,1},{25,9},{2,18},{10... | collective-permute-start | bytes 393224 | tf_op jit(solution)/shard_map/ppermute | solution.py:180
  36.0 2.3 %collective-permute-done.19.refs_15_ = bf16[256,256]{1,0:T(8,128)(2,1)S(1)} collective-permute-done((bf16[256,256]{1,0:T(8,128)(2,1)S(1)}, bf16[256,256]{1,0:T(8,128)(2,1)S(1)}, u32[]{:S(2)}, u32[]{:S(2)}) %collective-permute-start.19) | collective-permute-done | bytes 131104 | tf_op jit(solution)/shard_map/ppermute | solution.py:180
  38.4 1.9 %collective-permute-start.4 = (bf16[256,256]{1,0:T(8,128)(2,1)}, bf16[256,256]{1,0:T(8,128)(2,1)S(1)}, u32[]{:S(2)}, u32[]{:S(2)}) collective-permute-start(bf16[256,256]{1,0:T(8,128)(2,1)} %copy-done.13), channel_id=1, source_target_pairs={{0,2},{1,3},{2,0},{3,1},{4,6},{5,7},{6,4},{7,5},{8,10},{9,11},{10,... | collective-permute-start | bytes 393224 | tf_op jit(solution)/shard_map/ppermute | solution.py:188
  42.3 2.8 %shard_map.111 = (f32[512,128]{1,0:T(8,128)S(1)}, bf16[512,256]{1,0:T(8,128)(2,1)S(1)}) custom-call(bf16[128,2048]{1,0:T(8,128)(2,1)S(1)} %copy-done, bf16[128,2048]{1,0:T(8,128)(2,1)S(1)} %collective-permute-done.refs_1_, bf16[128,2048]{1,0:T(8,128)(2,1)S(1)} %collective-permute-done.1.refs_2_, bf16[128,2048]{1,0:T(8,128)(2,1)S(1)} %collective-permute-done.2.refs_3_, ...), custom_call_target="tpu_custom_call" | custom-call | flops 805306368 | bytes 5767168 | tf_op jit(solution)/shard_map/pallas_call | solution.py:28
  45.8 1.8 %collective-permute-start.5 = (bf16[256,256]{1,0:T(8,128)(2,1)S(1)}, bf16[256,256]{1,0:T(8,128)(2,1)S(1)}, u32[]{:S(2)}, u32[]{:S(2)}) collective-permute-start(bf16[256,256]{1,0:T(8,128)(2,1)S(1)} %collective-permute-done.4.refs_6_.refs_3_), channel_id=1, source_target_pairs={{0,16},{8,24},{16,0},{24,8},{1,17},{9,25},{17,1},{25,9},{2,18},{10... | collective-permute-start | bytes 393224 | tf_op jit(solution)/shard_map/ppermute | solution.py:180
  47.8 1.8 %collective-permute-start.9 = (bf16[256,256]{1,0:T(8,128)(2,1)S(1)}, bf16[256,256]{1,0:T(8,128)(2,1)S(1)}, u32[]{:S(2)}, u32[]{:S(2)}) collective-permute-start(bf16[256,256]{1,0:T(8,128)(2,1)S(1)} %collective-permute-done.8.refs_10_.refs_7_), channel_id=1, source_target_pairs={{0,16},{8,24},{16,0},{24,8},{1,17},{9,25},{17,1},{25,9},{2,18},{10... | collective-permute-start | bytes 393224 | tf_op jit(solution)/shard_map/ppermute | solution.py:180
  49.6 3.6 %collective-permute-start.36 = (bf16[2,2,3,32,128]{4,3,2,1,0:T(8,128)(2,1)S(1)}, bf16[2,2,3,32,128]{4,3,2,1,0:T(8,128)(2,1)S(1)}, u32[]{:S(2)}, u32[]{:S(2)}) collective-permute-start(bf16[2,2,3,32,128]{4,3,2,1,0:T(8,128)(2,1)S(1)} %get-tuple-element.51), channel_id=1, source_target_pairs={{0,6},{1,7},{2,4},{3,5},{4,2},{5,3},{6,0},{7,1},{8,14},{9,15},{10,... | collective-permute-start | bytes 294920 | tf_op jit(solution)/shard_map/ppermute | solution.py:177
  53.2 1.8 %collective-permute-start.35 = (bf16[2,2,3,32,128]{4,3,2,1,0:T(8,128)(2,1)S(1)}, bf16[2,2,3,32,128]{4,3,2,1,0:T(8,128)(2,1)S(1)}, u32[]{:S(2)}, u32[]{:S(2)}) collective-permute-start(bf16[2,2,3,32,128]{4,3,2,1,0:T(8,128)(2,1)S(1)} %get-tuple-element.51), channel_id=1, source_target_pairs={{0,4},{1,5},{2,6},{3,7},{4,0},{5,1},{6,2},{7,3},{8,12},{9,13},{10,... | collective-permute-start | bytes 294920 | tf_op jit(solution)/shard_map/ppermute | solution.py:177
  55.0 1.8 %collective-permute-start.34 = (bf16[2,2,3,32,128]{4,3,2,1,0:T(8,128)(2,1)S(1)}, bf16[2,2,3,32,128]{4,3,2,1,0:T(8,128)(2,1)S(1)}, u32[]{:S(2)}, u32[]{:S(2)}) collective-permute-start(bf16[2,2,3,32,128]{4,3,2,1,0:T(8,128)(2,1)S(1)} %get-tuple-element.51), channel_id=1, source_target_pairs={{0,2},{1,3},{2,0},{3,1},{4,6},{5,7},{6,4},{7,5},{8,10},{9,11},{10,... | collective-permute-start | bytes 294920 | tf_op jit(solution)/shard_map/ppermute | solution.py:177
  58.5 3.7 %collective-permute-start.26 = (bf16[3,64,128]{2,1,0:T(8,128)(2,1)S(1)}, bf16[3,64,128]{2,1,0:T(8,128)(2,1)S(1)}, u32[]{:S(2)}, u32[]{:S(2)}) collective-permute-start(bf16[3,64,128]{2,1,0:T(8,128)(2,1)S(1)} %get-tuple-element.28), channel_id=1, source_target_pairs={{0,6},{1,7},{2,4},{3,5},{4,2},{5,3},{6,0},{7,1},{8,14},{9,15},{10,... | collective-permute-start | bytes 147464 | tf_op jit(solution)/shard_map/ppermute | solution.py:177
  63.0 1.6 %collective-permute-start.37 = (bf16[4,2,2,3,32,128]{5,4,3,2,1,0:T(8,128)(2,1)S(1)}, bf16[4,2,2,3,32,128]{5,4,3,2,1,0:T(8,128)(2,1)S(1)}, u32[]{:S(2)}, u32[]{:S(2)}) collective-permute-start(bf16[4,2,2,3,32,128]{5,4,3,2,1,0:T(8,128)(2,1)S(1)} %get-tuple-element.33), channel_id=1, source_target_pairs={{0,8},{8,0},{16,24},{24,16},{1,9},{9,1},{17,25},{25,17},{2,10},{10... | collective-permute-start | bytes 1179656 | tf_op jit(solution)/shard_map/ppermute | solution.py:180
  64.9 2.3 %collective-permute-done.25 = bf16[3,64,128]{2,1,0:T(8,128)(2,1)S(1)} collective-permute-done((bf16[3,64,128]{2,1,0:T(8,128)(2,1)S(1)}, bf16[3,64,128]{2,1,0:T(8,128)(2,1)S(1)}, u32[]{:S(2)}, u32[]{:S(2)}) %collective-permute-start.25) | collective-permute-done | bytes 49184 | tf_op jit(solution)/shard_map/ppermute | solution.py:177
  67.2 1.5 %collective-permute-start.27 = (bf16[3,64,128]{2,1,0:T(8,128)(2,1)S(1)}, bf16[3,64,128]{2,1,0:T(8,128)(2,1)S(1)}, u32[]{:S(2)}, u32[]{:S(2)}) collective-permute-start(bf16[3,64,128]{2,1,0:T(8,128)(2,1)S(1)} %add_convert_fusion.3), channel_id=1, source_target_pairs={{0,16},{8,24},{16,0},{24,8},{1,17},{9,25},{17,1},{25,9},{2,18},{10... | collective-permute-start | bytes 147464 | tf_op jit(solution)/shard_map/ppermute | solution.py:180
  68.7 1.6 %shard_map.113 = (f32[128,2048]{1,0:T(8,128)S(1)}, f32[128,2048]{1,0:T(8,128)S(1)}, bf16[128,2048]{1,0:T(8,128)(2,1)S(1)}, bf16[128,2048]{1,0:T(8,128)(2,1)S(1)}) custom-call(bf16[512,256]{1,0:T(8,128)(2,1)S(1)} %get-tuple-element.20.refs_0_, bf16[256,256]{1,0:T(8,128)(2,1)S(1)} %pad_maximum_fusion.4.refs_4_.refs_1_, ...), custom_call_target="tpu_custom_call" | custom-call | flops 536870912 | bytes 4456448 | tf_op jit(solution)/shard_map/pallas_call | solution.py:28
  71.4 1.8 %collective-permute-start.30 = (bf16[3,64,128]{2,1,0:T(8,128)(2,1)S(1)}, bf16[3,64,128]{2,1,0:T(8,128)(2,1)S(1)}, u32[]{:S(2)}, u32[]{:S(2)}) collective-permute-start(bf16[3,64,128]{2,1,0:T(8,128)(2,1)S(1)} %add_convert_fusion.2), channel_id=1, source_target_pairs={{0,6},{1,7},{2,4},{3,5},{4,2},{5,3},{6,0},{7,1},{8,14},{9,15},{10,... | collective-permute-start | bytes 147464 | tf_op jit(solution)/shard_map/ppermute | solution.py:177
  73.5 2.3 %collective-permute-start.28 = (bf16[3,64,128]{2,1,0:T(8,128)(2,1)S(1)}, bf16[3,64,128]{2,1,0:T(8,128)(2,1)S(1)}, u32[]{:S(2)}, u32[]{:S(2)}) collective-permute-start(bf16[3,64,128]{2,1,0:T(8,128)(2,1)S(1)} %add_convert_fusion.2), channel_id=1, source_target_pairs={{0,2},{1,3},{2,0},{3,1},{4,6},{5,7},{6,4},{7,5},{8,10},{9,11},{10,... | collective-permute-start | bytes 147464 | tf_op jit(solution)/shard_map/ppermute | solution.py:177
  76.0 1.7 %collective-permute-done.30 = bf16[3,64,128]{2,1,0:T(8,128)(2,1)S(1)} collective-permute-done((bf16[3,64,128]{2,1,0:T(8,128)(2,1)S(1)}, bf16[3,64,128]{2,1,0:T(8,128)(2,1)S(1)}, u32[]{:S(2)}, u32[]{:S(2)}) %collective-permute-start.30) | collective-permute-done | bytes 49184 | tf_op jit(solution)/shard_map/ppermute | solution.py:177
  78.7 1.5 %collective-permute-start.31 = (bf16[4,3,64,128]{3,2,1,0:T(8,128)(2,1)S(1)}, bf16[4,3,64,128]{3,2,1,0:T(8,128)(2,1)S(1)}, u32[]{:S(2)}, u32[]{:S(2)}) collective-permute-start(bf16[4,3,64,128]{3,2,1,0:T(8,128)(2,1)S(1)} %get-tuple-element.46.refs_0_), channel_id=1, source_target_pairs={{0,8},{8,0},{16,24},{24,16},{1,9},{9,1},{17,25},{25,17},{2,10},{10... | collective-permute-start | bytes 589832 | tf_op jit(solution)/shard_map/ppermute | solution.py:180
  81.0 5.6 %collective-permute-done.31.refs_1_ = bf16[4,3,64,128]{3,2,1,0:T(8,128)(2,1)S(1)} collective-permute-done((bf16[4,3,64,128]{3,2,1,0:T(8,128)(2,1)S(1)}, bf16[4,3,64,128]{3,2,1,0:T(8,128)(2,1)S(1)}, u32[]{:S(2)}, u32[]{:S(2)}) %collective-permute-start.31) | collective-permute-done | bytes 196640 | tf_op jit(solution)/shard_map/ppermute | solution.py:180
  86.8 1.7 %collective-permute-done.32.refs_2_ = bf16[2,4,3,64,128]{4,3,2,1,0:T(8,128)(2,1)S(1)} collective-permute-done((bf16[2,4,3,64,128]{4,3,2,1,0:T(8,128)(2,1)S(1)}, bf16[2,4,3,64,128]{4,3,2,1,0:T(8,128)(2,1)S(1)}, u32[]{:S(2)}, u32[]{:S(2)}) %collective-permute-start.32) | collective-permute-done | bytes 393248 | tf_op jit(solution)/shard_map/ppermute | solution.py:177
  88.5 3.2 %shard_map.114 = (f32[3,32,512]{2,1,0:T(8,128)}, f32[3,32,512]{2,1,0:T(8,128)}, f32[3,256,512]{2,1,0:T(8,128)}) custom-call(bf16[4,3,64,128]{3,2,1,0:T(8,128)(2,1)S(1)} %get-tuple-element.46.refs_0_, bf16[4,3,64,128]{3,2,1,0:T(8,128)(2,1)S(1)} %collective-permute-done.31.refs_1_, bf16[2,4,3,64,128]{4,3,2,1,0:T(8,128)(2,1)S(1)} %collective-permute-done.32.refs_2_, ...), custom_call_target="tpu_custom_call" | custom-call | flops 402653184 | bytes 4980736 | tf_op jit(solution)/shard_map/pallas_call | solution.py:28
  91.7 4.6 %collective-permute-done.23 = bf16[128,2048]{1,0:T(8,128)(2,1)S(1)} collective-permute-done((bf16[128,2048]{1,0:T(8,128)(2,1)S(1)}, bf16[128,2048]{1,0:T(8,128)(2,1)S(1)}, u32[]{:S(2)}, u32[]{:S(2)}) %collective-permute-start.23) | collective-permute-done | bytes 524320 | tf_op jit(solution)/shard_map/ppermute | solution.py:180
  (99 shorter events, 17.3 us)
Async XLA Ops:
  0.7 25.3 %collective-permute-start.1 = (bf16[128,2048]{1,0:T(8,128)(2,1)}, bf16[128,2048]{1,0:T(8,128)(2,1)S(1)}, u32[]{:S(2)}, u32[]{:S(2)}) collective-permute-start(bf16[128,2048]{1,0:T(8,128)(2,1)} %refs_0_.3), channel_id=1, source_target_pairs={{0,8},{8,0},{16,24},{24,16},{1,9},{9,1},{17,25},{25,17},{2,10},{10... | collective-permute-start | bytes 1572872 | tf_op jit(solution)/shard_map/ppermute | solution.py:180
  3.7 23.5 %collective-permute-start.11 = (bf16[128,2048]{1,0:T(8,128)(2,1)}, bf16[128,2048]{1,0:T(8,128)(2,1)}, u32[]{:S(2)}, u32[]{:S(2)}) collective-permute-start(bf16[128,2048]{1,0:T(8,128)(2,1)} %refs_4_.1), channel_id=1, source_target_pairs={{0,8},{8,0},{16,24},{24,16},{1,9},{9,1},{17,25},{25,17},{2,10},{10... | collective-permute-start | bytes 1572872 | tf_op jit(solution)/shard_map/ppermute | solution.py:180
  7.0 10.5 %collective-permute-start.6 = (bf16[256,256]{1,0:T(8,128)(2,1)S(1)}, bf16[256,256]{1,0:T(8,128)(2,1)S(1)}, u32[]{:S(2)}, u32[]{:S(2)}) collective-permute-start(bf16[256,256]{1,0:T(8,128)(2,1)S(1)} %pad_maximum_fusion.6), channel_id=1, source_target_pairs={{0,4},{1,5},{2,6},{3,7},{4,0},{5,1},{6,2},{7,3},{8,12},{9,13},{10,... | collective-permute-start | bytes 393224 | tf_op jit(solution)/shard_map/ppermute | solution.py:188
  10.9 6.6 %collective-permute-start.14 = (bf16[256,256]{1,0:T(8,128)(2,1)S(1)}, bf16[256,256]{1,0:T(8,128)(2,1)S(1)}, u32[]{:S(2)}, u32[]{:S(2)}) collective-permute-start(bf16[256,256]{1,0:T(8,128)(2,1)S(1)} %pad_maximum_fusion.9), channel_id=1, source_target_pairs={{0,2},{1,3},{2,0},{3,1},{4,6},{5,7},{6,4},{7,5},{8,10},{9,11},{10,... | collective-permute-start | bytes 393224 | tf_op jit(solution)/shard_map/ppermute | solution.py:188
  12.5 9.1 %collective-permute-start.16 = (bf16[256,256]{1,0:T(8,128)(2,1)S(1)}, bf16[256,256]{1,0:T(8,128)(2,1)}, u32[]{:S(2)}, u32[]{:S(2)}) collective-permute-start(bf16[256,256]{1,0:T(8,128)(2,1)S(1)} %pad_maximum_fusion.9), channel_id=1, source_target_pairs={{0,4},{1,5},{2,6},{3,7},{4,0},{5,1},{6,2},{7,3},{8,12},{9,13},{10,... | collective-permute-start | bytes 393224 | tf_op jit(solution)/shard_map/ppermute | solution.py:188
  17.5 6.6 %collective-permute-start.13 = (bf16[256,256]{1,0:T(8,128)(2,1)S(1)}, bf16[256,256]{1,0:T(8,128)(2,1)S(1)}, u32[]{:S(2)}, u32[]{:S(2)}) collective-permute-start(bf16[256,256]{1,0:T(8,128)(2,1)S(1)} %pad_maximum_fusion.8), channel_id=1, source_target_pairs={{0,1},{1,0},{2,3},{3,2},{4,5},{5,4},{6,7},{7,6},{8,9},{9,8},{10,11... | collective-permute-start | bytes 393224 | tf_op jit(solution)/shard_map/ppermute | solution.py:177
  17.5 7.3 %collective-permute-start.15 = (bf16[256,256]{1,0:T(8,128)(2,1)S(1)}, bf16[256,256]{1,0:T(8,128)(2,1)S(1)}, u32[]{:S(2)}, u32[]{:S(2)}) collective-permute-start(bf16[256,256]{1,0:T(8,128)(2,1)S(1)} %collective-permute-done.14.refs_10_), channel_id=1, source_target_pairs={{0,16},{8,24},{16,0},{24,8},{1,17},{9,25},{17,1},{25,9},{2,18},{10... | collective-permute-start | bytes 393224 | tf_op jit(solution)/shard_map/ppermute | solution.py:180
  21.6 6.6 %collective-permute-start.17 = (bf16[256,256]{1,0:T(8,128)(2,1)}, bf16[256,256]{1,0:T(8,128)(2,1)}, u32[]{:S(2)}, u32[]{:S(2)}) collective-permute-start(bf16[256,256]{1,0:T(8,128)(2,1)} %collective-permute-done.16.refs_12_), channel_id=1, source_target_pairs={{0,16},{8,24},{16,0},{24,8},{1,17},{9,25},{17,1},{25,9},{2,18},{10... | collective-permute-start | bytes 393224 | tf_op jit(solution)/shard_map/ppermute | solution.py:180
  24.8 15.5 %collective-permute-start = (bf16[128,2048]{1,0:T(8,128)(2,1)S(1)}, bf16[128,2048]{1,0:T(8,128)(2,1)S(1)}, u32[]{:S(2)}, u32[]{:S(2)}) collective-permute-start(bf16[128,2048]{1,0:T(8,128)(2,1)S(1)} %copy-done), channel_id=1, source_target_pairs={{0,1},{1,0},{2,3},{3,2},{4,5},{5,4},{6,7},{7,6},{8,9},{9,8},{10,11... | collective-permute-start | bytes 1572872 | tf_op jit(solution)/shard_map/ppermute | solution.py:177
  25.5 14.8 %collective-permute-start.10 = (bf16[128,2048]{1,0:T(8,128)(2,1)S(1)}, bf16[128,2048]{1,0:T(8,128)(2,1)}, u32[]{:S(2)}, u32[]{:S(2)}) collective-permute-start(bf16[128,2048]{1,0:T(8,128)(2,1)S(1)} %copy-done.4), channel_id=1, source_target_pairs={{0,1},{1,0},{2,3},{3,2},{4,5},{5,4},{6,7},{7,6},{8,9},{9,8},{10,11... | collective-permute-start | bytes 1572872 | tf_op jit(solution)/shard_map/ppermute | solution.py:177
  26.0 14.5 %collective-permute-start.2 = (bf16[128,2048]{1,0:T(8,128)(2,1)S(1)}, bf16[128,2048]{1,0:T(8,128)(2,1)S(1)}, u32[]{:S(2)}, u32[]{:S(2)}) collective-permute-start(bf16[128,2048]{1,0:T(8,128)(2,1)S(1)} %collective-permute-done.1.refs_2_), channel_id=1, source_target_pairs={{0,1},{1,0},{2,3},{3,2},{4,5},{5,4},{6,7},{7,6},{8,9},{9,8},{10,11... | collective-permute-start | bytes 1572872 | tf_op jit(solution)/shard_map/ppermute | solution.py:177
  27.2 13.3 %collective-permute-start.12 = (bf16[128,2048]{1,0:T(8,128)(2,1)}, bf16[128,2048]{1,0:T(8,128)(2,1)}, u32[]{:S(2)}, u32[]{:S(2)}) collective-permute-start(bf16[128,2048]{1,0:T(8,128)(2,1)} %collective-permute-done.11.refs_6_), channel_id=1, source_target_pairs={{0,1},{1,0},{2,3},{3,2},{4,5},{5,4},{6,7},{7,6},{8,9},{9,8},{10,11... | collective-permute-start | bytes 1572872 | tf_op jit(solution)/shard_map/ppermute | solution.py:177
  28.2 5.2 %collective-permute-start.18 = (bf16[256,256]{1,0:T(8,128)(2,1)}, bf16[256,256]{1,0:T(8,128)(2,1)S(1)}, u32[]{:S(2)}, u32[]{:S(2)}) collective-permute-start(bf16[256,256]{1,0:T(8,128)(2,1)} %collective-permute-done.16.refs_12_), channel_id=1, source_target_pairs={{0,2},{1,3},{2,0},{3,1},{4,6},{5,7},{6,4},{7,5},{8,10},{9,11},{10,... | collective-permute-start | bytes 393224 | tf_op jit(solution)/shard_map/ppermute | solution.py:177
  38.4 7.4 %collective-permute-start.4 = (bf16[256,256]{1,0:T(8,128)(2,1)}, bf16[256,256]{1,0:T(8,128)(2,1)S(1)}, u32[]{:S(2)}, u32[]{:S(2)}) collective-permute-start(bf16[256,256]{1,0:T(8,128)(2,1)} %copy-done.13), channel_id=1, source_target_pairs={{0,2},{1,3},{2,0},{3,1},{4,6},{5,7},{6,4},{7,5},{8,10},{9,11},{10,... | collective-permute-start | bytes 393224 | tf_op jit(solution)/shard_map/ppermute | solution.py:188
  40.2 7.3 %collective-permute-start.33 = (bf16[2,3,32,128]{3,2,1,0:T(8,128)(2,1)S(1)}, bf16[2,3,32,128]{3,2,1,0:T(8,128)(2,1)S(1)}, u32[]{:S(2)}, u32[]{:S(2)}) collective-permute-start(bf16[2,3,32,128]{3,2,1,0:T(8,128)(2,1)S(1)} %get-tuple-element.44), channel_id=1, source_target_pairs={{0,1},{1,0},{2,3},{3,2},{4,5},{5,4},{6,7},{7,6},{8,9},{9,8},{10,11... | collective-permute-start | bytes 147464 | tf_op jit(solution)/shard_map/ppermute | solution.py:177
  40.3 7.6 %collective-permute-start.8 = (bf16[256,256]{1,0:T(8,128)(2,1)S(1)}, bf16[256,256]{1,0:T(8,128)(2,1)S(1)}, u32[]{:S(2)}, u32[]{:S(2)}) collective-permute-start(bf16[256,256]{1,0:T(8,128)(2,1)S(1)} %collective-permute-done.6.refs_8_.refs_5_), channel_id=1, source_target_pairs={{0,2},{1,3},{2,0},{3,1},{4,6},{5,7},{6,4},{7,5},{8,10},{9,11},{10,... | collective-permute-start | bytes 393224 | tf_op jit(solution)/shard_map/ppermute | solution.py:177
  45.1 12.0 %collective-permute-start.20 = (bf16[512,256]{1,0:T(8,128)(2,1)S(1)}, bf16[512,256]{1,0:T(8,128)(2,1)S(1)}, u32[]{:S(2)}, u32[]{:S(2)}) collective-permute-start(bf16[512,256]{1,0:T(8,128)(2,1)S(1)} %get-tuple-element.19.refs_13_), channel_id=1, source_target_pairs={{0,1},{1,0},{2,3},{3,2},{4,5},{5,4},{6,7},{7,6},{8,9},{9,8},{10,11... | collective-permute-start | bytes 786440 | tf_op jit(solution)/shard_map/ppermute | solution.py:177
  45.8 7.4 %collective-permute-start.5 = (bf16[256,256]{1,0:T(8,128)(2,1)S(1)}, bf16[256,256]{1,0:T(8,128)(2,1)S(1)}, u32[]{:S(2)}, u32[]{:S(2)}) collective-permute-start(bf16[256,256]{1,0:T(8,128)(2,1)S(1)} %collective-permute-done.4.refs_6_.refs_3_), channel_id=1, source_target_pairs={{0,16},{8,24},{16,0},{24,8},{1,17},{9,25},{17,1},{25,9},{2,18},{10... | collective-permute-start | bytes 393224 | tf_op jit(solution)/shard_map/ppermute | solution.py:180
  47.6 7.4 %collective-permute-start.7 = (bf16[256,256]{1,0:T(8,128)(2,1)S(1)}, bf16[256,256]{1,0:T(8,128)(2,1)S(1)}, u32[]{:S(2)}, u32[]{:S(2)}) collective-permute-start(bf16[256,256]{1,0:T(8,128)(2,1)S(1)} %collective-permute-done.6.refs_8_.refs_5_), channel_id=1, source_target_pairs={{0,16},{8,24},{16,0},{24,8},{1,17},{9,25},{17,1},{25,9},{2,18},{10... | collective-permute-start | bytes 393224 | tf_op jit(solution)/shard_map/ppermute | solution.py:180
  47.8 9.3 %collective-permute-start.9 = (bf16[256,256]{1,0:T(8,128)(2,1)S(1)}, bf16[256,256]{1,0:T(8,128)(2,1)S(1)}, u32[]{:S(2)}, u32[]{:S(2)}) collective-permute-start(bf16[256,256]{1,0:T(8,128)(2,1)S(1)} %collective-permute-done.8.refs_10_.refs_7_), channel_id=1, source_target_pairs={{0,16},{8,24},{16,0},{24,8},{1,17},{9,25},{17,1},{25,9},{2,18},{10... | collective-permute-start | bytes 393224 | tf_op jit(solution)/shard_map/ppermute | solution.py:180
  49.6 12.5 %collective-permute-start.36 = (bf16[2,2,3,32,128]{4,3,2,1,0:T(8,128)(2,1)S(1)}, bf16[2,2,3,32,128]{4,3,2,1,0:T(8,128)(2,1)S(1)}, u32[]{:S(2)}, u32[]{:S(2)}) collective-permute-start(bf16[2,2,3,32,128]{4,3,2,1,0:T(8,128)(2,1)S(1)} %get-tuple-element.51), channel_id=1, source_target_pairs={{0,6},{1,7},{2,4},{3,5},{4,2},{5,3},{6,0},{7,1},{8,14},{9,15},{10,... | collective-permute-start | bytes 294920 | tf_op jit(solution)/shard_map/ppermute | solution.py:177
  53.2 9.7 %collective-permute-start.35 = (bf16[2,2,3,32,128]{4,3,2,1,0:T(8,128)(2,1)S(1)}, bf16[2,2,3,32,128]{4,3,2,1,0:T(8,128)(2,1)S(1)}, u32[]{:S(2)}, u32[]{:S(2)}) collective-permute-start(bf16[2,2,3,32,128]{4,3,2,1,0:T(8,128)(2,1)S(1)} %get-tuple-element.51), channel_id=1, source_target_pairs={{0,4},{1,5},{2,6},{3,7},{4,0},{5,1},{6,2},{7,3},{8,12},{9,13},{10,... | collective-permute-start | bytes 294920 | tf_op jit(solution)/shard_map/ppermute | solution.py:177
  55.0 7.9 %collective-permute-start.34 = (bf16[2,2,3,32,128]{4,3,2,1,0:T(8,128)(2,1)S(1)}, bf16[2,2,3,32,128]{4,3,2,1,0:T(8,128)(2,1)S(1)}, u32[]{:S(2)}, u32[]{:S(2)}) collective-permute-start(bf16[2,2,3,32,128]{4,3,2,1,0:T(8,128)(2,1)S(1)} %get-tuple-element.51), channel_id=1, source_target_pairs={{0,2},{1,3},{2,0},{3,1},{4,6},{5,7},{6,4},{7,5},{8,10},{9,11},{10,... | collective-permute-start | bytes 294920 | tf_op jit(solution)/shard_map/ppermute | solution.py:177
  58.5 6.4 %collective-permute-start.26 = (bf16[3,64,128]{2,1,0:T(8,128)(2,1)S(1)}, bf16[3,64,128]{2,1,0:T(8,128)(2,1)S(1)}, u32[]{:S(2)}, u32[]{:S(2)}) collective-permute-start(bf16[3,64,128]{2,1,0:T(8,128)(2,1)S(1)} %get-tuple-element.28), channel_id=1, source_target_pairs={{0,6},{1,7},{2,4},{3,5},{4,2},{5,3},{6,0},{7,1},{8,14},{9,15},{10,... | collective-permute-start | bytes 147464 | tf_op jit(solution)/shard_map/ppermute | solution.py:177
  63.0 12.8 %collective-permute-start.37 = (bf16[4,2,2,3,32,128]{5,4,3,2,1,0:T(8,128)(2,1)S(1)}, bf16[4,2,2,3,32,128]{5,4,3,2,1,0:T(8,128)(2,1)S(1)}, u32[]{:S(2)}, u32[]{:S(2)}) collective-permute-start(bf16[4,2,2,3,32,128]{5,4,3,2,1,0:T(8,128)(2,1)S(1)} %get-tuple-element.33), channel_id=1, source_target_pairs={{0,8},{8,0},{16,24},{24,16},{1,9},{9,1},{17,25},{25,17},{2,10},{10... | collective-permute-start | bytes 1179656 | tf_op jit(solution)/shard_map/ppermute | solution.py:180
  70.3 10.0 %collective-permute-start.22 = (bf16[128,2048]{1,0:T(8,128)(2,1)S(1)}, bf16[128,2048]{1,0:T(8,128)(2,1)S(1)}, u32[]{:S(2)}, u32[]{:S(2)}) collective-permute-start(bf16[128,2048]{1,0:T(8,128)(2,1)S(1)} %get-tuple-element.24), channel_id=1, source_target_pairs={{0,1},{1,0},{2,3},{3,2},{4,5},{5,4},{6,7},{7,6},{8,9},{9,8},{10,11... | collective-permute-start | bytes 1572872 | tf_op jit(solution)/shard_map/ppermute | solution.py:177
  71.4 6.3 %collective-permute-start.30 = (bf16[3,64,128]{2,1,0:T(8,128)(2,1)S(1)}, bf16[3,64,128]{2,1,0:T(8,128)(2,1)S(1)}, u32[]{:S(2)}, u32[]{:S(2)}) collective-permute-start(bf16[3,64,128]{2,1,0:T(8,128)(2,1)S(1)} %add_convert_fusion.2), channel_id=1, source_target_pairs={{0,6},{1,7},{2,4},{3,5},{4,2},{5,3},{6,0},{7,1},{8,14},{9,15},{10,... | collective-permute-start | bytes 147464 | tf_op jit(solution)/shard_map/ppermute | solution.py:177
  73.2 5.5 %collective-permute-start.29 = (bf16[3,64,128]{2,1,0:T(8,128)(2,1)S(1)}, bf16[3,64,128]{2,1,0:T(8,128)(2,1)S(1)}, u32[]{:S(2)}, u32[]{:S(2)}) collective-permute-start(bf16[3,64,128]{2,1,0:T(8,128)(2,1)S(1)} %add_convert_fusion.2), channel_id=1, source_target_pairs={{0,4},{1,5},{2,6},{3,7},{4,0},{5,1},{6,2},{7,3},{8,12},{9,13},{10,... | collective-permute-start | bytes 147464 | tf_op jit(solution)/shard_map/ppermute | solution.py:177
  75.9 10.9 %collective-permute-start.38 = (bf16[2,4,2,2,3,32,128]{6,5,4,3,2,1,0:T(8,128)(2,1)S(1)}, bf16[2,4,2,2,3,32,128]{6,5,4,3,2,1,0:T(8,128)(2,1)S(1)}, u32[]{:S(2)}, u32[]{:S(2)}) collective-permute-start(bf16[2,4,2,2,3,32,128]{6,5,4,3,2,1,0:T(8,128)(2,1)S(1)} %pad_maximum_fusion.refs_3_), channel_id=1, source_target_pairs={{0,1},{1,0},{2,3},{3,2},{4,5},{5,4},{6,7},{7,6},{8,9},{9,8},{10,11... | collective-permute-start | bytes 2359304 | tf_op jit(solution)/shard_map/ppermute | solution.py:177
  77.6 14.0 %collective-permute-start.21 = (bf16[128,2048]{1,0:T(8,128)(2,1)S(1)}, bf16[128,2048]{1,0:T(8,128)(2,1)S(1)}, u32[]{:S(2)}, u32[]{:S(2)}) collective-permute-start(bf16[128,2048]{1,0:T(8,128)(2,1)S(1)} %get-tuple-element.22), channel_id=1, source_target_pairs={{0,1},{1,0},{2,3},{3,2},{4,5},{5,4},{6,7},{7,6},{8,9},{9,8},{10,11... | collective-permute-start | bytes 1572872 | tf_op jit(solution)/shard_map/ppermute | solution.py:177
  78.7 7.9 %collective-permute-start.31 = (bf16[4,3,64,128]{3,2,1,0:T(8,128)(2,1)S(1)}, bf16[4,3,64,128]{3,2,1,0:T(8,128)(2,1)S(1)}, u32[]{:S(2)}, u32[]{:S(2)}) collective-permute-start(bf16[4,3,64,128]{3,2,1,0:T(8,128)(2,1)S(1)} %get-tuple-element.46.refs_0_), channel_id=1, source_target_pairs={{0,8},{8,0},{16,24},{24,16},{1,9},{9,1},{17,25},{25,17},{2,10},{10... | collective-permute-start | bytes 589832 | tf_op jit(solution)/shard_map/ppermute | solution.py:180
  80.4 15.9 %collective-permute-start.23 = (bf16[128,2048]{1,0:T(8,128)(2,1)S(1)}, bf16[128,2048]{1,0:T(8,128)(2,1)S(1)}, u32[]{:S(2)}, u32[]{:S(2)}) collective-permute-start(bf16[128,2048]{1,0:T(8,128)(2,1)S(1)} %add_convert_fusion.1), channel_id=1, source_target_pairs={{0,8},{8,0},{16,24},{24,16},{1,9},{9,1},{17,25},{25,17},{2,10},{10... | collective-permute-start | bytes 1572872 | tf_op jit(solution)/shard_map/ppermute | solution.py:180
  (21 other events, 200.9 us)

commit v2 on v1

v2 whole, which is shorter than its diff:
```python
import functools
import math

import jax
import jax.numpy as jnp
from jax import lax
from jax.experimental import pallas as pl
from jax.experimental.pallas import tpu as pltpu
from jax.sharding import PartitionSpec as P

BF = jnp.bfloat16
F32 = jnp.float32
ROWS = (((0,), (0,)), ((), ()))
COLS = (((1,), (1,)), ((), ()))


def dot(left, right, dims=(((1,), (0,)), ((), ()))):
    return lax.dot_general(left, right, dims, preferred_element_type=F32)


def call(body, outs, scratch, flops, *operands, space=pltpu.VMEM, mib=40):
    moved = sum(o.size * o.dtype.itemsize for o in operands)
    moved += sum(math.prod(s) * jnp.dtype(d).itemsize for s, d in outs)
    return pl.pallas_call(
        body,
        out_shape=[jax.ShapeDtypeStruct(s, d) for s, d in outs],
        in_specs=[pl.BlockSpec(memory_space=space)] * len(operands),
        out_specs=[pl.BlockSpec(memory_space=pltpu.VMEM)] * len(outs),
        scratch_shapes=scratch,
        compiler_params=pltpu.CompilerParams(vmem_limit_bytes=mib * 1024 * 1024),
        cost_estimate=pl.CostEstimate(
            flops=flops, bytes_accessed=moved, transcendentals=0
        ),
    )(*operands)


def places():
    group, member = lax.axis_index("group"), lax.axis_index("member")
    return group % 2, (group // 2) % 2, member // 2, member % 2, member


def sources(count):
    _, high, _, _, member = places()
    order = [member, member ^ 1]
    for k in range(1, count // 2):
        near = member ^ (2 * k) ^ high
        order += [near, near ^ 1]
    return order


def pack_kernel(parts, *refs):
    down_hbm, gate_hbm, up_hbm, basis_hbm, *moment_hbms, tok_hbm, cot_hbm = refs[:8]
    own_ref, sent_ref, core_ref, mom_ref, both_ref = refs[8:13]
    basis_ref, first_ref, second_ref, sems = refs[13:]
    toks = tok_hbm.shape[0]
    side, high, _, core, _ = places()
    depth, hidden = gate_hbm.shape
    unit, half = hidden // 4, basis_ref.shape[1] // 2
    own_rows = first_ref.shape[1]
    copies = []

    def start(source, target):
        copy = pltpu.make_async_copy(source, target, sems.at[len(copies)])
        copy.start()
        copies.append(copy)

    start(basis_hbm, basis_ref)
    start(moment_hbms[0], first_ref)
    start(moment_hbms[1], second_ref)
    targets = ((core ^ high, sent_ref), (core, own_ref), (1 - core, core_ref.at[:depth]))
    for which, ref in targets:
        column = pl.ds(pl.multiple_of((2 * side + which) * unit, unit), unit)
        for i, source in enumerate((down_hbm, gate_hbm, up_hbm)):
            lane = half + i * unit
            start(source.at[:, column], ref.at[:, lane : lane + unit])
    start(tok_hbm, both_ref.at[:toks])
    start(cot_hbm, both_ref.at[toks:])
    for copy in copies[:3]:
        copy.wait()
    for which, ref in targets:
        ranks = pl.ds(pl.multiple_of(which * half, half), half)
        ref[:, :half] = basis_ref[:, ranks].astype(BF)
    for which, ref in ((core, mom_ref), (1 - core, core_ref.at[depth:])):
        column = pl.ds(pl.multiple_of((2 * side + which) * unit, unit), unit)
        for f, source in enumerate((first_ref, second_ref)):
            rows = slice(f * own_rows, (f + 1) * own_rows)
            for i in range(parts):
                ref[rows, i * unit : (i + 1) * unit] = source[i, :, column].astype(BF)
    for copy in copies[3:]:
        copy.wait()


def joined(refs, rows):
    return jnp.concatenate([ref[rows, :] for ref in refs], axis=0)


def place_blocks(members, layout, refs, depth, full):
    for src, (which, row) in zip(sources(members), layout):
        at = pl.ds(pl.multiple_of(src * depth, depth), depth)
        full[at, :] = refs[which][row : row + depth, :]


def first_kernel(members, layout, depth, half, *refs):
    boths, blocks = refs[:4], refs[4:-4]
    toks = boths[0].shape[0] // 2
    proj_ref, dgu_ref, hidden_ref, full = refs[-4:]
    unit = hidden_ref.shape[1]
    place_blocks(members, layout, blocks, depth, full)
    tok, cot = joined(boths, slice(0, toks)), joined(boths, slice(toks, 2 * toks))
    from_cot = dot(cot, full[:, : half + unit])
    dhid = from_cot[:, half:]
    proj_ref[:, half:] = from_cot[:, :half].astype(BF)
    total = dot(tok, full[:, half + unit :])
    gate, up = total[:, :unit], total[:, unit:]
    sig = 1.0 / (1.0 + jnp.exp(-gate))
    silu = gate * sig
    hidden_ref[...] = (silu * up).astype(BF)
    dgu_ref[:, :unit] = (dhid * up * sig * (1.0 + gate * (1.0 - sig))).astype(BF)
    dgu_ref[:, unit:] = (dhid * silu).astype(BF)
    proj_ref[:, :half] = dot(tok, full[:, :half]).astype(BF)


def second_kernel(mine_ref, other_ref, dgu_ref, hidden_ref, *refs):
    *low_refs, low = refs
    unit = hidden_ref.shape[1]
    half = mine_ref.shape[1] // 2
    _, _, chip, core, _ = places()
    toks = mine_ref.shape[0] // 4
    dgu, hidden = dgu_ref[...], hidden_ref[...]
    other = jnp.concatenate(
        [other_ref[i * toks : (i + 1) * toks, :] for i in (1, 0, 3, 2)], axis=0
    )
    for away, proj in enumerate((mine_ref[...], other)):
        rows = pl.ds(away * half, half)
        tok_low = dot(proj[:, :half], dgu, ROWS)
        low[0, rows, :] = tok_low[:, :unit]
        low[1, rows, :] = tok_low[:, unit:]
        low[2, rows, :] = dot(proj[:, half:], hidden, ROWS)
    height = low_refs[0].shape[1]
    for k, ref in enumerate(low_refs):
        row = (chip ^ k) * height
        row = (row // half ^ core) * half + row % half
        rows = pl.ds(pl.multiple_of(row, height), height)
        for i in range(ref.shape[0]):
            ref[i] = low[i, rows, :].astype(ref.dtype)


def grad_kernel(dgu_ref, full_ref, keep_0, keep_1, send_0, send_1):
    toks = keep_0.shape[0]
    width = dgu_ref.shape[1]
    for i, ref in enumerate((keep_0, send_0, keep_1, send_1)):
        part = dot(dgu_ref[i * toks : (i + 1) * toks, :], full_ref[:, -width:], COLS)
        ref[...] = part.astype(ref.dtype)


def mirrored(value, size):
    out = 0
    while size > 1:
        out, value, size = out * 2 + value % 2, value // 2, size // 2
    return out


def last_kernel(chips, limit, *refs):
    lows, core_low, moms, core_moms = refs[:2], refs[2], refs[3:5], refs[5]
    basis_ref, first_ref, second_ref, new_first_ref, new_second_ref, upd_ref = refs[6:12]
    full, stepped = refs[12:]
    side, _, chip, core, member = places()
    height, unit = lows[0].shape[2:]
    squares = None
    for dc in range(2):
        for dx in range(2):
            column = ((side ^ dx) * 2 + (core ^ dc)) * unit
            columns = pl.ds(pl.multiple_of(column, unit), unit)
            for k in range(chips):
                low = (core_low[dx, k] if dc else lows[dx][k]).astype(F32)
                square = jnp.sum(low * low, axis=(0, 1), keepdims=True)
                squares = square if squares is None else squares + square
                rows = pl.ds(pl.multiple_of((chip ^ k) * height, height), height)
                full[:, rows, columns] = low
    total = jnp.sum(squares, axis=2, keepdims=True)
    factor = jnp.minimum(1.0, limit / jnp.sqrt(total + 1e-06))
    own_rows = first_ref.shape[1]
    mine = factor * full[:, pl.ds(pl.multiple_of(member * own_rows, own_rows), own_rows), :]
    new_first_ref[...] = 0.5 * first_ref[...] + 0.5 * mine
    new_second_ref[...] = 0.9 * second_ref[...] + 0.1 * mine * mine
    parts = first_ref.shape[0]
    for dc in range(2):
        for dx in range(2):
            column = ((side ^ dx) * 2 + (core ^ dc)) * unit
            columns = pl.ds(pl.multiple_of(column, unit), unit)
            for n, dr in ((n, dr) for n in range(chips) for dr in range(2)):
                row = ((chip ^ mirrored(n, chips)) * 2 + (core ^ dc ^ dr)) * own_rows
                rows = pl.ds(pl.multiple_of(row, own_rows), own_rows)
                for i in range(parts):
                    mom = []
                    for f in range(2):
                        where = pl.ds(f * own_rows, own_rows)
                        lanes = slice(i * unit, (i + 1) * unit)
                        ref = core_moms.at[dx] if dc else moms[dx]
                        mom.append(ref[n, dr, where, lanes].astype(F32))
                    grad = factor[0] * full[i, rows, columns]
                    first = 0.5 * mom[0] + 0.5 * grad
                    second = 0.9 * mom[1] + 0.1 * grad * grad
                    stepped[i, rows, columns] = first / (jnp.sqrt(second) + 1e-08)
    basis = basis_ref[...]
    high = basis.astype(BF)
    rest = (basis - high.astype(F32)).astype(BF)
    for i in range(upd_ref.shape[0]):
        step = stepped[i].astype(BF)
        upd_ref[i] = dot(high, step) + dot(rest, step)


def local(sizes, tokens, cotangent, w_gate, w_up, w_down, basis, first_moment, second_moment):
    groups, members = sizes
    chips = members // 2
    toks, width = tokens.shape
    depth, hidden_size = w_gate.shape
    rank = basis.shape[1]
    unit, half = hidden_size // 4, rank // 2
    own_rows = first_moment.shape[1]
    limit = math.sqrt(first_moment.shape[0] * rank * hidden_size)

    def by_member(value, bits):
        return lax.ppermute(value, "member", [(i, i ^ bits) for i in range(members)])

    def by_group(value, bits):
        return lax.ppermute(value, "group", [(i, i ^ bits) for i in range(groups)])

    def by_chip(value, bits):
        pairs = []
        for g in range(groups):
            for i in range(members):
                j = i ^ bits ^ ((g // 2) % 2)
                pairs.append((g * members + i, g * members + j))
        return lax.ppermute(value, ("group", "member"), pairs)

    parts = first_moment.shape[0]
    block = half + 3 * unit
    own, sent, to_core, mom_mine, both = call(
        functools.partial(pack_kernel, parts),
        [((depth, block), BF)] * 2
        + [((depth + 2 * own_rows, block), BF), ((2 * own_rows, parts * unit), BF), ((2 * toks, width), BF)],
        [
            pltpu.VMEM(basis.shape, F32),
            pltpu.VMEM(first_moment.shape, F32),
            pltpu.VMEM(second_moment.shape, F32),
            pltpu.SemaphoreType.DMA((14,)),
        ],
        0,
        w_down,
        w_gate,
        w_up,
        basis,
        first_moment,
        second_moment,
        tokens,
        cotangent,
        space=pltpu.HBM,
        mib=60,
    )
    direct = [k for k in range(1, chips) if k & (k - 1) == 0]
    passed = [k for k in range(1, chips) if k & (k - 1)]
    ordered = lax.optimization_barrier

    both_x = by_group(both, 1)
    near = {k: by_chip(sent, 2 * k) for k in reversed(direct)}
    from_core = by_member(to_core, 1)
    near, from_core, both = ordered((near, from_core, both))

    far = [by_group(jnp.concatenate([near[k] for k in direct]), 2)]
    for k in passed:
        near[k] = by_member(near[k & (k - 1)], 2 * (k & -k))
    moms = jnp.stack([mom_mine, from_core[depth:, : parts * unit]])[None]
    for bit in reversed(direct[1:]):
        moms = jnp.concatenate([moms, by_member(moms, 2 * bit)])
    both_x, both, far, near, moms = ordered((both_x, both, far, near, moms))

    far.append(by_group(jnp.concatenate([near[k] for k in passed]), 2))
    both_c = by_member(both, 1)
    both_xc = by_member(both_x, 1)
    moms = jnp.concatenate([moms, by_member(moms, 2)])
    far, both_c, both_xc, moms = ordered((far, both_c, both_xc, moms))

    layout = [(0, 0), (1, 0)]
    for k in range(1, chips):
        i = 0 if k in direct else 1
        layout += [(1 + k, 0), (1 + chips + i, (direct, passed)[i].index(k) * depth)]
    four = 4 * toks
    proj, dgu, hidden, full = call(
        functools.partial(first_kernel, members, tuple(layout), depth, half),
        [
            ((four, 2 * half), BF),
            ((four, 2 * unit), BF),
            ((four, unit), BF),
            ((width, block), BF),
        ],
        [],
        2 * four * width * (2 * half + 3 * unit),
        *(both, both_c, both_x, both_xc),
        *(own, from_core, *(near[k] for k in range(1, chips)), *far),
    )
    proj_core = by_member(proj, 1)
    moms_x = by_group(moms, 1)
    keep_0, keep_1, send_0, send_1 = call(
        grad_kernel,
        [((toks, width), F32)] * 2 + [((toks, width), BF)] * 2,
        [],
        2 * four * width * 2 * unit,
        dgu,
        full,
    )
    proj_core, send_1 = ordered((proj_core, send_1))
    near_part = by_member(send_1, 1)
    height = rank // chips
    piece = (parts, height, unit)
    lows = call(
        second_kernel,
        [(piece, BF if k else F32) for k in range(chips)],
        [pltpu.VMEM((parts, rank, unit), F32)],
        2 * four * 3 * rank * unit,
        proj,
        proj_core,
        dgu,
        hidden,
    )
    near_part = (keep_1 + near_part.astype(F32)).astype(BF)
    lows, near_part = ordered((lows, near_part))
    arrived = [by_member(lows[k], 2 * k) for k in range(1, chips)]
    arrived, moms_x = ordered((arrived, moms_x))
    core_moms = by_member(jnp.stack([moms, moms_x]), 1)
    grad_side = by_group(near_part, 1)
    share = lows[0]
    for low in arrived:
        share = share + low.astype(F32)
    bit = 2
    while bit < groups:
        sent = share.astype(BF)
        came = by_group(sent, bit)
        share = sent.astype(F32) + came.astype(F32)
        bit *= 2
    share = share.astype(BF)

    low_mine = [share] + [by_member(share, 2 * k) for k in range(1, chips)]
    low_mine, grad_side = ordered((low_mine, grad_side))
    low_mine = jnp.stack(low_mine)
    low_side = by_group(low_mine, 1)
    mine_part = keep_0 + by_member(send_0, 1).astype(F32)
    input_grad = (mine_part + grad_side.astype(F32)).astype(BF)
    low_core = by_member(jnp.stack([low_mine, low_side]), 1)
    new_first, new_second, updates = call(
        functools.partial(last_kernel, chips, limit),
        [(first_moment.shape, F32), (second_moment.shape, F32), ((3, depth, hidden_size), F32)],
        [pltpu.VMEM((3, rank, hidden_size), F32)] * 2,
        4 * 3 * depth * rank * hidden_size,
        low_mine,
        low_side,
        low_core,
        moms,
        moms_x,
        core_moms,
        basis,
        first_moment,
        second_moment,
    )
    return (input_grad, new_first, new_second, updates)


def solution(mesh):
    sizes = (mesh.shape["group"], mesh.shape["member"])
    tokens = P(("group", "member"), None)
    rows = P("member", None)
    low = P(None, "member", None)
    return jax.shard_map(
        functools.partial(local, sizes),
        mesh=mesh,
        in_specs=(tokens, tokens, rows, rows, rows, rows, low, low),
        out_specs=(tokens, low, low, low),
        check_vma=False,
    )
```

time: 97.6 us -> 86.3 us (0.88)
  starting transfers between devices: 44 us -> 29.1 us
  waiting for transfers between devices: 34 us -> 43.8 us
  local copies, waits for them, and re-layouts: 7.08 us -> 0.04 us
  Pallas kernels: 8.9 us -> 10.1 us
    ppermute x12 -> x7, starting transfers between devices: 18.5 us -> 9.38 us  [by_group(): return lax.ppermute(value, 'group', [(i, i ^ bits) for i in range(groups)])]
    ppermute x4 -> x2, waiting for transfers between devices: 6.52 us -> 11.6 us  [by_chip(): return lax.ppermute(value, ('group', 'member'), pairs)]
    dynamic_slice x3 -> x0, local copies, waits for them, and re-layouts: 3.92 us -> none  [cut(): return lax.dynamic_slice_in_dim(value, column, size, axis=value.ndim - 1)]
    ppermute x12 -> x7, waiting for transfers between devices: 16.1 us -> 19.4 us  [by_group(): return lax.ppermute(value, 'group', [(i, i ^ bits) for i in range(groups)])]
    unnamed x28 -> x10, local copies, waits for them, and re-layouts: 3.15 us -> 0.03 us
    ppermute x23 -> x17, starting transfers between devices: 18.5 us -> 15.6 us  [by_member(): lax.ppermute(value, 'member', [(i, i ^ bits) for i in range(members)])]
    ppermute x4 -> x2, starting transfers between devices: 6.94 us -> 4.17 us  [by_chip(): return lax.ppermute(value, ('group', 'member'), pairs)]
    ppermute x23 -> x17, waiting for transfers between devices: 11.4 us -> 12.8 us  [by_member(): lax.ppermute(value, 'member', [(i, i ^ bits) for i in range(members)])]
  transfers between devices with their start and end apart: 39 -> 26, of which waited for: 15 -> 14; matrix products, arithmetic and copies ran while one was open for 5% -> 3% of each run, Pallas kernels for 9% -> 2%
where the time goes in v2:
time: 86.3 us; the launch traced here: 86.1 us
  waiting for transfers between devices  43.8 us (51%)
  starting transfers between devices  29.1 us (34%)
  Pallas kernels  10.1 us (12%)
  other arithmetic  2.22 us (3%)
    ppermute x7, waiting for transfers between devices, by_group(): return lax.ppermute(value, 'group', [(i, i ^ bits) for i in range(groups)])  19.4 us
    ppermute x17, starting transfers between devices, by_member(): lax.ppermute(value, 'member', [(i, i ^ bits) for i in range(members)])  15.6 us
    ppermute x17, waiting for transfers between devices, by_member(): lax.ppermute(value, 'member', [(i, i ^ bits) for i in range(members)])  12.8 us
    ppermute x2, waiting for transfers between devices, by_chip(): return lax.ppermute(value, ('group', 'member'), pairs)  11.6 us
    pallas_call x5, Pallas kernels, call(): pl.pallas_call(body, out_shape=[jax.ShapeDtypeStruct(s, d) for s, d in ou...  10.1 us
    ppermute x7, starting transfers between devices, by_group(): return lax.ppermute(value, 'group', [(i, i ^ bits) for i in range(groups)])  9.38 us
    ppermute x2, starting transfers between devices, by_chip(): return lax.ppermute(value, ('group', 'member'), pairs)  4.17 us
  transfers between devices with their start and end apart: 26, of which 14 were waited for; matrix products, arithmetic and copies ran while one was open for 3% of the time, Pallas kernels for 2%

profile of v2, /device:TPU:0, one launch (start us, length us, event | category | flops | bytes accessed | tf_op | source)
XLA Modules:
  0.0 86.1 jit_solution(5653141710498893273)
XLA Ops:
  0.6 3.1 %shard_map.111 = (bf16[256,512]{1,0:T(8,128)(2,1)}, bf16[256,512]{1,0:T(8,128)(2,1)}, bf16[320,512]{1,0:T(8,128)(2,1)}, bf16[64,384]{1,0:T(8,128)(2,1)}, bf16[256,2048]{1,0:T(8,128)(2,1)}) custom-call(bf16[256,512]{1,0:T(8,128)(2,1)} %refs_0_.1, bf16[256,512]{1,0:T(8,128)(2,1)} %refs_1_.1, bf16[256,512]{1,0:T(8,128)(2,1)} %refs_2_.1, f32[256,256]{1,0:T(8,128)} %refs_6_.3, ...), custom_call_target="tpu_custom_call" | custom-call | bytes 4440064 | tf_op jit(solution)/shard_map/pallas_call | solution.py:24
  3.7 3.0 %collective-permute-start = (bf16[256,2048]{1,0:T(8,128)(2,1)}, bf16[256,2048]{1,0:T(8,128)(2,1)S(1)}, u32[]{:S(2)}, u32[]{:S(2)}) collective-permute-start(bf16[256,2048]{1,0:T(8,128)(2,1)} %get-tuple-element.64.refs_0_), channel_id=1, source_target_pairs={{0,8},{8,0},{16,24},{24,16},{1,9},{9,1},{17,25},{25,17},{2,10},{10... | collective-permute-start | bytes 3145736 | tf_op jit(solution)/shard_map/ppermute | solution.py:227
  6.7 2.6 %collective-permute-start.2 = (bf16[256,512]{1,0:T(8,128)(2,1)}, bf16[256,512]{1,0:T(8,128)(2,1)S(1)}, u32[]{:S(2)}, u32[]{:S(2)}) collective-permute-start(bf16[256,512]{1,0:T(8,128)(2,1)} %get-tuple-element.57), channel_id=1, source_target_pairs={{0,4},{1,5},{2,6},{3,7},{4,0},{5,1},{6,2},{7,3},{8,12},{9,13},{10,... | collective-permute-start | bytes 786440 | tf_op jit(solution)/shard_map/ppermute | solution.py:235
  9.3 1.6 %collective-permute-start.1 = (bf16[256,512]{1,0:T(8,128)(2,1)}, bf16[256,512]{1,0:T(8,128)(2,1)S(1)}, u32[]{:S(2)}, u32[]{:S(2)}) collective-permute-start(bf16[256,512]{1,0:T(8,128)(2,1)} %get-tuple-element.57), channel_id=1, source_target_pairs={{0,2},{1,3},{2,0},{3,1},{4,6},{5,7},{6,4},{7,5},{8,10},{9,11},{10,... | collective-permute-start | bytes 786440 | tf_op jit(solution)/shard_map/ppermute | solution.py:235
  10.9 11.4 %collective-permute-done.2.refs_7_ = bf16[256,512]{1,0:T(8,128)(2,1)S(1)} collective-permute-done((bf16[256,512]{1,0:T(8,128)(2,1)}, bf16[256,512]{1,0:T(8,128)(2,1)S(1)}, u32[]{:S(2)}, u32[]{:S(2)}) %collective-permute-start.2) | collective-permute-done | bytes 262176 | tf_op jit(solution)/shard_map/ppermute | solution.py:235
  22.5 1.4 %collective-permute-start.5 = (bf16[256,512]{1,0:T(8,128)(2,1)S(1)}, bf16[256,512]{1,0:T(8,128)(2,1)S(1)}, u32[]{:S(2)}, u32[]{:S(2)}) collective-permute-start(bf16[256,512]{1,0:T(8,128)(2,1)S(1)} %collective-permute-done.2.refs_7_), channel_id=1, source_target_pairs={{0,2},{1,3},{2,0},{3,1},{4,6},{5,7},{6,4},{7,5},{8,10},{9,11},{10,... | collective-permute-start | bytes 786440 | tf_op jit(solution)/shard_map/ppermute | solution.py:224
  24.0 0.8 collective-permute-start.4
  24.8 0.8 maximum_bitcast_fusion
  25.6 3.0 %collective-permute-start.6 = (bf16[1,2,64,384]{3,2,1,0:T(8,128)(2,1)S(1)}, bf16[1,2,64,384]{3,2,1,0:T(8,128)(2,1)S(1)}, u32[]{:S(2)}, u32[]{:S(2)}) collective-permute-start(bf16[1,2,64,384]{3,2,1,0:T(8,128)(2,1)S(1)} %maximum_bitcast_fusion), channel_id=1, source_target_pairs={{0,4},{1,5},{2,6},{3,7},{4,0},{5,1},{6,2},{7,3},{8,12},{9,13},{10,... | collective-permute-start | bytes 294920 | tf_op jit(solution)/shard_map/ppermute | solution.py:224
  28.6 3.0 %collective-permute-done.6 = bf16[1,2,64,384]{3,2,1,0:T(8,128)(2,1)S(1)} collective-permute-done((bf16[1,2,64,384]{3,2,1,0:T(8,128)(2,1)S(1)}, bf16[1,2,64,384]{3,2,1,0:T(8,128)(2,1)S(1)}, u32[]{:S(2)}, u32[]{:S(2)}) %collective-permute-start.6) | collective-permute-done | bytes 98336 | tf_op jit(solution)/shard_map/ppermute | solution.py:224
  32.3 5.1 %collective-permute-done.4.refs_9_ = bf16[512,512]{1,0:T(8,128)(2,1)S(1)} collective-permute-done((bf16[512,512]{1,0:T(8,128)(2,1)S(1)}, bf16[512,512]{1,0:T(8,128)(2,1)S(1)}, u32[]{:S(2)}, u32[]{:S(2)}) %collective-permute-start.4) | collective-permute-done | bytes 524320 | tf_op jit(solution)/shard_map/ppermute | solution.py:227
  37.9 1.0 %collective-permute-start.10 = (bf16[2,2,64,384]{3,2,1,0:T(8,128)(2,1)S(1)}, bf16[2,2,64,384]{3,2,1,0:T(8,128)(2,1)S(1)}, u32[]{:S(2)}, u32[]{:S(2)}) collective-permute-start(bf16[2,2,64,384]{3,2,1,0:T(8,128)(2,1)S(1)} %pad_maximum_fusion.4), channel_id=1, source_target_pairs={{0,2},{1,3},{2,0},{3,1},{4,6},{5,7},{6,4},{7,5},{8,10},{9,11},{10,... | collective-permute-start | bytes 589832 | tf_op jit(solution)/shard_map/ppermute | solution.py:224
  38.9 1.7 %collective-permute-start.7 = (bf16[256,512]{1,0:T(8,128)(2,1)S(1)}, bf16[256,512]{1,0:T(8,128)(2,1)S(1)}, u32[]{:S(2)}, u32[]{:S(2)}) collective-permute-start(bf16[256,512]{1,0:T(8,128)(2,1)S(1)} %collective-permute-done.5.refs_8_), channel_id=1, source_target_pairs={{0,16},{8,24},{16,0},{24,8},{1,17},{9,25},{17,1},{25,9},{2,18},{10... | collective-permute-start | bytes 786440 | tf_op jit(solution)/shard_map/ppermute | solution.py:227
  40.6 4.1 %collective-permute-done.10 = bf16[2,2,64,384]{3,2,1,0:T(8,128)(2,1)S(1)} collective-permute-done((bf16[2,2,64,384]{3,2,1,0:T(8,128)(2,1)S(1)}, bf16[2,2,64,384]{3,2,1,0:T(8,128)(2,1)S(1)}, u32[]{:S(2)}, u32[]{:S(2)}) %collective-permute-start.10) | collective-permute-done | bytes 196640 | tf_op jit(solution)/shard_map/ppermute | solution.py:224
  44.7 2.1 %collective-permute-done.7.refs_10_ = bf16[256,512]{1,0:T(8,128)(2,1)S(1)} collective-permute-done((bf16[256,512]{1,0:T(8,128)(2,1)S(1)}, bf16[256,512]{1,0:T(8,128)(2,1)S(1)}, u32[]{:S(2)}, u32[]{:S(2)}) %collective-permute-start.7) | collective-permute-done | bytes 262176 | tf_op jit(solution)/shard_map/ppermute | solution.py:227
  46.8 2.0 %shard_map.112 = (bf16[512,256]{1,0:T(8,128)(2,1)S(1)}, bf16[512,256]{1,0:T(8,128)(2,1)S(1)}, bf16[512,128]{1,0:T(8,128)(2,1)S(1)}, bf16[2048,512]{1,0:T(8,128)(2,1)S(1)}) custom-call(bf16[256,2048]{1,0:T(8,128)(2,1)S(1)} %copy-done, bf16[256,2048]{1,0:T(8,128)(2,1)S(1)} %collective-permute-done.8.refs_1_, ...), custom_call_target="tpu_custom_call" | custom-call | flops 1342177280 | bytes 9109504 | tf_op jit(solution)/shard_map/pallas_call | solution.py:24
  48.9 1.5 %shard_map.113 = (f32[128,2048]{1,0:T(8,128)S(1)}, f32[128,2048]{1,0:T(8,128)S(1)}, bf16[128,2048]{1,0:T(8,128)(2,1)S(1)}, bf16[128,2048]{1,0:T(8,128)(2,1)S(1)}) custom-call(bf16[512,256]{1,0:T(8,128)(2,1)S(1)} %get-tuple-element.76.dgu_ref, bf16[2048,512]{1,0:T(8,128)(2,1)S(1)} %get-tuple-element.77.full_ref), custom_call_target="tpu_custom_call" | custom-call | flops 536870912 | bytes 5505024 | tf_op jit(solution)/shard_map/pallas_call | solution.py:24
  52.6 1.1 %collective-permute-start.14 = (bf16[3,64,128]{2,1,0:T(8,128)(2,1)S(1)}, bf16[3,64,128]{2,1,0:T(8,128)(2,1)S(1)}, u32[]{:S(2)}, u32[]{:S(2)}) collective-permute-start(bf16[3,64,128]{2,1,0:T(8,128)(2,1)S(1)} %get-tuple-element.91), channel_id=1, source_target_pairs={{0,2},{1,3},{2,0},{3,1},{4,6},{5,7},{6,4},{7,5},{8,10},{9,11},{10,... | collective-permute-start | bytes 147464 | tf_op jit(solution)/shard_map/ppermute | solution.py:224
  53.7 2.6 %collective-permute-start.15 = (bf16[3,64,128]{2,1,0:T(8,128)(2,1)S(1)}, bf16[3,64,128]{2,1,0:T(8,128)(2,1)S(1)}, u32[]{:S(2)}, u32[]{:S(2)}) collective-permute-start(bf16[3,64,128]{2,1,0:T(8,128)(2,1)S(1)} %get-tuple-element.92), channel_id=1, source_target_pairs={{0,4},{1,5},{2,6},{3,7},{4,0},{5,1},{6,2},{7,3},{8,12},{9,13},{10,... | collective-permute-start | bytes 147464 | tf_op jit(solution)/shard_map/ppermute | solution.py:224
  56.3 0.7 collective-permute-start.16
  57.1 0.9 %collective-permute-start.22 = (bf16[128,2048]{1,0:T(8,128)(2,1)S(1)}, bf16[128,2048]{1,0:T(8,128)(2,1)S(1)}, u32[]{:S(2)}, u32[]{:S(2)}) collective-permute-start(bf16[128,2048]{1,0:T(8,128)(2,1)S(1)} %add_convert_fusion.1), channel_id=1, source_target_pairs={{0,8},{8,0},{16,24},{24,16},{1,9},{9,1},{17,25},{25,17},{2,10},{10... | collective-permute-start | bytes 1572872 | tf_op jit(solution)/shard_map/ppermute | solution.py:227
  57.9 5.0 %collective-permute-done.17.refs_4_ = bf16[4,2,64,384]{3,2,1,0:T(8,128)(2,1)S(1)} collective-permute-done((bf16[4,2,64,384]{3,2,1,0:T(8,128)(2,1)S(1)}, bf16[4,2,64,384]{3,2,1,0:T(8,128)(2,1)S(1)}, u32[]{:S(2)}, u32[]{:S(2)}) %collective-permute-start.17) | collective-permute-done | bytes 393248 | tf_op jit(solution)/shard_map/ppermute | solution.py:227
  63.0 1.8 %collective-permute-start.18 = (bf16[3,64,128]{2,1,0:T(8,128)(2,1)S(1)}, bf16[3,64,128]{2,1,0:T(8,128)(2,1)S(1)}, u32[]{:S(2)}, u32[]{:S(2)}) collective-permute-start(bf16[3,64,128]{2,1,0:T(8,128)(2,1)S(1)} %add_convert_fusion.3), channel_id=1, source_target_pairs={{0,16},{8,24},{16,0},{24,8},{1,17},{9,25},{17,1},{25,9},{2,18},{10... | collective-permute-start | bytes 147464 | tf_op jit(solution)/shard_map/ppermute | solution.py:227
  64.8 2.4 %collective-permute-done.18 = bf16[3,64,128]{2,1,0:T(8,128)(2,1)S(1)} collective-permute-done((bf16[3,64,128]{2,1,0:T(8,128)(2,1)S(1)}, bf16[3,64,128]{2,1,0:T(8,128)(2,1)S(1)}, u32[]{:S(2)}, u32[]{:S(2)}) %collective-permute-start.18) | collective-permute-done | bytes 49184 | tf_op jit(solution)/shard_map/ppermute | solution.py:227
  67.1 3.2 %collective-permute-start.21 = (bf16[3,64,128]{2,1,0:T(8,128)(2,1)S(1)}, bf16[3,64,128]{2,1,0:T(8,128)(2,1)S(1)}, u32[]{:S(2)}, u32[]{:S(2)}) collective-permute-start(bf16[3,64,128]{2,1,0:T(8,128)(2,1)S(1)} %add_convert_fusion.2), channel_id=1, source_target_pairs={{0,6},{1,7},{2,4},{3,5},{4,2},{5,3},{6,0},{7,1},{8,14},{9,15},{10,... | collective-permute-start | bytes 147464 | tf_op jit(solution)/shard_map/ppermute | solution.py:224
  70.3 1.3 %collective-permute-start.19 = (bf16[3,64,128]{2,1,0:T(8,128)(2,1)S(1)}, bf16[3,64,128]{2,1,0:T(8,128)(2,1)S(1)}, u32[]{:S(2)}, u32[]{:S(2)}) collective-permute-start(bf16[3,64,128]{2,1,0:T(8,128)(2,1)S(1)} %add_convert_fusion.2), channel_id=1, source_target_pairs={{0,2},{1,3},{2,0},{3,1},{4,6},{5,7},{6,4},{7,5},{8,10},{9,11},{10,... | collective-permute-start | bytes 147464 | tf_op jit(solution)/shard_map/ppermute | solution.py:224
  71.6 1.7 %collective-permute-done.21 = bf16[3,64,128]{2,1,0:T(8,128)(2,1)S(1)} collective-permute-done((bf16[3,64,128]{2,1,0:T(8,128)(2,1)S(1)}, bf16[3,64,128]{2,1,0:T(8,128)(2,1)S(1)}, u32[]{:S(2)}, u32[]{:S(2)}) %collective-permute-start.21) | collective-permute-done | bytes 49184 | tf_op jit(solution)/shard_map/ppermute | solution.py:224
  73.3 2.0 %collective-permute-done.20 = bf16[3,64,128]{2,1,0:T(8,128)(2,1)S(1)} collective-permute-done((bf16[3,64,128]{2,1,0:T(8,128)(2,1)S(1)}, bf16[3,64,128]{2,1,0:T(8,128)(2,1)S(1)}, u32[]{:S(2)}, u32[]{:S(2)}) %collective-permute-start.20) | collective-permute-done | bytes 49184 | tf_op jit(solution)/shard_map/ppermute | solution.py:224
  76.1 4.9 %collective-permute-done.23.refs_1_ = bf16[4,3,64,128]{3,2,1,0:T(8,128)(2,1)S(1)} collective-permute-done((bf16[4,3,64,128]{3,2,1,0:T(8,128)(2,1)S(1)}, bf16[4,3,64,128]{3,2,1,0:T(8,128)(2,1)S(1)}, u32[]{:S(2)}, u32[]{:S(2)}) %collective-permute-start.23) | collective-permute-done | bytes 196640 | tf_op jit(solution)/shard_map/ppermute | solution.py:227
  81.2 1.0 %add_convert_fusion = bf16[128,2048]{1,0:T(8,128)(2,1)} fusion(bf16[128,2048]{1,0:T(8,128)(2,1)S(1)} %collective-permute-done.22, f32[128,2048]{1,0:T(8,128)S(1)} %get-tuple-element.78, bf16[128,2048]{1,0:T(8,128)(2,1)S(1)} %collective-permute-done.11), kind=kLoop, calls=%fused_computation | loop fusion | flops 1310720 | bytes 2621440 | tf_op jit(solution)/shard_map/convert_element_type | solution.py:348
  82.2 0.7 collective-permute-done.24.refs_2_
  82.9 3.2 %shard_map.115 = (f32[3,32,512]{2,1,0:T(8,128)}, f32[3,32,512]{2,1,0:T(8,128)}, f32[3,256,512]{2,1,0:T(8,128)}) custom-call(bf16[4,3,64,128]{3,2,1,0:T(8,128)(2,1)S(1)} %get-tuple-element.109.refs_0_, bf16[4,3,64,128]{3,2,1,0:T(8,128)(2,1)S(1)} %collective-permute-done.23.refs_1_, bf16[2,4,3,64,128]{4,3,2,1,0:T(8,128)(2,1)S(1)} %collective-permute-done.24.refs_2_, ...), custom_call_target="tpu_custom_call" | custom-call | flops 402653184 | bytes 4980736 | tf_op jit(solution)/shard_map/pallas_call | solution.py:24
  (47 shorter events, 4.8 us)
Async XLA Ops:
  3.7 43.1 %copy-start = (bf16[256,2048]{1,0:T(8,128)(2,1)S(1)}, bf16[256,2048]{1,0:T(8,128)(2,1)}, u32[]{:S(2)}) copy-start(bf16[256,2048]{1,0:T(8,128)(2,1)} %get-tuple-element.64.refs_0_) | copy-start | bytes 3145732
  3.7 43.1 %copy-start.4 = (bf16[256,512]{1,0:T(8,128)(2,1)S(1)}, bf16[256,512]{1,0:T(8,128)(2,1)}, u32[]{:S(2)}) copy-start(bf16[256,512]{1,0:T(8,128)(2,1)} %get-tuple-element.71.refs_4_) | copy-start | bytes 786436
  3.7 33.6 %collective-permute-start = (bf16[256,2048]{1,0:T(8,128)(2,1)}, bf16[256,2048]{1,0:T(8,128)(2,1)S(1)}, u32[]{:S(2)}, u32[]{:S(2)}) collective-permute-start(bf16[256,2048]{1,0:T(8,128)(2,1)} %get-tuple-element.64.refs_0_), channel_id=1, source_target_pairs={{0,8},{8,0},{16,24},{24,16},{1,9},{9,1},{17,25},{25,17},{2,10},{10... | collective-permute-start | bytes 3145736 | tf_op jit(solution)/shard_map/ppermute | solution.py:227
  6.7 15.7 %collective-permute-start.3 = (bf16[320,512]{1,0:T(8,128)(2,1)}, bf16[320,512]{1,0:T(8,128)(2,1)S(1)}, u32[]{:S(2)}, u32[]{:S(2)}) collective-permute-start(bf16[320,512]{1,0:T(8,128)(2,1)} %get-tuple-element.58), channel_id=1, source_target_pairs={{0,1},{1,0},{2,3},{3,2},{4,5},{5,4},{6,7},{7,6},{8,9},{9,8},{10,11... | collective-permute-start | bytes 983048 | tf_op jit(solution)/shard_map/ppermute | solution.py:224
  6.7 15.6 %collective-permute-start.2 = (bf16[256,512]{1,0:T(8,128)(2,1)}, bf16[256,512]{1,0:T(8,128)(2,1)S(1)}, u32[]{:S(2)}, u32[]{:S(2)}) collective-permute-start(bf16[256,512]{1,0:T(8,128)(2,1)} %get-tuple-element.57), channel_id=1, source_target_pairs={{0,4},{1,5},{2,6},{3,7},{4,0},{5,1},{6,2},{7,3},{8,12},{9,13},{10,... | collective-permute-start | bytes 786440 | tf_op jit(solution)/shard_map/ppermute | solution.py:235
  9.3 13.2 %collective-permute-start.1 = (bf16[256,512]{1,0:T(8,128)(2,1)}, bf16[256,512]{1,0:T(8,128)(2,1)S(1)}, u32[]{:S(2)}, u32[]{:S(2)}) collective-permute-start(bf16[256,512]{1,0:T(8,128)(2,1)} %get-tuple-element.57), channel_id=1, source_target_pairs={{0,2},{1,3},{2,0},{3,1},{4,6},{5,7},{6,4},{7,5},{8,10},{9,11},{10,... | collective-permute-start | bytes 786440 | tf_op jit(solution)/shard_map/ppermute | solution.py:235
  22.5 9.8 %collective-permute-start.5 = (bf16[256,512]{1,0:T(8,128)(2,1)S(1)}, bf16[256,512]{1,0:T(8,128)(2,1)S(1)}, u32[]{:S(2)}, u32[]{:S(2)}) collective-permute-start(bf16[256,512]{1,0:T(8,128)(2,1)S(1)} %collective-permute-done.2.refs_7_), channel_id=1, source_target_pairs={{0,2},{1,3},{2,0},{3,1},{4,6},{5,7},{6,4},{7,5},{8,10},{9,11},{10,... | collective-permute-start | bytes 786440 | tf_op jit(solution)/shard_map/ppermute | solution.py:224
  24.0 13.4 %collective-permute-start.4 = (bf16[512,512]{1,0:T(8,128)(2,1)S(1)}, bf16[512,512]{1,0:T(8,128)(2,1)S(1)}, u32[]{:S(2)}, u32[]{:S(2)}) collective-permute-start(bf16[512,512]{1,0:T(8,128)(2,1)S(1)} %pad_maximum_fusion.1), channel_id=1, source_target_pairs={{0,16},{8,24},{16,0},{24,8},{1,17},{9,25},{17,1},{25,9},{2,18},{10... | collective-permute-start | bytes 1572872 | tf_op jit(solution)/shard_map/ppermute | solution.py:227
  25.6 6.0 %collective-permute-start.6 = (bf16[1,2,64,384]{3,2,1,0:T(8,128)(2,1)S(1)}, bf16[1,2,64,384]{3,2,1,0:T(8,128)(2,1)S(1)}, u32[]{:S(2)}, u32[]{:S(2)}) collective-permute-start(bf16[1,2,64,384]{3,2,1,0:T(8,128)(2,1)S(1)} %maximum_bitcast_fusion), channel_id=1, source_target_pairs={{0,4},{1,5},{2,6},{3,7},{4,0},{5,1},{6,2},{7,3},{8,12},{9,13},{10,... | collective-permute-start | bytes 294920 | tf_op jit(solution)/shard_map/ppermute | solution.py:224
  37.4 9.4 %collective-permute-start.8 = (bf16[256,2048]{1,0:T(8,128)(2,1)}, bf16[256,2048]{1,0:T(8,128)(2,1)S(1)}, u32[]{:S(2)}, u32[]{:S(2)}) collective-permute-start(bf16[256,2048]{1,0:T(8,128)(2,1)} %get-tuple-element.64.refs_0_), channel_id=1, source_target_pairs={{0,1},{1,0},{2,3},{3,2},{4,5},{5,4},{6,7},{7,6},{8,9},{9,8},{10,11... | collective-permute-start | bytes 3145736 | tf_op jit(solution)/shard_map/ppermute | solution.py:224
  37.4 9.4 %collective-permute-start.9 = (bf16[256,2048]{1,0:T(8,128)(2,1)S(1)}, bf16[256,2048]{1,0:T(8,128)(2,1)S(1)}, u32[]{:S(2)}, u32[]{:S(2)}) collective-permute-start(bf16[256,2048]{1,0:T(8,128)(2,1)S(1)} %collective-permute-done.refs_2_), channel_id=1, source_target_pairs={{0,1},{1,0},{2,3},{3,2},{4,5},{5,4},{6,7},{7,6},{8,9},{9,8},{10,11... | collective-permute-start | bytes 3145736 | tf_op jit(solution)/shard_map/ppermute | solution.py:224
  37.9 6.8 %collective-permute-start.10 = (bf16[2,2,64,384]{3,2,1,0:T(8,128)(2,1)S(1)}, bf16[2,2,64,384]{3,2,1,0:T(8,128)(2,1)S(1)}, u32[]{:S(2)}, u32[]{:S(2)}) collective-permute-start(bf16[2,2,64,384]{3,2,1,0:T(8,128)(2,1)S(1)} %pad_maximum_fusion.4), channel_id=1, source_target_pairs={{0,2},{1,3},{2,0},{3,1},{4,6},{5,7},{6,4},{7,5},{8,10},{9,11},{10,... | collective-permute-start | bytes 589832 | tf_op jit(solution)/shard_map/ppermute | solution.py:224
  38.9 7.9 %collective-permute-start.7 = (bf16[256,512]{1,0:T(8,128)(2,1)S(1)}, bf16[256,512]{1,0:T(8,128)(2,1)S(1)}, u32[]{:S(2)}, u32[]{:S(2)}) collective-permute-start(bf16[256,512]{1,0:T(8,128)(2,1)S(1)} %collective-permute-done.5.refs_8_), channel_id=1, source_target_pairs={{0,16},{8,24},{16,0},{24,8},{1,17},{9,25},{17,1},{25,9},{2,18},{10... | collective-permute-start | bytes 786440 | tf_op jit(solution)/shard_map/ppermute | solution.py:227
  48.8 1.6 %collective-permute-start.12 = (bf16[512,256]{1,0:T(8,128)(2,1)S(1)}, bf16[512,256]{1,0:T(8,128)(2,1)S(1)}, u32[]{:S(2)}, u32[]{:S(2)}) collective-permute-start(bf16[512,256]{1,0:T(8,128)(2,1)S(1)} %get-tuple-element.80.mine_ref), channel_id=1, source_target_pairs={{0,1},{1,0},{2,3},{3,2},{4,5},{5,4},{6,7},{7,6},{8,9},{9,8},{10,11... | collective-permute-start | bytes 786440 | tf_op jit(solution)/shard_map/ppermute | solution.py:224
  50.4 2.1 %collective-permute-start.13 = (bf16[128,2048]{1,0:T(8,128)(2,1)S(1)}, bf16[128,2048]{1,0:T(8,128)(2,1)S(1)}, u32[]{:S(2)}, u32[]{:S(2)}) collective-permute-start(bf16[128,2048]{1,0:T(8,128)(2,1)S(1)} %get-tuple-element.89), channel_id=1, source_target_pairs={{0,1},{1,0},{2,3},{3,2},{4,5},{5,4},{6,7},{7,6},{8,9},{9,8},{10,11... | collective-permute-start | bytes 1572872 | tf_op jit(solution)/shard_map/ppermute | solution.py:224
  50.9 12.0 %collective-permute-start.17 = (bf16[4,2,64,384]{3,2,1,0:T(8,128)(2,1)S(1)}, bf16[4,2,64,384]{3,2,1,0:T(8,128)(2,1)S(1)}, u32[]{:S(2)}, u32[]{:S(2)}) collective-permute-start(bf16[4,2,64,384]{3,2,1,0:T(8,128)(2,1)S(1)} %pad_maximum_fusion.2.refs_3_), channel_id=1, source_target_pairs={{0,8},{8,0},{16,24},{24,16},{1,9},{9,1},{17,25},{25,17},{2,10},{10... | collective-permute-start | bytes 1179656 | tf_op jit(solution)/shard_map/ppermute | solution.py:227
  52.6 10.3 %collective-permute-start.14 = (bf16[3,64,128]{2,1,0:T(8,128)(2,1)S(1)}, bf16[3,64,128]{2,1,0:T(8,128)(2,1)S(1)}, u32[]{:S(2)}, u32[]{:S(2)}) collective-permute-start(bf16[3,64,128]{2,1,0:T(8,128)(2,1)S(1)} %get-tuple-element.91), channel_id=1, source_target_pairs={{0,2},{1,3},{2,0},{3,1},{4,6},{5,7},{6,4},{7,5},{8,10},{9,11},{10,... | collective-permute-start | bytes 147464 | tf_op jit(solution)/shard_map/ppermute | solution.py:224
  53.7 9.2 %collective-permute-start.15 = (bf16[3,64,128]{2,1,0:T(8,128)(2,1)S(1)}, bf16[3,64,128]{2,1,0:T(8,128)(2,1)S(1)}, u32[]{:S(2)}, u32[]{:S(2)}) collective-permute-start(bf16[3,64,128]{2,1,0:T(8,128)(2,1)S(1)} %get-tuple-element.92), channel_id=1, source_target_pairs={{0,4},{1,5},{2,6},{3,7},{4,0},{5,1},{6,2},{7,3},{8,12},{9,13},{10,... | collective-permute-start | bytes 147464 | tf_op jit(solution)/shard_map/ppermute | solution.py:224
  56.3 6.6 %collective-permute-start.16 = (bf16[3,64,128]{2,1,0:T(8,128)(2,1)S(1)}, bf16[3,64,128]{2,1,0:T(8,128)(2,1)S(1)}, u32[]{:S(2)}, u32[]{:S(2)}) collective-permute-start(bf16[3,64,128]{2,1,0:T(8,128)(2,1)S(1)} %get-tuple-element.93), channel_id=1, source_target_pairs={{0,6},{1,7},{2,4},{3,5},{4,2},{5,3},{6,0},{7,1},{8,14},{9,15},{10,... | collective-permute-start | bytes 147464 | tf_op jit(solution)/shard_map/ppermute | solution.py:224
  57.1 18.2 %collective-permute-start.22 = (bf16[128,2048]{1,0:T(8,128)(2,1)S(1)}, bf16[128,2048]{1,0:T(8,128)(2,1)S(1)}, u32[]{:S(2)}, u32[]{:S(2)}) collective-permute-start(bf16[128,2048]{1,0:T(8,128)(2,1)S(1)} %add_convert_fusion.1), channel_id=1, source_target_pairs={{0,8},{8,0},{16,24},{24,16},{1,9},{9,1},{17,25},{25,17},{2,10},{10... | collective-permute-start | bytes 1572872 | tf_op jit(solution)/shard_map/ppermute | solution.py:227
  63.0 4.2 %collective-permute-start.18 = (bf16[3,64,128]{2,1,0:T(8,128)(2,1)S(1)}, bf16[3,64,128]{2,1,0:T(8,128)(2,1)S(1)}, u32[]{:S(2)}, u32[]{:S(2)}) collective-permute-start(bf16[3,64,128]{2,1,0:T(8,128)(2,1)S(1)} %add_convert_fusion.3), channel_id=1, source_target_pairs={{0,16},{8,24},{16,0},{24,8},{1,17},{9,25},{17,1},{25,9},{2,18},{10... | collective-permute-start | bytes 147464 | tf_op jit(solution)/shard_map/ppermute | solution.py:227
  67.1 6.1 %collective-permute-start.21 = (bf16[3,64,128]{2,1,0:T(8,128)(2,1)S(1)}, bf16[3,64,128]{2,1,0:T(8,128)(2,1)S(1)}, u32[]{:S(2)}, u32[]{:S(2)}) collective-permute-start(bf16[3,64,128]{2,1,0:T(8,128)(2,1)S(1)} %add_convert_fusion.2), channel_id=1, source_target_pairs={{0,6},{1,7},{2,4},{3,5},{4,2},{5,3},{6,0},{7,1},{8,14},{9,15},{10,... | collective-permute-start | bytes 147464 | tf_op jit(solution)/shard_map/ppermute | solution.py:224
  70.3 5.0 %collective-permute-start.20 = (bf16[3,64,128]{2,1,0:T(8,128)(2,1)S(1)}, bf16[3,64,128]{2,1,0:T(8,128)(2,1)S(1)}, u32[]{:S(2)}, u32[]{:S(2)}) collective-permute-start(bf16[3,64,128]{2,1,0:T(8,128)(2,1)S(1)} %add_convert_fusion.2), channel_id=1, source_target_pairs={{0,4},{1,5},{2,6},{3,7},{4,0},{5,1},{6,2},{7,3},{8,12},{9,13},{10,... | collective-permute-start | bytes 147464 | tf_op jit(solution)/shard_map/ppermute | solution.py:224
  70.3 5.0 %collective-permute-start.19 = (bf16[3,64,128]{2,1,0:T(8,128)(2,1)S(1)}, bf16[3,64,128]{2,1,0:T(8,128)(2,1)S(1)}, u32[]{:S(2)}, u32[]{:S(2)}) collective-permute-start(bf16[3,64,128]{2,1,0:T(8,128)(2,1)S(1)} %add_convert_fusion.2), channel_id=1, source_target_pairs={{0,2},{1,3},{2,0},{3,1},{4,6},{5,7},{6,4},{7,5},{8,10},{9,11},{10,... | collective-permute-start | bytes 147464 | tf_op jit(solution)/shard_map/ppermute | solution.py:224
  71.6 9.6 %collective-permute-start.11 = (bf16[128,2048]{1,0:T(8,128)(2,1)S(1)}, bf16[128,2048]{1,0:T(8,128)(2,1)S(1)}, u32[]{:S(2)}, u32[]{:S(2)}) collective-permute-start(bf16[128,2048]{1,0:T(8,128)(2,1)S(1)} %get-tuple-element.79), channel_id=1, source_target_pairs={{0,1},{1,0},{2,3},{3,2},{4,5},{5,4},{6,7},{7,6},{8,9},{9,8},{10,11... | collective-permute-start | bytes 1572872 | tf_op jit(solution)/shard_map/ppermute | solution.py:224
  75.3 5.7 %collective-permute-start.23 = (bf16[4,3,64,128]{3,2,1,0:T(8,128)(2,1)S(1)}, bf16[4,3,64,128]{3,2,1,0:T(8,128)(2,1)S(1)}, u32[]{:S(2)}, u32[]{:S(2)}) collective-permute-start(bf16[4,3,64,128]{3,2,1,0:T(8,128)(2,1)S(1)} %get-tuple-element.109.refs_0_), channel_id=1, source_target_pairs={{0,8},{8,0},{16,24},{24,16},{1,9},{9,1},{17,25},{25,17},{2,10},{10... | collective-permute-start | bytes 589832 | tf_op jit(solution)/shard_map/ppermute | solution.py:227
  76.0 6.9 %copy-start.1 = (f32[256,256]{1,0:T(8,128)S(1)}, f32[256,256]{1,0:T(8,128)}, u32[]{:S(2)}) copy-start(f32[256,256]{1,0:T(8,128)} %refs_6_.3) | copy-start | bytes 786436
  76.0 6.9 %copy-start.2 = (f32[3,32,512]{2,1,0:T(8,128)S(1)}, f32[3,32,512]{2,1,0:T(8,128)}, u32[]{:S(2)}) copy-start(f32[3,32,512]{2,1,0:T(8,128)} %refs_7_.3) | copy-start | bytes 589828
  76.1 6.9 %copy-start.3 = (f32[3,32,512]{2,1,0:T(8,128)S(1)}, f32[3,32,512]{2,1,0:T(8,128)}, u32[]{:S(2)}) copy-start(f32[3,32,512]{2,1,0:T(8,128)} %refs_8_.1) | copy-start | bytes 589828
  76.1 6.1 %collective-permute-start.25 = (bf16[2,4,2,64,384]{4,3,2,1,0:T(8,128)(2,1)S(1)}, bf16[2,4,2,64,384]{4,3,2,1,0:T(8,128)(2,1)S(1)}, u32[]{:S(2)}, u32[]{:S(2)}) collective-permute-start(bf16[2,4,2,64,384]{4,3,2,1,0:T(8,128)(2,1)S(1)} %pad_maximum_fusion), channel_id=1, source_target_pairs={{0,1},{1,0},{2,3},{3,2},{4,5},{5,4},{6,7},{7,6},{8,9},{9,8},{10,11... | collective-permute-start | bytes 2359304 | tf_op jit(solution)/shard_map/ppermute | solution.py:224
  81.1 1.8 %collective-permute-start.24 = (bf16[2,4,3,64,128]{4,3,2,1,0:T(8,128)(2,1)S(1)}, bf16[2,4,3,64,128]{4,3,2,1,0:T(8,128)(2,1)S(1)}, u32[]{:S(2)}, u32[]{:S(2)}) collective-permute-start(bf16[2,4,3,64,128]{4,3,2,1,0:T(8,128)(2,1)S(1)} %pad_maximum_fusion.3), channel_id=1, source_target_pairs={{0,1},{1,0},{2,3},{3,2},{4,5},{5,4},{6,7},{7,6},{8,9},{9,8},{10,11... | collective-permute-start | bytes 1179656 | tf_op jit(solution)/shard_map/ppermute | solution.py:224

commit v3 on v2

--- a/solution.py
+++ b/solution.py
@@ -18,13 +18,15 @@
     return lax.dot_general(left, right, dims, preferred_element_type=F32)
 
 
-def call(body, outs, scratch, flops, *operands, space=pltpu.VMEM, mib=40):
+def call(body, outs, scratch, flops, *operands, pinned=False, mib=40):
+    if pinned:
+        operands = [pltpu.with_memory_space_constraint(o, pltpu.HBM) for o in operands]
     moved = sum(o.size * o.dtype.itemsize for o in operands)
     moved += sum(math.prod(s) * jnp.dtype(d).itemsize for s, d in outs)
     return pl.pallas_call(
         body,
-        out_shape=[jax.ShapeDtypeStruct(s, d) for s, d in outs],
-        in_specs=[pl.BlockSpec(memory_space=space)] * len(operands),
+        out_shape=[(pltpu.VMEM if pinned else jax.ShapeDtypeStruct)(s, d) for s, d in outs],
+        in_specs=[pl.BlockSpec(memory_space=pltpu.HBM if pinned else pltpu.VMEM)] * len(operands),
         out_specs=[pl.BlockSpec(memory_space=pltpu.VMEM)] * len(outs),
         scratch_shapes=scratch,
         compiler_params=pltpu.CompilerParams(vmem_limit_bytes=mib * 1024 * 1024),
@@ -255,8 +257,8 @@
         second_moment,
         tokens,
         cotangent,
-        space=pltpu.HBM,
-        mib=60,
+        pinned=True,
+        mib=16,
     )
     direct = [k for k in range(1, chips) if k & (k - 1) == 0]
     passed = [k for k in range(1, chips) if k & (k - 1)]
@@ -265,17 +267,21 @@
     both_x = by_group(both, 1)
     near = {k: by_chip(sent, 2 * k) for k in reversed(direct)}
     from_core = by_member(to_core, 1)
-    near, from_core, both = ordered((near, from_core, both))
-
-    far = [by_group(jnp.concatenate([near[k] for k in direct]), 2)]
+    groups_of = [direct[:1], direct[1:], passed]
+
+    def forward(which):
+        return by_group(jnp.concatenate([near[k] for k in groups_of[which]]), 2)
+
+    far = [forward(0), forward(1)]
     for k in passed:
         near[k] = by_member(near[k & (k - 1)], 2 * (k & -k))
+    far[0], from_core = ordered((far[0], from_core))
     moms = jnp.stack([mom_mine, from_core[depth:, : parts * unit]])[None]
     for bit in reversed(direct[1:]):
         moms = jnp.concatenate([moms, by_member(moms, 2 * bit)])
     both_x, both, far, near, moms = ordered((both_x, both, far, near, moms))
 
-    far.append(by_group(jnp.concatenate([near[k] for k in passed]), 2))
+    far.append(forward(2))
     both_c = by_member(both, 1)
     both_xc = by_member(both_x, 1)
     moms = jnp.concatenate([moms, by_member(moms, 2)])
@@ -283,8 +289,8 @@
 
     layout = [(0, 0), (1, 0)]
     for k in range(1, chips):
-        i = 0 if k in direct else 1
-        layout += [(1 + k, 0), (1 + chips + i, (direct, passed)[i].index(k) * depth)]
+        i = [k in group for group in groups_of].index(True)
+        layout += [(1 + k, 0), (1 + chips + i, groups_of[i].index(k) * depth)]
     four = 4 * toks
     proj, dgu, hidden, full = call(
         functools.partial(first_kernel, members, tuple(layout), depth, half),

time: 86.3 us -> 80.6 us (0.934)
  waiting for transfers between devices: 43.8 us -> 37.7 us
  starting transfers between devices: 29.1 us -> 31.7 us
  Pallas kernels: 10.1 us -> 8.83 us
    ppermute x7 -> x8, waiting for transfers between devices: 19.4 us -> 15 us  [by_group(): return lax.ppermute(value, 'group', [(i, i ^ bits) for i in range(groups)])]
    ppermute x7 -> x8, starting transfers between devices: 9.38 us -> 12.7 us  [by_group(): return lax.ppermute(value, 'group', [(i, i ^ bits) for i in range(groups)])]
    ppermute x2, waiting for transfers between devices: 11.6 us -> 9.25 us  [by_chip(): return lax.ppermute(value, ('group', 'member'), pairs)]
    ppermute x17, starting transfers between devices: 15.6 us -> 13.3 us  [by_member(): lax.ppermute(value, 'member', [(i, i ^ bits) for i in range(members)])]
    ppermute x2, starting transfers between devices: 4.17 us -> 5.68 us  [by_chip(): return lax.ppermute(value, ('group', 'member'), pairs)]
    pallas_call x5, Pallas kernels: 10.1 us -> 8.83 us  [call(): pl.pallas_call(body, out_shape=[(pltpu.VMEM if pinned else jax.ShapeDtype...]
  transfers between devices with their start and end apart: 26 -> 27, of which waited for: 14 -> 13; matrix products, arithmetic and copies ran while one was open for 3% -> 2% of each run, Pallas kernels for 2% -> 2%
where the time goes in v3:
time: 80.6 us; the launch traced here: 80.5 us
  waiting for transfers between devices  37.7 us (47%)
  starting transfers between devices  31.7 us (39%)
  Pallas kernels  8.83 us (11%)
  other arithmetic  1.39 us (2%)
  between operations  0.81 us (1%)
    ppermute x8, waiting for transfers between devices, by_group(): return lax.ppermute(value, 'group', [(i, i ^ bits) for i in range(groups)])  15 us
    ppermute x17, waiting for transfers between devices, by_member(): lax.ppermute(value, 'member', [(i, i ^ bits) for i in range(members)])  13.5 us
    ppermute x17, starting transfers between devices, by_member(): lax.ppermute(value, 'member', [(i, i ^ bits) for i in range(members)])  13.3 us
    ppermute x8, starting transfers between devices, by_group(): return lax.ppermute(value, 'group', [(i, i ^ bits) for i in range(groups)])  12.7 us
    ppermute x2, waiting for transfers between devices, by_chip(): return lax.ppermute(value, ('group', 'member'), pairs)  9.25 us
    pallas_call x5, Pallas kernels, call(): pl.pallas_call(body, out_shape=[(pltpu.VMEM if pinned else jax.ShapeDtype...  8.83 us
    ppermute x2, starting transfers between devices, by_chip(): return lax.ppermute(value, ('group', 'member'), pairs)  5.68 us
  transfers between devices with their start and end apart: 27, of which 13 were waited for; matrix products, arithmetic and copies ran while one was open for 2% of the time, Pallas kernels for 2%

profile of v3, /device:TPU:0, one launch (start us, length us, event | category | flops | bytes accessed | tf_op | source)
XLA Modules:
  0.0 80.5 jit_solution(12222499843367749950)
XLA Ops:
  0.6 1.8 %shard_map.111 = (bf16[256,512]{1,0:T(8,128)(2,1)S(1)}, bf16[256,512]{1,0:T(8,128)(2,1)S(1)}, bf16[320,512]{1,0:T(8,128)(2,1)S(1)}, bf16[64,384]{1,0:T(8,128)(2,1)S(1)}, bf16[256,2048]{1,0:T(8,128)(2,1)S(1)}) custom-call(bf16[256,512]{1,0:T(8,128)(2,1)} %refs_0_.1, bf16[256,512]{1,0:T(8,128)(2,1)} %refs_1_.1, bf16[256,512]{1,0:T(8,128)(2,1)} %refs_2_.1, ...), custom_call_target="tpu_custom_call" | custom-call | bytes 4440064 | tf_op jit(solution)/shard_map/pallas_call | solution.py:26
  2.4 3.1 %collective-permute-start.1 = (bf16[256,512]{1,0:T(8,128)(2,1)S(1)}, bf16[256,512]{1,0:T(8,128)(2,1)S(1)}, u32[]{:S(2)}, u32[]{:S(2)}) collective-permute-start(bf16[256,512]{1,0:T(8,128)(2,1)S(1)} %get-tuple-element.57), channel_id=1, source_target_pairs={{0,2},{1,3},{2,0},{3,1},{4,6},{5,7},{6,4},{7,5},{8,10},{9,11},{10,... | collective-permute-start | bytes 786440 | tf_op jit(solution)/shard_map/ppermute | solution.py:237
  5.5 1.5 %collective-permute-start = (bf16[256,2048]{1,0:T(8,128)(2,1)S(1)}, bf16[256,2048]{1,0:T(8,128)(2,1)S(1)}, u32[]{:S(2)}, u32[]{:S(2)}) collective-permute-start(bf16[256,2048]{1,0:T(8,128)(2,1)S(1)} %get-tuple-element.62.refs_0_), channel_id=1, source_target_pairs={{0,8},{8,0},{16,24},{24,16},{1,9},{9,1},{17,25},{25,17},{2,10},{10... | collective-permute-start | bytes 3145736 | tf_op jit(solution)/shard_map/ppermute | solution.py:229
  7.0 2.6 %collective-permute-start.4 = (bf16[256,512]{1,0:T(8,128)(2,1)S(1)}, bf16[256,512]{1,0:T(8,128)(2,1)S(1)}, u32[]{:S(2)}, u32[]{:S(2)}) collective-permute-start(bf16[256,512]{1,0:T(8,128)(2,1)S(1)} %get-tuple-element.57), channel_id=1, source_target_pairs={{0,4},{1,5},{2,6},{3,7},{4,0},{5,1},{6,2},{7,3},{8,12},{9,13},{10,... | collective-permute-start | bytes 786440 | tf_op jit(solution)/shard_map/ppermute | solution.py:237
  9.6 4.8 %collective-permute-done.1.refs_6_ = bf16[256,512]{1,0:T(8,128)(2,1)S(1)} collective-permute-done((bf16[256,512]{1,0:T(8,128)(2,1)S(1)}, bf16[256,512]{1,0:T(8,128)(2,1)S(1)}, u32[]{:S(2)}, u32[]{:S(2)}) %collective-permute-start.1) | collective-permute-done | bytes 262176 | tf_op jit(solution)/shard_map/ppermute | solution.py:237
  14.4 3.4 %collective-permute-start.2 = (bf16[256,512]{1,0:T(8,128)(2,1)S(1)}, bf16[256,512]{1,0:T(8,128)(2,1)S(1)}, u32[]{:S(2)}, u32[]{:S(2)}) collective-permute-start(bf16[256,512]{1,0:T(8,128)(2,1)S(1)} %collective-permute-done.1.refs_6_), channel_id=1, source_target_pairs={{0,16},{8,24},{16,0},{24,8},{1,17},{9,25},{17,1},{25,9},{2,18},{10... | collective-permute-start | bytes 786440 | tf_op jit(solution)/shard_map/ppermute | solution.py:229
  17.8 4.5 %collective-permute-done.4.refs_7_ = bf16[256,512]{1,0:T(8,128)(2,1)S(1)} collective-permute-done((bf16[256,512]{1,0:T(8,128)(2,1)S(1)}, bf16[256,512]{1,0:T(8,128)(2,1)S(1)}, u32[]{:S(2)}, u32[]{:S(2)}) %collective-permute-start.4) | collective-permute-done | bytes 262176 | tf_op jit(solution)/shard_map/ppermute | solution.py:237
  23.3 1.3 %collective-permute-done.2.refs_9_ = bf16[256,512]{1,0:T(8,128)(2,1)S(1)} collective-permute-done((bf16[256,512]{1,0:T(8,128)(2,1)S(1)}, bf16[256,512]{1,0:T(8,128)(2,1)S(1)}, u32[]{:S(2)}, u32[]{:S(2)}) %collective-permute-start.2) | collective-permute-done | bytes 262176 | tf_op jit(solution)/shard_map/ppermute | solution.py:229
  24.6 1.7 %collective-permute-start.7 = (bf16[1,2,64,384]{3,2,1,0:T(8,128)(2,1)S(1)}, bf16[1,2,64,384]{3,2,1,0:T(8,128)(2,1)S(1)}, u32[]{:S(2)}, u32[]{:S(2)}) collective-permute-start(bf16[1,2,64,384]{3,2,1,0:T(8,128)(2,1)S(1)} %maximum_bitcast_fusion), channel_id=1, source_target_pairs={{0,4},{1,5},{2,6},{3,7},{4,0},{5,1},{6,2},{7,3},{8,12},{9,13},{10,... | collective-permute-start | bytes 294920 | tf_op jit(solution)/shard_map/ppermute | solution.py:226
  26.3 4.0 %collective-permute-done.7 = bf16[1,2,64,384]{3,2,1,0:T(8,128)(2,1)S(1)} collective-permute-done((bf16[1,2,64,384]{3,2,1,0:T(8,128)(2,1)S(1)}, bf16[1,2,64,384]{3,2,1,0:T(8,128)(2,1)S(1)}, u32[]{:S(2)}, u32[]{:S(2)}) %collective-permute-start.7) | collective-permute-done | bytes 98336 | tf_op jit(solution)/shard_map/ppermute | solution.py:226
  30.3 2.0 %collective-permute-done.6.refs_8_ = bf16[256,512]{1,0:T(8,128)(2,1)S(1)} collective-permute-done((bf16[256,512]{1,0:T(8,128)(2,1)S(1)}, bf16[256,512]{1,0:T(8,128)(2,1)S(1)}, u32[]{:S(2)}, u32[]{:S(2)}) %collective-permute-start.6) | collective-permute-done | bytes 262176 | tf_op jit(solution)/shard_map/ppermute | solution.py:226
  32.9 1.4 %collective-permute-start.11 = (bf16[2,2,64,384]{3,2,1,0:T(8,128)(2,1)S(1)}, bf16[2,2,64,384]{3,2,1,0:T(8,128)(2,1)S(1)}, u32[]{:S(2)}, u32[]{:S(2)}) collective-permute-start(bf16[2,2,64,384]{3,2,1,0:T(8,128)(2,1)S(1)} %pad_maximum_fusion.3), channel_id=1, source_target_pairs={{0,2},{1,3},{2,0},{3,1},{4,6},{5,7},{6,4},{7,5},{8,10},{9,11},{10,... | collective-permute-start | bytes 589832 | tf_op jit(solution)/shard_map/ppermute | solution.py:226
  34.3 1.3 %collective-permute-start.8 = (bf16[256,512]{1,0:T(8,128)(2,1)S(1)}, bf16[256,512]{1,0:T(8,128)(2,1)S(1)}, u32[]{:S(2)}, u32[]{:S(2)}) collective-permute-start(bf16[256,512]{1,0:T(8,128)(2,1)S(1)} %collective-permute-done.6.refs_8_), channel_id=1, source_target_pairs={{0,16},{8,24},{16,0},{24,8},{1,17},{9,25},{17,1},{25,9},{2,18},{10... | collective-permute-start | bytes 786440 | tf_op jit(solution)/shard_map/ppermute | solution.py:229
  35.6 4.1 %collective-permute-done.11 = bf16[2,2,64,384]{3,2,1,0:T(8,128)(2,1)S(1)} collective-permute-done((bf16[2,2,64,384]{3,2,1,0:T(8,128)(2,1)S(1)}, bf16[2,2,64,384]{3,2,1,0:T(8,128)(2,1)S(1)}, u32[]{:S(2)}, u32[]{:S(2)}) %collective-permute-start.11) | collective-permute-done | bytes 196640 | tf_op jit(solution)/shard_map/ppermute | solution.py:226
  39.8 2.5 %collective-permute-done.8.refs_11_ = bf16[256,512]{1,0:T(8,128)(2,1)S(1)} collective-permute-done((bf16[256,512]{1,0:T(8,128)(2,1)S(1)}, bf16[256,512]{1,0:T(8,128)(2,1)S(1)}, u32[]{:S(2)}, u32[]{:S(2)}) %collective-permute-start.8) | collective-permute-done | bytes 262176 | tf_op jit(solution)/shard_map/ppermute | solution.py:229
  42.3 2.0 %shard_map.112 = (bf16[512,256]{1,0:T(8,128)(2,1)S(1)}, bf16[512,256]{1,0:T(8,128)(2,1)S(1)}, bf16[512,128]{1,0:T(8,128)(2,1)S(1)}, bf16[2048,512]{1,0:T(8,128)(2,1)S(1)}) custom-call(bf16[256,2048]{1,0:T(8,128)(2,1)S(1)} %get-tuple-element.62.refs_0_, bf16[256,2048]{1,0:T(8,128)(2,1)S(1)} %collective-permute-done.9.refs_1_, ...), custom_call_target="tpu_custom_call" | custom-call | flops 1342177280 | bytes 9109504 | tf_op jit(solution)/shard_map/pallas_call | solution.py:26
  44.4 1.5 %shard_map.113 = (f32[128,2048]{1,0:T(8,128)S(1)}, f32[128,2048]{1,0:T(8,128)S(1)}, bf16[128,2048]{1,0:T(8,128)(2,1)S(1)}, bf16[128,2048]{1,0:T(8,128)(2,1)S(1)}) custom-call(bf16[512,256]{1,0:T(8,128)(2,1)S(1)} %get-tuple-element.76.dgu_ref, bf16[2048,512]{1,0:T(8,128)(2,1)S(1)} %get-tuple-element.77.full_ref), custom_call_target="tpu_custom_call" | custom-call | flops 536870912 | bytes 5505024 | tf_op jit(solution)/shard_map/pallas_call | solution.py:26
  46.4 1.2 %collective-permute-start.18 = (bf16[4,2,64,384]{3,2,1,0:T(8,128)(2,1)S(1)}, bf16[4,2,64,384]{3,2,1,0:T(8,128)(2,1)S(1)}, u32[]{:S(2)}, u32[]{:S(2)}) collective-permute-start(bf16[4,2,64,384]{3,2,1,0:T(8,128)(2,1)S(1)} %pad_maximum_fusion.1.refs_3_), channel_id=1, source_target_pairs={{0,8},{8,0},{16,24},{24,16},{1,9},{9,1},{17,25},{25,17},{2,10},{10... | collective-permute-start | bytes 1179656 | tf_op jit(solution)/shard_map/ppermute | solution.py:229
  48.1 1.8 %collective-permute-start.15 = (bf16[3,64,128]{2,1,0:T(8,128)(2,1)S(1)}, bf16[3,64,128]{2,1,0:T(8,128)(2,1)S(1)}, u32[]{:S(2)}, u32[]{:S(2)}) collective-permute-start(bf16[3,64,128]{2,1,0:T(8,128)(2,1)S(1)} %get-tuple-element.91), channel_id=1, source_target_pairs={{0,2},{1,3},{2,0},{3,1},{4,6},{5,7},{6,4},{7,5},{8,10},{9,11},{10,... | collective-permute-start | bytes 147464 | tf_op jit(solution)/shard_map/ppermute | solution.py:226
  50.7 1.9 %collective-permute-start.17 = (bf16[3,64,128]{2,1,0:T(8,128)(2,1)S(1)}, bf16[3,64,128]{2,1,0:T(8,128)(2,1)S(1)}, u32[]{:S(2)}, u32[]{:S(2)}) collective-permute-start(bf16[3,64,128]{2,1,0:T(8,128)(2,1)S(1)} %get-tuple-element.93), channel_id=1, source_target_pairs={{0,6},{1,7},{2,4},{3,5},{4,2},{5,3},{6,0},{7,1},{8,14},{9,15},{10,... | collective-permute-start | bytes 147464 | tf_op jit(solution)/shard_map/ppermute | solution.py:226
  52.6 1.2 %collective-permute-start.23 = (bf16[128,2048]{1,0:T(8,128)(2,1)S(1)}, bf16[128,2048]{1,0:T(8,128)(2,1)S(1)}, u32[]{:S(2)}, u32[]{:S(2)}) collective-permute-start(bf16[128,2048]{1,0:T(8,128)(2,1)S(1)} %add_convert_fusion.1), channel_id=1, source_target_pairs={{0,8},{8,0},{16,24},{24,16},{1,9},{9,1},{17,25},{25,17},{2,10},{10... | collective-permute-start | bytes 1572872 | tf_op jit(solution)/shard_map/ppermute | solution.py:229
  53.7 4.7 %collective-permute-done.18.refs_4_ = bf16[4,2,64,384]{3,2,1,0:T(8,128)(2,1)S(1)} collective-permute-done((bf16[4,2,64,384]{3,2,1,0:T(8,128)(2,1)S(1)}, bf16[4,2,64,384]{3,2,1,0:T(8,128)(2,1)S(1)}, u32[]{:S(2)}, u32[]{:S(2)}) %collective-permute-start.18) | collective-permute-done | bytes 393248 | tf_op jit(solution)/shard_map/ppermute | solution.py:229
  58.4 1.4 %collective-permute-start.19 = (bf16[3,64,128]{2,1,0:T(8,128)(2,1)S(1)}, bf16[3,64,128]{2,1,0:T(8,128)(2,1)S(1)}, u32[]{:S(2)}, u32[]{:S(2)}) collective-permute-start(bf16[3,64,128]{2,1,0:T(8,128)(2,1)S(1)} %add_convert_fusion.3), channel_id=1, source_target_pairs={{0,16},{8,24},{16,0},{24,8},{1,17},{9,25},{17,1},{25,9},{2,18},{10... | collective-permute-start | bytes 147464 | tf_op jit(solution)/shard_map/ppermute | solution.py:229
  59.8 2.8 %collective-permute-done.19 = bf16[3,64,128]{2,1,0:T(8,128)(2,1)S(1)} collective-permute-done((bf16[3,64,128]{2,1,0:T(8,128)(2,1)S(1)}, bf16[3,64,128]{2,1,0:T(8,128)(2,1)S(1)}, u32[]{:S(2)}, u32[]{:S(2)}) %collective-permute-start.19) | collective-permute-done | bytes 49184 | tf_op jit(solution)/shard_map/ppermute | solution.py:229
  62.6 1.5 %collective-permute-start.22 = (bf16[3,64,128]{2,1,0:T(8,128)(2,1)S(1)}, bf16[3,64,128]{2,1,0:T(8,128)(2,1)S(1)}, u32[]{:S(2)}, u32[]{:S(2)}) collective-permute-start(bf16[3,64,128]{2,1,0:T(8,128)(2,1)S(1)} %add_convert_fusion.2), channel_id=1, source_target_pairs={{0,6},{1,7},{2,4},{3,5},{4,2},{5,3},{6,0},{7,1},{8,14},{9,15},{10,... | collective-permute-start | bytes 147464 | tf_op jit(solution)/shard_map/ppermute | solution.py:226
  65.0 2.0 %collective-permute-start.20 = (bf16[3,64,128]{2,1,0:T(8,128)(2,1)S(1)}, bf16[3,64,128]{2,1,0:T(8,128)(2,1)S(1)}, u32[]{:S(2)}, u32[]{:S(2)}) collective-permute-start(bf16[3,64,128]{2,1,0:T(8,128)(2,1)S(1)} %add_convert_fusion.2), channel_id=1, source_target_pairs={{0,2},{1,3},{2,0},{3,1},{4,6},{5,7},{6,4},{7,5},{8,10},{9,11},{10,... | collective-permute-start | bytes 147464 | tf_op jit(solution)/shard_map/ppermute | solution.py:226
  67.1 1.5 %collective-permute-done.22 = bf16[3,64,128]{2,1,0:T(8,128)(2,1)S(1)} collective-permute-done((bf16[3,64,128]{2,1,0:T(8,128)(2,1)S(1)}, bf16[3,64,128]{2,1,0:T(8,128)(2,1)S(1)}, u32[]{:S(2)}, u32[]{:S(2)}) %collective-permute-start.22) | collective-permute-done | bytes 49184 | tf_op jit(solution)/shard_map/ppermute | solution.py:226
  68.6 1.1 %collective-permute-done.21 = bf16[3,64,128]{2,1,0:T(8,128)(2,1)S(1)} collective-permute-done((bf16[3,64,128]{2,1,0:T(8,128)(2,1)S(1)}, bf16[3,64,128]{2,1,0:T(8,128)(2,1)S(1)}, u32[]{:S(2)}, u32[]{:S(2)}) %collective-permute-start.21) | collective-permute-done | bytes 49184 | tf_op jit(solution)/shard_map/ppermute | solution.py:226
  69.7 1.8 %collective-permute-start.24 = (bf16[4,3,64,128]{3,2,1,0:T(8,128)(2,1)S(1)}, bf16[4,3,64,128]{3,2,1,0:T(8,128)(2,1)S(1)}, u32[]{:S(2)}, u32[]{:S(2)}) collective-permute-start(bf16[4,3,64,128]{3,2,1,0:T(8,128)(2,1)S(1)} %get-tuple-element.109.refs_0_), channel_id=1, source_target_pairs={{0,8},{8,0},{16,24},{24,16},{1,9},{9,1},{17,25},{25,17},{2,10},{10... | collective-permute-start | bytes 589832 | tf_op jit(solution)/shard_map/ppermute | solution.py:229
  71.7 3.8 %collective-permute-done.24.refs_1_ = bf16[4,3,64,128]{3,2,1,0:T(8,128)(2,1)S(1)} collective-permute-done((bf16[4,3,64,128]{3,2,1,0:T(8,128)(2,1)S(1)}, bf16[4,3,64,128]{3,2,1,0:T(8,128)(2,1)S(1)}, u32[]{:S(2)}, u32[]{:S(2)}) %collective-permute-start.24) | collective-permute-done | bytes 196640 | tf_op jit(solution)/shard_map/ppermute | solution.py:229
  75.6 1.0 %add_convert_fusion = bf16[128,2048]{1,0:T(8,128)(2,1)} fusion(bf16[128,2048]{1,0:T(8,128)(2,1)S(1)} %collective-permute-done.23, f32[128,2048]{1,0:T(8,128)S(1)} %get-tuple-element.78, bf16[128,2048]{1,0:T(8,128)(2,1)S(1)} %collective-permute-done.12), kind=kLoop, calls=%fused_computation | loop fusion | flops 1310720 | bytes 2621440 | tf_op jit(solution)/shard_map/convert_element_type | solution.py:354
  77.3 3.2 %shard_map.115 = (f32[3,32,512]{2,1,0:T(8,128)}, f32[3,32,512]{2,1,0:T(8,128)}, f32[3,256,512]{2,1,0:T(8,128)}) custom-call(bf16[4,3,64,128]{3,2,1,0:T(8,128)(2,1)S(1)} %get-tuple-element.109.refs_0_, bf16[4,3,64,128]{3,2,1,0:T(8,128)(2,1)S(1)} %collective-permute-done.24.refs_1_, bf16[2,4,3,64,128]{4,3,2,1,0:T(8,128)(2,1)S(1)} %collective-permute-done.25.refs_2_, ...), custom_call_target="tpu_custom_call" | custom-call | flops 402653184 | bytes 4980736 | tf_op jit(solution)/shard_map/pallas_call | solution.py:26
  (44 shorter events, 5.4 us)
Async XLA Ops:
  2.4 12.0 %collective-permute-start.1 = (bf16[256,512]{1,0:T(8,128)(2,1)S(1)}, bf16[256,512]{1,0:T(8,128)(2,1)S(1)}, u32[]{:S(2)}, u32[]{:S(2)}) collective-permute-start(bf16[256,512]{1,0:T(8,128)(2,1)S(1)} %get-tuple-element.57), channel_id=1, source_target_pairs={{0,2},{1,3},{2,0},{3,1},{4,6},{5,7},{6,4},{7,5},{8,10},{9,11},{10,... | collective-permute-start | bytes 786440 | tf_op jit(solution)/shard_map/ppermute | solution.py:237
  5.5 26.8 %collective-permute-start = (bf16[256,2048]{1,0:T(8,128)(2,1)S(1)}, bf16[256,2048]{1,0:T(8,128)(2,1)S(1)}, u32[]{:S(2)}, u32[]{:S(2)}) collective-permute-start(bf16[256,2048]{1,0:T(8,128)(2,1)S(1)} %get-tuple-element.62.refs_0_), channel_id=1, source_target_pairs={{0,8},{8,0},{16,24},{24,16},{1,9},{9,1},{17,25},{25,17},{2,10},{10... | collective-permute-start | bytes 3145736 | tf_op jit(solution)/shard_map/ppermute | solution.py:229
  7.0 16.2 %collective-permute-start.3 = (bf16[320,512]{1,0:T(8,128)(2,1)S(1)}, bf16[320,512]{1,0:T(8,128)(2,1)S(1)}, u32[]{:S(2)}, u32[]{:S(2)}) collective-permute-start(bf16[320,512]{1,0:T(8,128)(2,1)S(1)} %get-tuple-element.58), channel_id=1, source_target_pairs={{0,1},{1,0},{2,3},{3,2},{4,5},{5,4},{6,7},{7,6},{8,9},{9,8},{10,11... | collective-permute-start | bytes 983048 | tf_op jit(solution)/shard_map/ppermute | solution.py:226
  7.0 15.3 %collective-permute-start.4 = (bf16[256,512]{1,0:T(8,128)(2,1)S(1)}, bf16[256,512]{1,0:T(8,128)(2,1)S(1)}, u32[]{:S(2)}, u32[]{:S(2)}) collective-permute-start(bf16[256,512]{1,0:T(8,128)(2,1)S(1)} %get-tuple-element.57), channel_id=1, source_target_pairs={{0,4},{1,5},{2,6},{3,7},{4,0},{5,1},{6,2},{7,3},{8,12},{9,13},{10,... | collective-permute-start | bytes 786440 | tf_op jit(solution)/shard_map/ppermute | solution.py:237
  14.4 10.2 %collective-permute-start.2 = (bf16[256,512]{1,0:T(8,128)(2,1)S(1)}, bf16[256,512]{1,0:T(8,128)(2,1)S(1)}, u32[]{:S(2)}, u32[]{:S(2)}) collective-permute-start(bf16[256,512]{1,0:T(8,128)(2,1)S(1)} %collective-permute-done.1.refs_6_), channel_id=1, source_target_pairs={{0,16},{8,24},{16,0},{24,8},{1,17},{9,25},{17,1},{25,9},{2,18},{10... | collective-permute-start | bytes 786440 | tf_op jit(solution)/shard_map/ppermute | solution.py:229
  22.3 10.0 %collective-permute-start.6 = (bf16[256,512]{1,0:T(8,128)(2,1)S(1)}, bf16[256,512]{1,0:T(8,128)(2,1)S(1)}, u32[]{:S(2)}, u32[]{:S(2)}) collective-permute-start(bf16[256,512]{1,0:T(8,128)(2,1)S(1)} %collective-permute-done.4.refs_7_), channel_id=1, source_target_pairs={{0,2},{1,3},{2,0},{3,1},{4,6},{5,7},{6,4},{7,5},{8,10},{9,11},{10,... | collective-permute-start | bytes 786440 | tf_op jit(solution)/shard_map/ppermute | solution.py:226
  22.3 10.0 %collective-permute-start.5 = (bf16[256,512]{1,0:T(8,128)(2,1)S(1)}, bf16[256,512]{1,0:T(8,128)(2,1)S(1)}, u32[]{:S(2)}, u32[]{:S(2)}) collective-permute-start(bf16[256,512]{1,0:T(8,128)(2,1)S(1)} %collective-permute-done.4.refs_7_), channel_id=1, source_target_pairs={{0,16},{8,24},{16,0},{24,8},{1,17},{9,25},{17,1},{25,9},{2,18},{10... | collective-permute-start | bytes 786440 | tf_op jit(solution)/shard_map/ppermute | solution.py:229
  24.6 5.7 %collective-permute-start.7 = (bf16[1,2,64,384]{3,2,1,0:T(8,128)(2,1)S(1)}, bf16[1,2,64,384]{3,2,1,0:T(8,128)(2,1)S(1)}, u32[]{:S(2)}, u32[]{:S(2)}) collective-permute-start(bf16[1,2,64,384]{3,2,1,0:T(8,128)(2,1)S(1)} %maximum_bitcast_fusion), channel_id=1, source_target_pairs={{0,4},{1,5},{2,6},{3,7},{4,0},{5,1},{6,2},{7,3},{8,12},{9,13},{10,... | collective-permute-start | bytes 294920 | tf_op jit(solution)/shard_map/ppermute | solution.py:226
  32.4 9.9 %collective-permute-start.9 = (bf16[256,2048]{1,0:T(8,128)(2,1)S(1)}, bf16[256,2048]{1,0:T(8,128)(2,1)S(1)}, u32[]{:S(2)}, u32[]{:S(2)}) collective-permute-start(bf16[256,2048]{1,0:T(8,128)(2,1)S(1)} %get-tuple-element.62.refs_0_), channel_id=1, source_target_pairs={{0,1},{1,0},{2,3},{3,2},{4,5},{5,4},{6,7},{7,6},{8,9},{9,8},{10,11... | collective-permute-start | bytes 3145736 | tf_op jit(solution)/shard_map/ppermute | solution.py:226
  32.4 9.9 %collective-permute-start.10 = (bf16[256,2048]{1,0:T(8,128)(2,1)S(1)}, bf16[256,2048]{1,0:T(8,128)(2,1)S(1)}, u32[]{:S(2)}, u32[]{:S(2)}) collective-permute-start(bf16[256,2048]{1,0:T(8,128)(2,1)S(1)} %collective-permute-done.refs_2_), channel_id=1, source_target_pairs={{0,1},{1,0},{2,3},{3,2},{4,5},{5,4},{6,7},{7,6},{8,9},{9,8},{10,11... | collective-permute-start | bytes 3145736 | tf_op jit(solution)/shard_map/ppermute | solution.py:226
  32.9 6.9 %collective-permute-start.11 = (bf16[2,2,64,384]{3,2,1,0:T(8,128)(2,1)S(1)}, bf16[2,2,64,384]{3,2,1,0:T(8,128)(2,1)S(1)}, u32[]{:S(2)}, u32[]{:S(2)}) collective-permute-start(bf16[2,2,64,384]{3,2,1,0:T(8,128)(2,1)S(1)} %pad_maximum_fusion.3), channel_id=1, source_target_pairs={{0,2},{1,3},{2,0},{3,1},{4,6},{5,7},{6,4},{7,5},{8,10},{9,11},{10,... | collective-permute-start | bytes 589832 | tf_op jit(solution)/shard_map/ppermute | solution.py:226
  34.3 8.0 %collective-permute-start.8 = (bf16[256,512]{1,0:T(8,128)(2,1)S(1)}, bf16[256,512]{1,0:T(8,128)(2,1)S(1)}, u32[]{:S(2)}, u32[]{:S(2)}) collective-permute-start(bf16[256,512]{1,0:T(8,128)(2,1)S(1)} %collective-permute-done.6.refs_8_), channel_id=1, source_target_pairs={{0,16},{8,24},{16,0},{24,8},{1,17},{9,25},{17,1},{25,9},{2,18},{10... | collective-permute-start | bytes 786440 | tf_op jit(solution)/shard_map/ppermute | solution.py:229
  44.3 1.6 %collective-permute-start.13 = (bf16[512,256]{1,0:T(8,128)(2,1)S(1)}, bf16[512,256]{1,0:T(8,128)(2,1)S(1)}, u32[]{:S(2)}, u32[]{:S(2)}) collective-permute-start(bf16[512,256]{1,0:T(8,128)(2,1)S(1)} %get-tuple-element.80.mine_ref), channel_id=1, source_target_pairs={{0,1},{1,0},{2,3},{3,2},{4,5},{5,4},{6,7},{7,6},{8,9},{9,8},{10,11... | collective-permute-start | bytes 786440 | tf_op jit(solution)/shard_map/ppermute | solution.py:226
  45.9 2.1 %collective-permute-start.14 = (bf16[128,2048]{1,0:T(8,128)(2,1)S(1)}, bf16[128,2048]{1,0:T(8,128)(2,1)S(1)}, u32[]{:S(2)}, u32[]{:S(2)}) collective-permute-start(bf16[128,2048]{1,0:T(8,128)(2,1)S(1)} %get-tuple-element.89), channel_id=1, source_target_pairs={{0,1},{1,0},{2,3},{3,2},{4,5},{5,4},{6,7},{7,6},{8,9},{9,8},{10,11... | collective-permute-start | bytes 1572872 | tf_op jit(solution)/shard_map/ppermute | solution.py:226
  46.4 12.0 %collective-permute-start.18 = (bf16[4,2,64,384]{3,2,1,0:T(8,128)(2,1)S(1)}, bf16[4,2,64,384]{3,2,1,0:T(8,128)(2,1)S(1)}, u32[]{:S(2)}, u32[]{:S(2)}) collective-permute-start(bf16[4,2,64,384]{3,2,1,0:T(8,128)(2,1)S(1)} %pad_maximum_fusion.1.refs_3_), channel_id=1, source_target_pairs={{0,8},{8,0},{16,24},{24,16},{1,9},{9,1},{17,25},{25,17},{2,10},{10... | collective-permute-start | bytes 1179656 | tf_op jit(solution)/shard_map/ppermute | solution.py:229
  48.1 10.3 %collective-permute-start.15 = (bf16[3,64,128]{2,1,0:T(8,128)(2,1)S(1)}, bf16[3,64,128]{2,1,0:T(8,128)(2,1)S(1)}, u32[]{:S(2)}, u32[]{:S(2)}) collective-permute-start(bf16[3,64,128]{2,1,0:T(8,128)(2,1)S(1)} %get-tuple-element.91), channel_id=1, source_target_pairs={{0,2},{1,3},{2,0},{3,1},{4,6},{5,7},{6,4},{7,5},{8,10},{9,11},{10,... | collective-permute-start | bytes 147464 | tf_op jit(solution)/shard_map/ppermute | solution.py:226
  49.9 8.5 %collective-permute-start.16 = (bf16[3,64,128]{2,1,0:T(8,128)(2,1)S(1)}, bf16[3,64,128]{2,1,0:T(8,128)(2,1)S(1)}, u32[]{:S(2)}, u32[]{:S(2)}) collective-permute-start(bf16[3,64,128]{2,1,0:T(8,128)(2,1)S(1)} %get-tuple-element.92), channel_id=1, source_target_pairs={{0,4},{1,5},{2,6},{3,7},{4,0},{5,1},{6,2},{7,3},{8,12},{9,13},{10,... | collective-permute-start | bytes 147464 | tf_op jit(solution)/shard_map/ppermute | solution.py:226
  50.7 7.7 %collective-permute-start.17 = (bf16[3,64,128]{2,1,0:T(8,128)(2,1)S(1)}, bf16[3,64,128]{2,1,0:T(8,128)(2,1)S(1)}, u32[]{:S(2)}, u32[]{:S(2)}) collective-permute-start(bf16[3,64,128]{2,1,0:T(8,128)(2,1)S(1)} %get-tuple-element.93), channel_id=1, source_target_pairs={{0,6},{1,7},{2,4},{3,5},{4,2},{5,3},{6,0},{7,1},{8,14},{9,15},{10,... | collective-permute-start | bytes 147464 | tf_op jit(solution)/shard_map/ppermute | solution.py:226
  52.6 17.1 %collective-permute-start.23 = (bf16[128,2048]{1,0:T(8,128)(2,1)S(1)}, bf16[128,2048]{1,0:T(8,128)(2,1)S(1)}, u32[]{:S(2)}, u32[]{:S(2)}) collective-permute-start(bf16[128,2048]{1,0:T(8,128)(2,1)S(1)} %add_convert_fusion.1), channel_id=1, source_target_pairs={{0,8},{8,0},{16,24},{24,16},{1,9},{9,1},{17,25},{25,17},{2,10},{10... | collective-permute-start | bytes 1572872 | tf_op jit(solution)/shard_map/ppermute | solution.py:229
  58.4 4.2 %collective-permute-start.19 = (bf16[3,64,128]{2,1,0:T(8,128)(2,1)S(1)}, bf16[3,64,128]{2,1,0:T(8,128)(2,1)S(1)}, u32[]{:S(2)}, u32[]{:S(2)}) collective-permute-start(bf16[3,64,128]{2,1,0:T(8,128)(2,1)S(1)} %add_convert_fusion.3), channel_id=1, source_target_pairs={{0,16},{8,24},{16,0},{24,8},{1,17},{9,25},{17,1},{25,9},{2,18},{10... | collective-permute-start | bytes 147464 | tf_op jit(solution)/shard_map/ppermute | solution.py:229
  62.6 6.0 %collective-permute-start.22 = (bf16[3,64,128]{2,1,0:T(8,128)(2,1)S(1)}, bf16[3,64,128]{2,1,0:T(8,128)(2,1)S(1)}, u32[]{:S(2)}, u32[]{:S(2)}) collective-permute-start(bf16[3,64,128]{2,1,0:T(8,128)(2,1)S(1)} %add_convert_fusion.2), channel_id=1, source_target_pairs={{0,6},{1,7},{2,4},{3,5},{4,2},{5,3},{6,0},{7,1},{8,14},{9,15},{10,... | collective-permute-start | bytes 147464 | tf_op jit(solution)/shard_map/ppermute | solution.py:226
  64.1 5.5 %collective-permute-start.21 = (bf16[3,64,128]{2,1,0:T(8,128)(2,1)S(1)}, bf16[3,64,128]{2,1,0:T(8,128)(2,1)S(1)}, u32[]{:S(2)}, u32[]{:S(2)}) collective-permute-start(bf16[3,64,128]{2,1,0:T(8,128)(2,1)S(1)} %add_convert_fusion.2), channel_id=1, source_target_pairs={{0,4},{1,5},{2,6},{3,7},{4,0},{5,1},{6,2},{7,3},{8,12},{9,13},{10,... | collective-permute-start | bytes 147464 | tf_op jit(solution)/shard_map/ppermute | solution.py:226
  65.0 4.6 %collective-permute-start.20 = (bf16[3,64,128]{2,1,0:T(8,128)(2,1)S(1)}, bf16[3,64,128]{2,1,0:T(8,128)(2,1)S(1)}, u32[]{:S(2)}, u32[]{:S(2)}) collective-permute-start(bf16[3,64,128]{2,1,0:T(8,128)(2,1)S(1)} %add_convert_fusion.2), channel_id=1, source_target_pairs={{0,2},{1,3},{2,0},{3,1},{4,6},{5,7},{6,4},{7,5},{8,10},{9,11},{10,... | collective-permute-start | bytes 147464 | tf_op jit(solution)/shard_map/ppermute | solution.py:226
  67.1 8.5 %collective-permute-start.12 = (bf16[128,2048]{1,0:T(8,128)(2,1)S(1)}, bf16[128,2048]{1,0:T(8,128)(2,1)S(1)}, u32[]{:S(2)}, u32[]{:S(2)}) collective-permute-start(bf16[128,2048]{1,0:T(8,128)(2,1)S(1)} %get-tuple-element.79), channel_id=1, source_target_pairs={{0,1},{1,0},{2,3},{3,2},{4,5},{5,4},{6,7},{7,6},{8,9},{9,8},{10,11... | collective-permute-start | bytes 1572872 | tf_op jit(solution)/shard_map/ppermute | solution.py:226
  69.7 5.7 %collective-permute-start.24 = (bf16[4,3,64,128]{3,2,1,0:T(8,128)(2,1)S(1)}, bf16[4,3,64,128]{3,2,1,0:T(8,128)(2,1)S(1)}, u32[]{:S(2)}, u32[]{:S(2)}) collective-permute-start(bf16[4,3,64,128]{3,2,1,0:T(8,128)(2,1)S(1)} %get-tuple-element.109.refs_0_), channel_id=1, source_target_pairs={{0,8},{8,0},{16,24},{24,16},{1,9},{9,1},{17,25},{25,17},{2,10},{10... | collective-permute-start | bytes 589832 | tf_op jit(solution)/shard_map/ppermute | solution.py:229
  71.6 5.7 %copy-start = (f32[256,256]{1,0:T(8,128)S(1)}, f32[256,256]{1,0:T(8,128)}, u32[]{:S(2)}) copy-start(f32[256,256]{1,0:T(8,128)} %refs_6_.3) | copy-start | bytes 786436
  71.6 5.7 %copy-start.1 = (f32[3,32,512]{2,1,0:T(8,128)S(1)}, f32[3,32,512]{2,1,0:T(8,128)}, u32[]{:S(2)}) copy-start(f32[3,32,512]{2,1,0:T(8,128)} %refs_7_.3) | copy-start | bytes 589828
  71.6 5.7 %copy-start.2 = (f32[3,32,512]{2,1,0:T(8,128)S(1)}, f32[3,32,512]{2,1,0:T(8,128)}, u32[]{:S(2)}) copy-start(f32[3,32,512]{2,1,0:T(8,128)} %refs_8_.1) | copy-start | bytes 589828
  71.6 5.0 %collective-permute-start.26 = (bf16[2,4,2,64,384]{4,3,2,1,0:T(8,128)(2,1)S(1)}, bf16[2,4,2,64,384]{4,3,2,1,0:T(8,128)(2,1)S(1)}, u32[]{:S(2)}, u32[]{:S(2)}) collective-permute-start(bf16[2,4,2,64,384]{4,3,2,1,0:T(8,128)(2,1)S(1)} %pad_maximum_fusion), channel_id=1, source_target_pairs={{0,1},{1,0},{2,3},{3,2},{4,5},{5,4},{6,7},{7,6},{8,9},{9,8},{10,11... | collective-permute-start | bytes 2359304 | tf_op jit(solution)/shard_map/ppermute | solution.py:226
  75.5 1.8 %collective-permute-start.25 = (bf16[2,4,3,64,128]{4,3,2,1,0:T(8,128)(2,1)S(1)}, bf16[2,4,3,64,128]{4,3,2,1,0:T(8,128)(2,1)S(1)}, u32[]{:S(2)}, u32[]{:S(2)}) collective-permute-start(bf16[2,4,3,64,128]{4,3,2,1,0:T(8,128)(2,1)S(1)} %pad_maximum_fusion.2), channel_id=1, source_target_pairs={{0,1},{1,0},{2,3},{3,2},{4,5},{5,4},{6,7},{7,6},{8,9},{9,8},{10,11... | collective-permute-start | bytes 1179656 | tf_op jit(solution)/shard_map/ppermute | solution.py:226

commit v4 on v3

--- a/solution.py
+++ b/solution.py
@@ -18,7 +18,7 @@
     return lax.dot_general(left, right, dims, preferred_element_type=F32)
 
 
-def call(body, outs, scratch, flops, *operands, pinned=False, mib=40):
+def call(body, outs, scratch, flops, *operands, pinned=False, mib=40, results=pltpu.VMEM):
     if pinned:
         operands = [pltpu.with_memory_space_constraint(o, pltpu.HBM) for o in operands]
     moved = sum(o.size * o.dtype.itemsize for o in operands)
@@ -27,7 +27,7 @@
         body,
         out_shape=[(pltpu.VMEM if pinned else jax.ShapeDtypeStruct)(s, d) for s, d in outs],
         in_specs=[pl.BlockSpec(memory_space=pltpu.HBM if pinned else pltpu.VMEM)] * len(operands),
-        out_specs=[pl.BlockSpec(memory_space=pltpu.VMEM)] * len(outs),
+        out_specs=[pl.BlockSpec(memory_space=results)] * len(outs),
         scratch_shapes=scratch,
         compiler_params=pltpu.CompilerParams(vmem_limit_bytes=mib * 1024 * 1024),
         cost_estimate=pl.CostEstimate(
@@ -164,8 +164,8 @@
 
 def last_kernel(chips, limit, *refs):
     lows, core_low, moms, core_moms = refs[:2], refs[2], refs[3:5], refs[5]
-    basis_ref, first_ref, second_ref, new_first_ref, new_second_ref, upd_ref = refs[6:12]
-    full, stepped = refs[12:]
+    basis_ref, first_ref, second_ref, *out_hbms = refs[6:12]
+    full, stepped, new_first_ref, new_second_ref, products, sems = refs[12:]
     side, _, chip, core, member = places()
     height, unit = lows[0].shape[2:]
     squares = None
@@ -175,41 +175,50 @@
             columns = pl.ds(pl.multiple_of(column, unit), unit)
             for k in range(chips):
                 low = (core_low[dx, k] if dc else lows[dx][k]).astype(F32)
-                square = jnp.sum(low * low, axis=(0, 1), keepdims=True)
+                square = jnp.sum((low * low).reshape(-1, 8, unit), axis=0)
                 squares = square if squares is None else squares + square
                 rows = pl.ds(pl.multiple_of((chip ^ k) * height, height), height)
                 full[:, rows, columns] = low
-    total = jnp.sum(squares, axis=2, keepdims=True)
+    total = jnp.sum(squares, axis=(0, 1), keepdims=True)
     factor = jnp.minimum(1.0, limit / jnp.sqrt(total + 1e-06))
     own_rows = first_ref.shape[1]
-    mine = factor * full[:, pl.ds(pl.multiple_of(member * own_rows, own_rows), own_rows), :]
-    new_first_ref[...] = 0.5 * first_ref[...] + 0.5 * mine
-    new_second_ref[...] = 0.9 * second_ref[...] + 0.1 * mine * mine
     parts = first_ref.shape[0]
-    for dc in range(2):
-        for dx in range(2):
-            column = ((side ^ dx) * 2 + (core ^ dc)) * unit
-            columns = pl.ds(pl.multiple_of(column, unit), unit)
-            for n, dr in ((n, dr) for n in range(chips) for dr in range(2)):
-                row = ((chip ^ mirrored(n, chips)) * 2 + (core ^ dc ^ dr)) * own_rows
-                rows = pl.ds(pl.multiple_of(row, own_rows), own_rows)
-                for i in range(parts):
-                    mom = []
-                    for f in range(2):
-                        where = pl.ds(f * own_rows, own_rows)
-                        lanes = slice(i * unit, (i + 1) * unit)
-                        ref = core_moms.at[dx] if dc else moms[dx]
-                        mom.append(ref[n, dr, where, lanes].astype(F32))
-                    grad = factor[0] * full[i, rows, columns]
-                    first = 0.5 * mom[0] + 0.5 * grad
-                    second = 0.9 * mom[1] + 0.1 * grad * grad
-                    stepped[i, rows, columns] = first / (jnp.sqrt(second) + 1e-08)
+    half, tenth = 0.5 * factor, 0.1 * factor * factor
     basis = basis_ref[...]
     high = basis.astype(BF)
     rest = (basis - high.astype(F32)).astype(BF)
-    for i in range(upd_ref.shape[0]):
-        step = stepped[i].astype(BF)
-        upd_ref[i] = dot(high, step) + dot(rest, step)
+    mine = pl.ds(pl.multiple_of(member * own_rows, own_rows), own_rows)
+    copies = []
+
+    def start(source, target):
+        copies.append(pltpu.make_async_copy(source, target, sems.at[len(copies)]))
+        copies[-1].start()
+
+    low = full[:, mine, :]
+    new_first_ref[...] = 0.5 * first_ref[...] + half * low
+    new_second_ref[...] = 0.9 * second_ref[...] + tenth * low * low
+    start(new_first_ref, out_hbms[0])
+    start(new_second_ref, out_hbms[1])
+    for i in range(parts):
+        for dc in range(2):
+            for dx in range(2):
+                column = ((side ^ dx) * 2 + (core ^ dc)) * unit
+                columns = pl.ds(pl.multiple_of(column, unit), unit)
+                lanes = slice(i * unit, (i + 1) * unit)
+                ref = core_moms.at[dx] if dc else moms[dx]
+                for n, dr in ((n, dr) for n in range(chips) for dr in range(2)):
+                    row = ((chip ^ mirrored(n, chips)) * 2 + (core ^ dc ^ dr)) * own_rows
+                    rows = pl.ds(pl.multiple_of(row, own_rows), own_rows)
+                    low = full[i, rows, columns]
+                    first = 0.5 * ref[n, dr, :own_rows, lanes].astype(F32) + half * low
+                    second = 0.9 * ref[n, dr, own_rows:, lanes].astype(F32) + tenth * low * low
+                    root = second * lax.rsqrt(second) + 1e-08
+                    stepped[rows, columns] = first * pl.reciprocal(root, approx=True)
+        step = stepped[...].astype(BF)
+        products[i] = dot(high, step) + dot(rest, step)
+        start(products.at[i], out_hbms[2].at[i])
+    for copy in copies:
+        copy.wait()
 
 
 def local(sizes, tokens, cotangent, w_gate, w_up, w_down, basis, first_moment, second_moment):
@@ -355,8 +364,15 @@
     low_core = by_member(jnp.stack([low_mine, low_side]), 1)
     new_first, new_second, updates = call(
         functools.partial(last_kernel, chips, limit),
-        [(first_moment.shape, F32), (second_moment.shape, F32), ((3, depth, hidden_size), F32)],
-        [pltpu.VMEM((3, rank, hidden_size), F32)] * 2,
+        [(first_moment.shape, F32), (second_moment.shape, F32), ((parts, depth, hidden_size), F32)],
+        [
+            pltpu.VMEM((parts, rank, hidden_size), F32),
+            pltpu.VMEM((rank, hidden_size), F32),
+            pltpu.VMEM(first_moment.shape, F32),
+            pltpu.VMEM(second_moment.shape, F32),
+            pltpu.VMEM((parts, depth, hidden_size), F32),
+            pltpu.SemaphoreType.DMA((parts + 2,)),
+        ],
         4 * 3 * depth * rank * hidden_size,
         low_mine,
         low_side,
@@ -367,6 +383,7 @@
         basis,
         first_moment,
         second_moment,
+        results=pltpu.HBM,
     )
     return (input_grad, new_first, new_second, updates)
 

time: 80.6 us -> 80.2 us (level)
  no operation moved by 1% of the time
where the time goes in v4:
time: 80.2 us; the launch traced here: 80 us
  waiting for transfers between devices  37.7 us (47%)
  starting transfers between devices  31.7 us (40%)
  Pallas kernels  8.35 us (10%)
  other arithmetic  1.39 us (2%)
  between operations  0.81 us (1%)
    ppermute x8, waiting for transfers between devices, by_group(): return lax.ppermute(value, 'group', [(i, i ^ bits) for i in range(groups)])  15 us
    ppermute x17, waiting for transfers between devices, by_member(): lax.ppermute(value, 'member', [(i, i ^ bits) for i in range(members)])  13.5 us
    ppermute x17, starting transfers between devices, by_member(): lax.ppermute(value, 'member', [(i, i ^ bits) for i in range(members)])  13.3 us
    ppermute x8, starting transfers between devices, by_group(): return lax.ppermute(value, 'group', [(i, i ^ bits) for i in range(groups)])  12.7 us
    ppermute x2, waiting for transfers between devices, by_chip(): return lax.ppermute(value, ('group', 'member'), pairs)  9.25 us
    pallas_call x5, Pallas kernels, call(): pl.pallas_call(body, out_shape=[(pltpu.VMEM if pinned else jax.ShapeDtype...  8.35 us
    ppermute x2, starting transfers between devices, by_chip(): return lax.ppermute(value, ('group', 'member'), pairs)  5.68 us
  transfers between devices with their start and end apart: 27, of which 13 were waited for; matrix products, arithmetic and copies ran while one was open for 2% of the time, Pallas kernels for 2%

profile of v4, /device:TPU:0, one launch (start us, length us, event | category | flops | bytes accessed | tf_op | source)
XLA Modules:
  0.0 80.0 jit_solution(4980466675197645724)
XLA Ops:
  0.6 1.8 %shard_map.111 = (bf16[256,512]{1,0:T(8,128)(2,1)S(1)}, bf16[256,512]{1,0:T(8,128)(2,1)S(1)}, bf16[320,512]{1,0:T(8,128)(2,1)S(1)}, bf16[64,384]{1,0:T(8,128)(2,1)S(1)}, bf16[256,2048]{1,0:T(8,128)(2,1)S(1)}) custom-call(bf16[256,512]{1,0:T(8,128)(2,1)} %refs_0_.1, bf16[256,512]{1,0:T(8,128)(2,1)} %refs_1_.1, bf16[256,512]{1,0:T(8,128)(2,1)} %refs_2_.1, ...), custom_call_target="tpu_custom_call" | custom-call | bytes 4440064 | tf_op jit(solution)/shard_map/pallas_call | solution.py:26
  2.4 3.1 %collective-permute-start.1 = (bf16[256,512]{1,0:T(8,128)(2,1)S(1)}, bf16[256,512]{1,0:T(8,128)(2,1)S(1)}, u32[]{:S(2)}, u32[]{:S(2)}) collective-permute-start(bf16[256,512]{1,0:T(8,128)(2,1)S(1)} %get-tuple-element.57), channel_id=1, source_target_pairs={{0,2},{1,3},{2,0},{3,1},{4,6},{5,7},{6,4},{7,5},{8,10},{9,11},{10,... | collective-permute-start | bytes 786440 | tf_op jit(solution)/shard_map/ppermute | solution.py:246
  5.5 1.5 %collective-permute-start = (bf16[256,2048]{1,0:T(8,128)(2,1)S(1)}, bf16[256,2048]{1,0:T(8,128)(2,1)S(1)}, u32[]{:S(2)}, u32[]{:S(2)}) collective-permute-start(bf16[256,2048]{1,0:T(8,128)(2,1)S(1)} %get-tuple-element.62.refs_0_), channel_id=1, source_target_pairs={{0,8},{8,0},{16,24},{24,16},{1,9},{9,1},{17,25},{25,17},{2,10},{10... | collective-permute-start | bytes 3145736 | tf_op jit(solution)/shard_map/ppermute | solution.py:238
  7.0 2.6 %collective-permute-start.4 = (bf16[256,512]{1,0:T(8,128)(2,1)S(1)}, bf16[256,512]{1,0:T(8,128)(2,1)S(1)}, u32[]{:S(2)}, u32[]{:S(2)}) collective-permute-start(bf16[256,512]{1,0:T(8,128)(2,1)S(1)} %get-tuple-element.57), channel_id=1, source_target_pairs={{0,4},{1,5},{2,6},{3,7},{4,0},{5,1},{6,2},{7,3},{8,12},{9,13},{10,... | collective-permute-start | bytes 786440 | tf_op jit(solution)/shard_map/ppermute | solution.py:246
  9.6 4.8 %collective-permute-done.1.refs_6_ = bf16[256,512]{1,0:T(8,128)(2,1)S(1)} collective-permute-done((bf16[256,512]{1,0:T(8,128)(2,1)S(1)}, bf16[256,512]{1,0:T(8,128)(2,1)S(1)}, u32[]{:S(2)}, u32[]{:S(2)}) %collective-permute-start.1) | collective-permute-done | bytes 262176 | tf_op jit(solution)/shard_map/ppermute | solution.py:246
  14.4 3.4 %collective-permute-start.2 = (bf16[256,512]{1,0:T(8,128)(2,1)S(1)}, bf16[256,512]{1,0:T(8,128)(2,1)S(1)}, u32[]{:S(2)}, u32[]{:S(2)}) collective-permute-start(bf16[256,512]{1,0:T(8,128)(2,1)S(1)} %collective-permute-done.1.refs_6_), channel_id=1, source_target_pairs={{0,16},{8,24},{16,0},{24,8},{1,17},{9,25},{17,1},{25,9},{2,18},{10... | collective-permute-start | bytes 786440 | tf_op jit(solution)/shard_map/ppermute | solution.py:238
  17.8 4.5 %collective-permute-done.4.refs_7_ = bf16[256,512]{1,0:T(8,128)(2,1)S(1)} collective-permute-done((bf16[256,512]{1,0:T(8,128)(2,1)S(1)}, bf16[256,512]{1,0:T(8,128)(2,1)S(1)}, u32[]{:S(2)}, u32[]{:S(2)}) %collective-permute-start.4) | collective-permute-done | bytes 262176 | tf_op jit(solution)/shard_map/ppermute | solution.py:246
  23.3 1.3 %collective-permute-done.2.refs_9_ = bf16[256,512]{1,0:T(8,128)(2,1)S(1)} collective-permute-done((bf16[256,512]{1,0:T(8,128)(2,1)S(1)}, bf16[256,512]{1,0:T(8,128)(2,1)S(1)}, u32[]{:S(2)}, u32[]{:S(2)}) %collective-permute-start.2) | collective-permute-done | bytes 262176 | tf_op jit(solution)/shard_map/ppermute | solution.py:238
  24.6 1.7 %collective-permute-start.7 = (bf16[1,2,64,384]{3,2,1,0:T(8,128)(2,1)S(1)}, bf16[1,2,64,384]{3,2,1,0:T(8,128)(2,1)S(1)}, u32[]{:S(2)}, u32[]{:S(2)}) collective-permute-start(bf16[1,2,64,384]{3,2,1,0:T(8,128)(2,1)S(1)} %maximum_bitcast_fusion), channel_id=1, source_target_pairs={{0,4},{1,5},{2,6},{3,7},{4,0},{5,1},{6,2},{7,3},{8,12},{9,13},{10,... | collective-permute-start | bytes 294920 | tf_op jit(solution)/shard_map/ppermute | solution.py:235
  26.3 4.0 %collective-permute-done.7 = bf16[1,2,64,384]{3,2,1,0:T(8,128)(2,1)S(1)} collective-permute-done((bf16[1,2,64,384]{3,2,1,0:T(8,128)(2,1)S(1)}, bf16[1,2,64,384]{3,2,1,0:T(8,128)(2,1)S(1)}, u32[]{:S(2)}, u32[]{:S(2)}) %collective-permute-start.7) | collective-permute-done | bytes 98336 | tf_op jit(solution)/shard_map/ppermute | solution.py:235
  30.3 2.0 %collective-permute-done.6.refs_8_ = bf16[256,512]{1,0:T(8,128)(2,1)S(1)} collective-permute-done((bf16[256,512]{1,0:T(8,128)(2,1)S(1)}, bf16[256,512]{1,0:T(8,128)(2,1)S(1)}, u32[]{:S(2)}, u32[]{:S(2)}) %collective-permute-start.6) | collective-permute-done | bytes 262176 | tf_op jit(solution)/shard_map/ppermute | solution.py:235
  32.9 1.4 %collective-permute-start.11 = (bf16[2,2,64,384]{3,2,1,0:T(8,128)(2,1)S(1)}, bf16[2,2,64,384]{3,2,1,0:T(8,128)(2,1)S(1)}, u32[]{:S(2)}, u32[]{:S(2)}) collective-permute-start(bf16[2,2,64,384]{3,2,1,0:T(8,128)(2,1)S(1)} %pad_maximum_fusion.3), channel_id=1, source_target_pairs={{0,2},{1,3},{2,0},{3,1},{4,6},{5,7},{6,4},{7,5},{8,10},{9,11},{10,... | collective-permute-start | bytes 589832 | tf_op jit(solution)/shard_map/ppermute | solution.py:235
  34.3 1.3 %collective-permute-start.8 = (bf16[256,512]{1,0:T(8,128)(2,1)S(1)}, bf16[256,512]{1,0:T(8,128)(2,1)S(1)}, u32[]{:S(2)}, u32[]{:S(2)}) collective-permute-start(bf16[256,512]{1,0:T(8,128)(2,1)S(1)} %collective-permute-done.6.refs_8_), channel_id=1, source_target_pairs={{0,16},{8,24},{16,0},{24,8},{1,17},{9,25},{17,1},{25,9},{2,18},{10... | collective-permute-start | bytes 786440 | tf_op jit(solution)/shard_map/ppermute | solution.py:238
  35.6 4.1 %collective-permute-done.11 = bf16[2,2,64,384]{3,2,1,0:T(8,128)(2,1)S(1)} collective-permute-done((bf16[2,2,64,384]{3,2,1,0:T(8,128)(2,1)S(1)}, bf16[2,2,64,384]{3,2,1,0:T(8,128)(2,1)S(1)}, u32[]{:S(2)}, u32[]{:S(2)}) %collective-permute-start.11) | collective-permute-done | bytes 196640 | tf_op jit(solution)/shard_map/ppermute | solution.py:235
  39.8 2.5 %collective-permute-done.8.refs_11_ = bf16[256,512]{1,0:T(8,128)(2,1)S(1)} collective-permute-done((bf16[256,512]{1,0:T(8,128)(2,1)S(1)}, bf16[256,512]{1,0:T(8,128)(2,1)S(1)}, u32[]{:S(2)}, u32[]{:S(2)}) %collective-permute-start.8) | collective-permute-done | bytes 262176 | tf_op jit(solution)/shard_map/ppermute | solution.py:238
  42.3 2.0 %shard_map.112 = (bf16[512,256]{1,0:T(8,128)(2,1)S(1)}, bf16[512,256]{1,0:T(8,128)(2,1)S(1)}, bf16[512,128]{1,0:T(8,128)(2,1)S(1)}, bf16[2048,512]{1,0:T(8,128)(2,1)S(1)}) custom-call(bf16[256,2048]{1,0:T(8,128)(2,1)S(1)} %get-tuple-element.62.refs_0_, bf16[256,2048]{1,0:T(8,128)(2,1)S(1)} %collective-permute-done.9.refs_1_, ...), custom_call_target="tpu_custom_call" | custom-call | flops 1342177280 | bytes 9109504 | tf_op jit(solution)/shard_map/pallas_call | solution.py:26
  44.4 1.5 %shard_map.113 = (f32[128,2048]{1,0:T(8,128)S(1)}, f32[128,2048]{1,0:T(8,128)S(1)}, bf16[128,2048]{1,0:T(8,128)(2,1)S(1)}, bf16[128,2048]{1,0:T(8,128)(2,1)S(1)}) custom-call(bf16[512,256]{1,0:T(8,128)(2,1)S(1)} %get-tuple-element.76.dgu_ref, bf16[2048,512]{1,0:T(8,128)(2,1)S(1)} %get-tuple-element.77.full_ref), custom_call_target="tpu_custom_call" | custom-call | flops 536870912 | bytes 5505024 | tf_op jit(solution)/shard_map/pallas_call | solution.py:26
  46.4 1.2 %collective-permute-start.18 = (bf16[4,2,64,384]{3,2,1,0:T(8,128)(2,1)S(1)}, bf16[4,2,64,384]{3,2,1,0:T(8,128)(2,1)S(1)}, u32[]{:S(2)}, u32[]{:S(2)}) collective-permute-start(bf16[4,2,64,384]{3,2,1,0:T(8,128)(2,1)S(1)} %pad_maximum_fusion.1.refs_3_), channel_id=1, source_target_pairs={{0,8},{8,0},{16,24},{24,16},{1,9},{9,1},{17,25},{25,17},{2,10},{10... | collective-permute-start | bytes 1179656 | tf_op jit(solution)/shard_map/ppermute | solution.py:238
  48.1 1.8 %collective-permute-start.15 = (bf16[3,64,128]{2,1,0:T(8,128)(2,1)S(1)}, bf16[3,64,128]{2,1,0:T(8,128)(2,1)S(1)}, u32[]{:S(2)}, u32[]{:S(2)}) collective-permute-start(bf16[3,64,128]{2,1,0:T(8,128)(2,1)S(1)} %get-tuple-element.91), channel_id=1, source_target_pairs={{0,2},{1,3},{2,0},{3,1},{4,6},{5,7},{6,4},{7,5},{8,10},{9,11},{10,... | collective-permute-start | bytes 147464 | tf_op jit(solution)/shard_map/ppermute | solution.py:235
  50.7 1.9 %collective-permute-start.17 = (bf16[3,64,128]{2,1,0:T(8,128)(2,1)S(1)}, bf16[3,64,128]{2,1,0:T(8,128)(2,1)S(1)}, u32[]{:S(2)}, u32[]{:S(2)}) collective-permute-start(bf16[3,64,128]{2,1,0:T(8,128)(2,1)S(1)} %get-tuple-element.93), channel_id=1, source_target_pairs={{0,6},{1,7},{2,4},{3,5},{4,2},{5,3},{6,0},{7,1},{8,14},{9,15},{10,... | collective-permute-start | bytes 147464 | tf_op jit(solution)/shard_map/ppermute | solution.py:235
  52.6 1.2 %collective-permute-start.23 = (bf16[128,2048]{1,0:T(8,128)(2,1)S(1)}, bf16[128,2048]{1,0:T(8,128)(2,1)S(1)}, u32[]{:S(2)}, u32[]{:S(2)}) collective-permute-start(bf16[128,2048]{1,0:T(8,128)(2,1)S(1)} %add_convert_fusion.1), channel_id=1, source_target_pairs={{0,8},{8,0},{16,24},{24,16},{1,9},{9,1},{17,25},{25,17},{2,10},{10... | collective-permute-start | bytes 1572872 | tf_op jit(solution)/shard_map/ppermute | solution.py:238
  53.7 4.7 %collective-permute-done.18.refs_4_ = bf16[4,2,64,384]{3,2,1,0:T(8,128)(2,1)S(1)} collective-permute-done((bf16[4,2,64,384]{3,2,1,0:T(8,128)(2,1)S(1)}, bf16[4,2,64,384]{3,2,1,0:T(8,128)(2,1)S(1)}, u32[]{:S(2)}, u32[]{:S(2)}) %collective-permute-start.18) | collective-permute-done | bytes 393248 | tf_op jit(solution)/shard_map/ppermute | solution.py:238
  58.4 1.4 %collective-permute-start.19 = (bf16[3,64,128]{2,1,0:T(8,128)(2,1)S(1)}, bf16[3,64,128]{2,1,0:T(8,128)(2,1)S(1)}, u32[]{:S(2)}, u32[]{:S(2)}) collective-permute-start(bf16[3,64,128]{2,1,0:T(8,128)(2,1)S(1)} %add_convert_fusion.3), channel_id=1, source_target_pairs={{0,16},{8,24},{16,0},{24,8},{1,17},{9,25},{17,1},{25,9},{2,18},{10... | collective-permute-start | bytes 147464 | tf_op jit(solution)/shard_map/ppermute | solution.py:238
  59.8 2.8 %collective-permute-done.19 = bf16[3,64,128]{2,1,0:T(8,128)(2,1)S(1)} collective-permute-done((bf16[3,64,128]{2,1,0:T(8,128)(2,1)S(1)}, bf16[3,64,128]{2,1,0:T(8,128)(2,1)S(1)}, u32[]{:S(2)}, u32[]{:S(2)}) %collective-permute-start.19) | collective-permute-done | bytes 49184 | tf_op jit(solution)/shard_map/ppermute | solution.py:238
  62.6 1.5 %collective-permute-start.22 = (bf16[3,64,128]{2,1,0:T(8,128)(2,1)S(1)}, bf16[3,64,128]{2,1,0:T(8,128)(2,1)S(1)}, u32[]{:S(2)}, u32[]{:S(2)}) collective-permute-start(bf16[3,64,128]{2,1,0:T(8,128)(2,1)S(1)} %add_convert_fusion.2), channel_id=1, source_target_pairs={{0,6},{1,7},{2,4},{3,5},{4,2},{5,3},{6,0},{7,1},{8,14},{9,15},{10,... | collective-permute-start | bytes 147464 | tf_op jit(solution)/shard_map/ppermute | solution.py:235
  65.0 2.0 %collective-permute-start.20 = (bf16[3,64,128]{2,1,0:T(8,128)(2,1)S(1)}, bf16[3,64,128]{2,1,0:T(8,128)(2,1)S(1)}, u32[]{:S(2)}, u32[]{:S(2)}) collective-permute-start(bf16[3,64,128]{2,1,0:T(8,128)(2,1)S(1)} %add_convert_fusion.2), channel_id=1, source_target_pairs={{0,2},{1,3},{2,0},{3,1},{4,6},{5,7},{6,4},{7,5},{8,10},{9,11},{10,... | collective-permute-start | bytes 147464 | tf_op jit(solution)/shard_map/ppermute | solution.py:235
  67.1 1.5 %collective-permute-done.22 = bf16[3,64,128]{2,1,0:T(8,128)(2,1)S(1)} collective-permute-done((bf16[3,64,128]{2,1,0:T(8,128)(2,1)S(1)}, bf16[3,64,128]{2,1,0:T(8,128)(2,1)S(1)}, u32[]{:S(2)}, u32[]{:S(2)}) %collective-permute-start.22) | collective-permute-done | bytes 49184 | tf_op jit(solution)/shard_map/ppermute | solution.py:235
  68.6 1.1 %collective-permute-done.21 = bf16[3,64,128]{2,1,0:T(8,128)(2,1)S(1)} collective-permute-done((bf16[3,64,128]{2,1,0:T(8,128)(2,1)S(1)}, bf16[3,64,128]{2,1,0:T(8,128)(2,1)S(1)}, u32[]{:S(2)}, u32[]{:S(2)}) %collective-permute-start.21) | collective-permute-done | bytes 49184 | tf_op jit(solution)/shard_map/ppermute | solution.py:235
  69.7 1.8 %collective-permute-start.24 = (bf16[4,3,64,128]{3,2,1,0:T(8,128)(2,1)S(1)}, bf16[4,3,64,128]{3,2,1,0:T(8,128)(2,1)S(1)}, u32[]{:S(2)}, u32[]{:S(2)}) collective-permute-start(bf16[4,3,64,128]{3,2,1,0:T(8,128)(2,1)S(1)} %get-tuple-element.109.refs_0_), channel_id=1, source_target_pairs={{0,8},{8,0},{16,24},{24,16},{1,9},{9,1},{17,25},{25,17},{2,10},{10... | collective-permute-start | bytes 589832 | tf_op jit(solution)/shard_map/ppermute | solution.py:238
  71.7 3.8 %collective-permute-done.24.refs_1_ = bf16[4,3,64,128]{3,2,1,0:T(8,128)(2,1)S(1)} collective-permute-done((bf16[4,3,64,128]{3,2,1,0:T(8,128)(2,1)S(1)}, bf16[4,3,64,128]{3,2,1,0:T(8,128)(2,1)S(1)}, u32[]{:S(2)}, u32[]{:S(2)}) %collective-permute-start.24) | collective-permute-done | bytes 196640 | tf_op jit(solution)/shard_map/ppermute | solution.py:238
  75.6 1.0 %add_convert_fusion = bf16[128,2048]{1,0:T(8,128)(2,1)} fusion(bf16[128,2048]{1,0:T(8,128)(2,1)S(1)} %collective-permute-done.23, f32[128,2048]{1,0:T(8,128)S(1)} %get-tuple-element.78, bf16[128,2048]{1,0:T(8,128)(2,1)S(1)} %collective-permute-done.12), kind=kLoop, calls=%fused_computation | loop fusion | flops 1310720 | bytes 2621440 | tf_op jit(solution)/shard_map/convert_element_type | solution.py:363
  77.3 2.7 %shard_map.115 = (f32[3,32,512]{2,1,0:T(8,128)}, f32[3,32,512]{2,1,0:T(8,128)}, f32[3,256,512]{2,1,0:T(8,128)}) custom-call(bf16[4,3,64,128]{3,2,1,0:T(8,128)(2,1)S(1)} %get-tuple-element.109.refs_0_, bf16[4,3,64,128]{3,2,1,0:T(8,128)(2,1)S(1)} %collective-permute-done.24.refs_1_, bf16[2,4,3,64,128]{4,3,2,1,0:T(8,128)(2,1)S(1)} %collective-permute-done.25.refs_2_, ...), custom_call_target="tpu_custom_call" | custom-call | flops 402653184 | bytes 4980736 | tf_op jit(solution)/shard_map/pallas_call | solution.py:26
  (44 shorter events, 5.4 us)
Async XLA Ops:
  2.4 12.0 %collective-permute-start.1 = (bf16[256,512]{1,0:T(8,128)(2,1)S(1)}, bf16[256,512]{1,0:T(8,128)(2,1)S(1)}, u32[]{:S(2)}, u32[]{:S(2)}) collective-permute-start(bf16[256,512]{1,0:T(8,128)(2,1)S(1)} %get-tuple-element.57), channel_id=1, source_target_pairs={{0,2},{1,3},{2,0},{3,1},{4,6},{5,7},{6,4},{7,5},{8,10},{9,11},{10,... | collective-permute-start | bytes 786440 | tf_op jit(solution)/shard_map/ppermute | solution.py:246
  5.5 26.8 %collective-permute-start = (bf16[256,2048]{1,0:T(8,128)(2,1)S(1)}, bf16[256,2048]{1,0:T(8,128)(2,1)S(1)}, u32[]{:S(2)}, u32[]{:S(2)}) collective-permute-start(bf16[256,2048]{1,0:T(8,128)(2,1)S(1)} %get-tuple-element.62.refs_0_), channel_id=1, source_target_pairs={{0,8},{8,0},{16,24},{24,16},{1,9},{9,1},{17,25},{25,17},{2,10},{10... | collective-permute-start | bytes 3145736 | tf_op jit(solution)/shard_map/ppermute | solution.py:238
  7.0 16.2 %collective-permute-start.3 = (bf16[320,512]{1,0:T(8,128)(2,1)S(1)}, bf16[320,512]{1,0:T(8,128)(2,1)S(1)}, u32[]{:S(2)}, u32[]{:S(2)}) collective-permute-start(bf16[320,512]{1,0:T(8,128)(2,1)S(1)} %get-tuple-element.58), channel_id=1, source_target_pairs={{0,1},{1,0},{2,3},{3,2},{4,5},{5,4},{6,7},{7,6},{8,9},{9,8},{10,11... | collective-permute-start | bytes 983048 | tf_op jit(solution)/shard_map/ppermute | solution.py:235
  7.0 15.3 %collective-permute-start.4 = (bf16[256,512]{1,0:T(8,128)(2,1)S(1)}, bf16[256,512]{1,0:T(8,128)(2,1)S(1)}, u32[]{:S(2)}, u32[]{:S(2)}) collective-permute-start(bf16[256,512]{1,0:T(8,128)(2,1)S(1)} %get-tuple-element.57), channel_id=1, source_target_pairs={{0,4},{1,5},{2,6},{3,7},{4,0},{5,1},{6,2},{7,3},{8,12},{9,13},{10,... | collective-permute-start | bytes 786440 | tf_op jit(solution)/shard_map/ppermute | solution.py:246
  14.4 10.2 %collective-permute-start.2 = (bf16[256,512]{1,0:T(8,128)(2,1)S(1)}, bf16[256,512]{1,0:T(8,128)(2,1)S(1)}, u32[]{:S(2)}, u32[]{:S(2)}) collective-permute-start(bf16[256,512]{1,0:T(8,128)(2,1)S(1)} %collective-permute-done.1.refs_6_), channel_id=1, source_target_pairs={{0,16},{8,24},{16,0},{24,8},{1,17},{9,25},{17,1},{25,9},{2,18},{10... | collective-permute-start | bytes 786440 | tf_op jit(solution)/shard_map/ppermute | solution.py:238
  22.3 10.0 %collective-permute-start.6 = (bf16[256,512]{1,0:T(8,128)(2,1)S(1)}, bf16[256,512]{1,0:T(8,128)(2,1)S(1)}, u32[]{:S(2)}, u32[]{:S(2)}) collective-permute-start(bf16[256,512]{1,0:T(8,128)(2,1)S(1)} %collective-permute-done.4.refs_7_), channel_id=1, source_target_pairs={{0,2},{1,3},{2,0},{3,1},{4,6},{5,7},{6,4},{7,5},{8,10},{9,11},{10,... | collective-permute-start | bytes 786440 | tf_op jit(solution)/shard_map/ppermute | solution.py:235
  22.3 10.0 %collective-permute-start.5 = (bf16[256,512]{1,0:T(8,128)(2,1)S(1)}, bf16[256,512]{1,0:T(8,128)(2,1)S(1)}, u32[]{:S(2)}, u32[]{:S(2)}) collective-permute-start(bf16[256,512]{1,0:T(8,128)(2,1)S(1)} %collective-permute-done.4.refs_7_), channel_id=1, source_target_pairs={{0,16},{8,24},{16,0},{24,8},{1,17},{9,25},{17,1},{25,9},{2,18},{10... | collective-permute-start | bytes 786440 | tf_op jit(solution)/shard_map/ppermute | solution.py:238
  24.6 5.7 %collective-permute-start.7 = (bf16[1,2,64,384]{3,2,1,0:T(8,128)(2,1)S(1)}, bf16[1,2,64,384]{3,2,1,0:T(8,128)(2,1)S(1)}, u32[]{:S(2)}, u32[]{:S(2)}) collective-permute-start(bf16[1,2,64,384]{3,2,1,0:T(8,128)(2,1)S(1)} %maximum_bitcast_fusion), channel_id=1, source_target_pairs={{0,4},{1,5},{2,6},{3,7},{4,0},{5,1},{6,2},{7,3},{8,12},{9,13},{10,... | collective-permute-start | bytes 294920 | tf_op jit(solution)/shard_map/ppermute | solution.py:235
  32.4 9.9 %collective-permute-start.9 = (bf16[256,2048]{1,0:T(8,128)(2,1)S(1)}, bf16[256,2048]{1,0:T(8,128)(2,1)S(1)}, u32[]{:S(2)}, u32[]{:S(2)}) collective-permute-start(bf16[256,2048]{1,0:T(8,128)(2,1)S(1)} %get-tuple-element.62.refs_0_), channel_id=1, source_target_pairs={{0,1},{1,0},{2,3},{3,2},{4,5},{5,4},{6,7},{7,6},{8,9},{9,8},{10,11... | collective-permute-start | bytes 3145736 | tf_op jit(solution)/shard_map/ppermute | solution.py:235
  32.4 9.9 %collective-permute-start.10 = (bf16[256,2048]{1,0:T(8,128)(2,1)S(1)}, bf16[256,2048]{1,0:T(8,128)(2,1)S(1)}, u32[]{:S(2)}, u32[]{:S(2)}) collective-permute-start(bf16[256,2048]{1,0:T(8,128)(2,1)S(1)} %collective-permute-done.refs_2_), channel_id=1, source_target_pairs={{0,1},{1,0},{2,3},{3,2},{4,5},{5,4},{6,7},{7,6},{8,9},{9,8},{10,11... | collective-permute-start | bytes 3145736 | tf_op jit(solution)/shard_map/ppermute | solution.py:235
  32.9 6.9 %collective-permute-start.11 = (bf16[2,2,64,384]{3,2,1,0:T(8,128)(2,1)S(1)}, bf16[2,2,64,384]{3,2,1,0:T(8,128)(2,1)S(1)}, u32[]{:S(2)}, u32[]{:S(2)}) collective-permute-start(bf16[2,2,64,384]{3,2,1,0:T(8,128)(2,1)S(1)} %pad_maximum_fusion.3), channel_id=1, source_target_pairs={{0,2},{1,3},{2,0},{3,1},{4,6},{5,7},{6,4},{7,5},{8,10},{9,11},{10,... | collective-permute-start | bytes 589832 | tf_op jit(solution)/shard_map/ppermute | solution.py:235
  34.3 8.0 %collective-permute-start.8 = (bf16[256,512]{1,0:T(8,128)(2,1)S(1)}, bf16[256,512]{1,0:T(8,128)(2,1)S(1)}, u32[]{:S(2)}, u32[]{:S(2)}) collective-permute-start(bf16[256,512]{1,0:T(8,128)(2,1)S(1)} %collective-permute-done.6.refs_8_), channel_id=1, source_target_pairs={{0,16},{8,24},{16,0},{24,8},{1,17},{9,25},{17,1},{25,9},{2,18},{10... | collective-permute-start | bytes 786440 | tf_op jit(solution)/shard_map/ppermute | solution.py:238
  44.3 1.6 %collective-permute-start.13 = (bf16[512,256]{1,0:T(8,128)(2,1)S(1)}, bf16[512,256]{1,0:T(8,128)(2,1)S(1)}, u32[]{:S(2)}, u32[]{:S(2)}) collective-permute-start(bf16[512,256]{1,0:T(8,128)(2,1)S(1)} %get-tuple-element.80.mine_ref), channel_id=1, source_target_pairs={{0,1},{1,0},{2,3},{3,2},{4,5},{5,4},{6,7},{7,6},{8,9},{9,8},{10,11... | collective-permute-start | bytes 786440 | tf_op jit(solution)/shard_map/ppermute | solution.py:235
  45.9 2.1 %collective-permute-start.14 = (bf16[128,2048]{1,0:T(8,128)(2,1)S(1)}, bf16[128,2048]{1,0:T(8,128)(2,1)S(1)}, u32[]{:S(2)}, u32[]{:S(2)}) collective-permute-start(bf16[128,2048]{1,0:T(8,128)(2,1)S(1)} %get-tuple-element.89), channel_id=1, source_target_pairs={{0,1},{1,0},{2,3},{3,2},{4,5},{5,4},{6,7},{7,6},{8,9},{9,8},{10,11... | collective-permute-start | bytes 1572872 | tf_op jit(solution)/shard_map/ppermute | solution.py:235
  46.4 12.0 %collective-permute-start.18 = (bf16[4,2,64,384]{3,2,1,0:T(8,128)(2,1)S(1)}, bf16[4,2,64,384]{3,2,1,0:T(8,128)(2,1)S(1)}, u32[]{:S(2)}, u32[]{:S(2)}) collective-permute-start(bf16[4,2,64,384]{3,2,1,0:T(8,128)(2,1)S(1)} %pad_maximum_fusion.1.refs_3_), channel_id=1, source_target_pairs={{0,8},{8,0},{16,24},{24,16},{1,9},{9,1},{17,25},{25,17},{2,10},{10... | collective-permute-start | bytes 1179656 | tf_op jit(solution)/shard_map/ppermute | solution.py:238
  48.1 10.3 %collective-permute-start.15 = (bf16[3,64,128]{2,1,0:T(8,128)(2,1)S(1)}, bf16[3,64,128]{2,1,0:T(8,128)(2,1)S(1)}, u32[]{:S(2)}, u32[]{:S(2)}) collective-permute-start(bf16[3,64,128]{2,1,0:T(8,128)(2,1)S(1)} %get-tuple-element.91), channel_id=1, source_target_pairs={{0,2},{1,3},{2,0},{3,1},{4,6},{5,7},{6,4},{7,5},{8,10},{9,11},{10,... | collective-permute-start | bytes 147464 | tf_op jit(solution)/shard_map/ppermute | solution.py:235
  49.9 8.5 %collective-permute-start.16 = (bf16[3,64,128]{2,1,0:T(8,128)(2,1)S(1)}, bf16[3,64,128]{2,1,0:T(8,128)(2,1)S(1)}, u32[]{:S(2)}, u32[]{:S(2)}) collective-permute-start(bf16[3,64,128]{2,1,0:T(8,128)(2,1)S(1)} %get-tuple-element.92), channel_id=1, source_target_pairs={{0,4},{1,5},{2,6},{3,7},{4,0},{5,1},{6,2},{7,3},{8,12},{9,13},{10,... | collective-permute-start | bytes 147464 | tf_op jit(solution)/shard_map/ppermute | solution.py:235
  50.7 7.7 %collective-permute-start.17 = (bf16[3,64,128]{2,1,0:T(8,128)(2,1)S(1)}, bf16[3,64,128]{2,1,0:T(8,128)(2,1)S(1)}, u32[]{:S(2)}, u32[]{:S(2)}) collective-permute-start(bf16[3,64,128]{2,1,0:T(8,128)(2,1)S(1)} %get-tuple-element.93), channel_id=1, source_target_pairs={{0,6},{1,7},{2,4},{3,5},{4,2},{5,3},{6,0},{7,1},{8,14},{9,15},{10,... | collective-permute-start | bytes 147464 | tf_op jit(solution)/shard_map/ppermute | solution.py:235
  52.6 17.1 %collective-permute-start.23 = (bf16[128,2048]{1,0:T(8,128)(2,1)S(1)}, bf16[128,2048]{1,0:T(8,128)(2,1)S(1)}, u32[]{:S(2)}, u32[]{:S(2)}) collective-permute-start(bf16[128,2048]{1,0:T(8,128)(2,1)S(1)} %add_convert_fusion.1), channel_id=1, source_target_pairs={{0,8},{8,0},{16,24},{24,16},{1,9},{9,1},{17,25},{25,17},{2,10},{10... | collective-permute-start | bytes 1572872 | tf_op jit(solution)/shard_map/ppermute | solution.py:238
  58.4 4.2 %collective-permute-start.19 = (bf16[3,64,128]{2,1,0:T(8,128)(2,1)S(1)}, bf16[3,64,128]{2,1,0:T(8,128)(2,1)S(1)}, u32[]{:S(2)}, u32[]{:S(2)}) collective-permute-start(bf16[3,64,128]{2,1,0:T(8,128)(2,1)S(1)} %add_convert_fusion.3), channel_id=1, source_target_pairs={{0,16},{8,24},{16,0},{24,8},{1,17},{9,25},{17,1},{25,9},{2,18},{10... | collective-permute-start | bytes 147464 | tf_op jit(solution)/shard_map/ppermute | solution.py:238
  62.6 6.0 %collective-permute-start.22 = (bf16[3,64,128]{2,1,0:T(8,128)(2,1)S(1)}, bf16[3,64,128]{2,1,0:T(8,128)(2,1)S(1)}, u32[]{:S(2)}, u32[]{:S(2)}) collective-permute-start(bf16[3,64,128]{2,1,0:T(8,128)(2,1)S(1)} %add_convert_fusion.2), channel_id=1, source_target_pairs={{0,6},{1,7},{2,4},{3,5},{4,2},{5,3},{6,0},{7,1},{8,14},{9,15},{10,... | collective-permute-start | bytes 147464 | tf_op jit(solution)/shard_map/ppermute | solution.py:235
  64.1 5.5 %collective-permute-start.21 = (bf16[3,64,128]{2,1,0:T(8,128)(2,1)S(1)}, bf16[3,64,128]{2,1,0:T(8,128)(2,1)S(1)}, u32[]{:S(2)}, u32[]{:S(2)}) collective-permute-start(bf16[3,64,128]{2,1,0:T(8,128)(2,1)S(1)} %add_convert_fusion.2), channel_id=1, source_target_pairs={{0,4},{1,5},{2,6},{3,7},{4,0},{5,1},{6,2},{7,3},{8,12},{9,13},{10,... | collective-permute-start | bytes 147464 | tf_op jit(solution)/shard_map/ppermute | solution.py:235
  65.0 4.6 %collective-permute-start.20 = (bf16[3,64,128]{2,1,0:T(8,128)(2,1)S(1)}, bf16[3,64,128]{2,1,0:T(8,128)(2,1)S(1)}, u32[]{:S(2)}, u32[]{:S(2)}) collective-permute-start(bf16[3,64,128]{2,1,0:T(8,128)(2,1)S(1)} %add_convert_fusion.2), channel_id=1, source_target_pairs={{0,2},{1,3},{2,0},{3,1},{4,6},{5,7},{6,4},{7,5},{8,10},{9,11},{10,... | collective-permute-start | bytes 147464 | tf_op jit(solution)/shard_map/ppermute | solution.py:235
  67.1 8.5 %collective-permute-start.12 = (bf16[128,2048]{1,0:T(8,128)(2,1)S(1)}, bf16[128,2048]{1,0:T(8,128)(2,1)S(1)}, u32[]{:S(2)}, u32[]{:S(2)}) collective-permute-start(bf16[128,2048]{1,0:T(8,128)(2,1)S(1)} %get-tuple-element.79), channel_id=1, source_target_pairs={{0,1},{1,0},{2,3},{3,2},{4,5},{5,4},{6,7},{7,6},{8,9},{9,8},{10,11... | collective-permute-start | bytes 1572872 | tf_op jit(solution)/shard_map/ppermute | solution.py:235
  69.7 5.7 %collective-permute-start.24 = (bf16[4,3,64,128]{3,2,1,0:T(8,128)(2,1)S(1)}, bf16[4,3,64,128]{3,2,1,0:T(8,128)(2,1)S(1)}, u32[]{:S(2)}, u32[]{:S(2)}) collective-permute-start(bf16[4,3,64,128]{3,2,1,0:T(8,128)(2,1)S(1)} %get-tuple-element.109.refs_0_), channel_id=1, source_target_pairs={{0,8},{8,0},{16,24},{24,16},{1,9},{9,1},{17,25},{25,17},{2,10},{10... | collective-permute-start | bytes 589832 | tf_op jit(solution)/shard_map/ppermute | solution.py:238
  71.6 5.7 %copy-start = (f32[256,256]{1,0:T(8,128)S(1)}, f32[256,256]{1,0:T(8,128)}, u32[]{:S(2)}) copy-start(f32[256,256]{1,0:T(8,128)} %refs_6_.3) | copy-start | bytes 786436
  71.6 5.7 %copy-start.1 = (f32[3,32,512]{2,1,0:T(8,128)S(1)}, f32[3,32,512]{2,1,0:T(8,128)}, u32[]{:S(2)}) copy-start(f32[3,32,512]{2,1,0:T(8,128)} %refs_7_.3) | copy-start | bytes 589828
  71.6 5.7 %copy-start.2 = (f32[3,32,512]{2,1,0:T(8,128)S(1)}, f32[3,32,512]{2,1,0:T(8,128)}, u32[]{:S(2)}) copy-start(f32[3,32,512]{2,1,0:T(8,128)} %refs_8_.1) | copy-start | bytes 589828
  71.6 5.0 %collective-permute-start.26 = (bf16[2,4,2,64,384]{4,3,2,1,0:T(8,128)(2,1)S(1)}, bf16[2,4,2,64,384]{4,3,2,1,0:T(8,128)(2,1)S(1)}, u32[]{:S(2)}, u32[]{:S(2)}) collective-permute-start(bf16[2,4,2,64,384]{4,3,2,1,0:T(8,128)(2,1)S(1)} %pad_maximum_fusion), channel_id=1, source_target_pairs={{0,1},{1,0},{2,3},{3,2},{4,5},{5,4},{6,7},{7,6},{8,9},{9,8},{10,11... | collective-permute-start | bytes 2359304 | tf_op jit(solution)/shard_map/ppermute | solution.py:235
  75.5 1.8 %collective-permute-start.25 = (bf16[2,4,3,64,128]{4,3,2,1,0:T(8,128)(2,1)S(1)}, bf16[2,4,3,64,128]{4,3,2,1,0:T(8,128)(2,1)S(1)}, u32[]{:S(2)}, u32[]{:S(2)}) collective-permute-start(bf16[2,4,3,64,128]{4,3,2,1,0:T(8,128)(2,1)S(1)} %pad_maximum_fusion.2), channel_id=1, source_target_pairs={{0,1},{1,0},{2,3},{3,2},{4,5},{5,4},{6,7},{7,6},{8,9},{9,8},{10,11... | collective-permute-start | bytes 1179656 | tf_op jit(solution)/shard_map/ppermute | solution.py:235

commit v5 on v4

--- a/solution.py
+++ b/solution.py
@@ -281,20 +281,20 @@
     def forward(which):
         return by_group(jnp.concatenate([near[k] for k in groups_of[which]]), 2)
 
-    far = [forward(0), forward(1)]
     for k in passed:
         near[k] = by_member(near[k & (k - 1)], 2 * (k & -k))
+    far = [forward(0), forward(1)]
     far[0], from_core = ordered((far[0], from_core))
     moms = jnp.stack([mom_mine, from_core[depth:, : parts * unit]])[None]
     for bit in reversed(direct[1:]):
         moms = jnp.concatenate([moms, by_member(moms, 2 * bit)])
-    both_x, both, far, near, moms = ordered((both_x, both, far, near, moms))
+    near, far, both_x, both, moms = ordered((near, far, both_x, both, moms))
 
     far.append(forward(2))
     both_c = by_member(both, 1)
     both_xc = by_member(both_x, 1)
     moms = jnp.concatenate([moms, by_member(moms, 2)])
-    far, both_c, both_xc, moms = ordered((far, both_c, both_xc, moms))
+    far, both_c, both_xc = ordered((far, both_c, both_xc))
 
     layout = [(0, 0), (1, 0)]
     for k in range(1, chips):
@@ -314,6 +314,7 @@
         *(both, both_c, both_x, both_xc),
         *(own, from_core, *(near[k] for k in range(1, chips)), *far),
     )
+    dgu, moms = ordered((dgu, moms))
     proj_core = by_member(proj, 1)
     moms_x = by_group(moms, 1)
     keep_0, keep_1, send_0, send_1 = call(
@@ -340,8 +341,8 @@
     )
     near_part = (keep_1 + near_part.astype(F32)).astype(BF)
     lows, near_part = ordered((lows, near_part))
-    arrived = [by_member(lows[k], 2 * k) for k in range(1, chips)]
-    arrived, moms_x = ordered((arrived, moms_x))
+    arrived = [by_member(lows[k], 2 * k) for k in reversed(range(1, chips))]
+    moms_x, arrived = ordered((moms_x, arrived))
     core_moms = by_member(jnp.stack([moms, moms_x]), 1)
     grad_side = by_group(near_part, 1)
     share = lows[0]
@@ -355,9 +356,9 @@
         bit *= 2
     share = share.astype(BF)
 
-    low_mine = [share] + [by_member(share, 2 * k) for k in range(1, chips)]
-    low_mine, grad_side = ordered((low_mine, grad_side))
-    low_mine = jnp.stack(low_mine)
+    low_mine = [by_member(share, 2 * k) for k in reversed(range(1, chips))]
+    grad_side, low_mine = ordered((grad_side, low_mine))
+    low_mine = jnp.stack([share] + low_mine[::-1])
     low_side = by_group(low_mine, 1)
     mine_part = keep_0 + by_member(send_0, 1).astype(F32)
     input_grad = (mine_part + grad_side.astype(F32)).astype(BF)

time: 80.2 us -> 79.6 us (level)
  waiting for transfers between devices: 37.7 us -> 35.9 us
  starting transfers between devices: 31.7 us -> 33 us
    ppermute x17, waiting for transfers between devices: 13.5 us -> 9.68 us  [by_member(): lax.ppermute(value, 'member', [(i, i ^ bits) for i in range(members)])]
    ppermute x8, waiting for transfers between devices: 15 us -> 17 us  [by_group(): return lax.ppermute(value, 'group', [(i, i ^ bits) for i in range(groups)])]
    ppermute x8, starting transfers between devices: 12.7 us -> 14 us  [by_group(): return lax.ppermute(value, 'group', [(i, i ^ bits) for i in range(groups)])]
  transfers between devices with their start and end apart: 27 -> 27, of which waited for: 13 -> 12; matrix products, arithmetic and copies ran while one was open for 2% -> 2% of each run, Pallas kernels for 2% -> 5%
where the time goes in v5:
time: 79.6 us; the launch traced here: 79.5 us
  waiting for transfers between devices  35.9 us (45%)
  starting transfers between devices  33 us (41%)
  Pallas kernels  8.34 us (10%)
  other arithmetic  1.39 us (2%)
  between operations  0.83 us (1%)
    ppermute x8, waiting for transfers between devices, by_group(): return lax.ppermute(value, 'group', [(i, i ^ bits) for i in range(groups)])  17 us
    ppermute x8, starting transfers between devices, by_group(): return lax.ppermute(value, 'group', [(i, i ^ bits) for i in range(groups)])  14 us
    ppermute x17, starting transfers between devices, by_member(): lax.ppermute(value, 'member', [(i, i ^ bits) for i in range(members)])  13.3 us
    ppermute x17, waiting for transfers between devices, by_member(): lax.ppermute(value, 'member', [(i, i ^ bits) for i in range(members)])  9.68 us
    ppermute x2, waiting for transfers between devices, by_chip(): return lax.ppermute(value, ('group', 'member'), pairs)  9.25 us
    pallas_call x5, Pallas kernels, call(): pl.pallas_call(body, out_shape=[(pltpu.VMEM if pinned else jax.ShapeDtype...  8.34 us
    ppermute x2, starting transfers between devices, by_chip(): return lax.ppermute(value, ('group', 'member'), pairs)  5.68 us
  transfers between devices with their start and end apart: 27, of which 12 were waited for; matrix products, arithmetic and copies ran while one was open for 2% of the time, Pallas kernels for 5%

profile of v5, /device:TPU:0, one launch (start us, length us, event | category | flops | bytes accessed | tf_op | source)
XLA Modules:
  0.0 79.5 jit_solution(9463592554528310829)
XLA Ops:
  0.6 1.8 %shard_map.111 = (bf16[256,512]{1,0:T(8,128)(2,1)S(1)}, bf16[256,512]{1,0:T(8,128)(2,1)S(1)}, bf16[320,512]{1,0:T(8,128)(2,1)S(1)}, bf16[64,384]{1,0:T(8,128)(2,1)S(1)}, bf16[256,2048]{1,0:T(8,128)(2,1)S(1)}) custom-call(bf16[256,512]{1,0:T(8,128)(2,1)} %refs_0_.1, bf16[256,512]{1,0:T(8,128)(2,1)} %refs_1_.1, bf16[256,512]{1,0:T(8,128)(2,1)} %refs_2_.1, ...), custom_call_target="tpu_custom_call" | custom-call | bytes 4440064 | tf_op jit(solution)/shard_map/pallas_call | solution.py:26
  2.4 3.1 %collective-permute-start = (bf16[256,512]{1,0:T(8,128)(2,1)S(1)}, bf16[256,512]{1,0:T(8,128)(2,1)S(1)}, u32[]{:S(2)}, u32[]{:S(2)}) collective-permute-start(bf16[256,512]{1,0:T(8,128)(2,1)S(1)} %get-tuple-element.56), channel_id=1, source_target_pairs={{0,2},{1,3},{2,0},{3,1},{4,6},{5,7},{6,4},{7,5},{8,10},{9,11},{10,... | collective-permute-start | bytes 786440 | tf_op jit(solution)/shard_map/ppermute | solution.py:246
  5.5 1.5 %collective-permute-start.6 = (bf16[256,2048]{1,0:T(8,128)(2,1)S(1)}, bf16[256,2048]{1,0:T(8,128)(2,1)S(1)}, u32[]{:S(2)}, u32[]{:S(2)}) collective-permute-start(bf16[256,2048]{1,0:T(8,128)(2,1)S(1)} %get-tuple-element.62.refs_0_), channel_id=1, source_target_pairs={{0,8},{8,0},{16,24},{24,16},{1,9},{9,1},{17,25},{25,17},{2,10},{10... | collective-permute-start | bytes 3145736 | tf_op jit(solution)/shard_map/ppermute | solution.py:238
  7.0 2.6 %collective-permute-start.1 = (bf16[256,512]{1,0:T(8,128)(2,1)S(1)}, bf16[256,512]{1,0:T(8,128)(2,1)S(1)}, u32[]{:S(2)}, u32[]{:S(2)}) collective-permute-start(bf16[256,512]{1,0:T(8,128)(2,1)S(1)} %get-tuple-element.56), channel_id=1, source_target_pairs={{0,4},{1,5},{2,6},{3,7},{4,0},{5,1},{6,2},{7,3},{8,12},{9,13},{10,... | collective-permute-start | bytes 786440 | tf_op jit(solution)/shard_map/ppermute | solution.py:246
  9.6 4.8 %collective-permute-done.refs_6_ = bf16[256,512]{1,0:T(8,128)(2,1)S(1)} collective-permute-done((bf16[256,512]{1,0:T(8,128)(2,1)S(1)}, bf16[256,512]{1,0:T(8,128)(2,1)S(1)}, u32[]{:S(2)}, u32[]{:S(2)}) %collective-permute-start) | collective-permute-done | bytes 262176 | tf_op jit(solution)/shard_map/ppermute | solution.py:246
  14.4 3.4 %collective-permute-start.3 = (bf16[256,512]{1,0:T(8,128)(2,1)S(1)}, bf16[256,512]{1,0:T(8,128)(2,1)S(1)}, u32[]{:S(2)}, u32[]{:S(2)}) collective-permute-start(bf16[256,512]{1,0:T(8,128)(2,1)S(1)} %collective-permute-done.refs_6_), channel_id=1, source_target_pairs={{0,16},{8,24},{16,0},{24,8},{1,17},{9,25},{17,1},{25,9},{2,18},{10... | collective-permute-start | bytes 786440 | tf_op jit(solution)/shard_map/ppermute | solution.py:238
  17.8 4.5 %collective-permute-done.1.refs_7_ = bf16[256,512]{1,0:T(8,128)(2,1)S(1)} collective-permute-done((bf16[256,512]{1,0:T(8,128)(2,1)S(1)}, bf16[256,512]{1,0:T(8,128)(2,1)S(1)}, u32[]{:S(2)}, u32[]{:S(2)}) %collective-permute-start.1) | collective-permute-done | bytes 262176 | tf_op jit(solution)/shard_map/ppermute | solution.py:246
  22.3 0.9 %collective-permute-start.5 = (bf16[256,512]{1,0:T(8,128)(2,1)S(1)}, bf16[256,512]{1,0:T(8,128)(2,1)S(1)}, u32[]{:S(2)}, u32[]{:S(2)}) collective-permute-start(bf16[256,512]{1,0:T(8,128)(2,1)S(1)} %collective-permute-done.1.refs_7_), channel_id=1, source_target_pairs={{0,16},{8,24},{16,0},{24,8},{1,17},{9,25},{17,1},{25,9},{2,18},{10... | collective-permute-start | bytes 786440 | tf_op jit(solution)/shard_map/ppermute | solution.py:238
  23.3 1.3 %collective-permute-done.3.refs_9_ = bf16[256,512]{1,0:T(8,128)(2,1)S(1)} collective-permute-done((bf16[256,512]{1,0:T(8,128)(2,1)S(1)}, bf16[256,512]{1,0:T(8,128)(2,1)S(1)}, u32[]{:S(2)}, u32[]{:S(2)}) %collective-permute-start.3) | collective-permute-done | bytes 262176 | tf_op jit(solution)/shard_map/ppermute | solution.py:238
  24.6 1.7 %collective-permute-start.7 = (bf16[1,2,64,384]{3,2,1,0:T(8,128)(2,1)S(1)}, bf16[1,2,64,384]{3,2,1,0:T(8,128)(2,1)S(1)}, u32[]{:S(2)}, u32[]{:S(2)}) collective-permute-start(bf16[1,2,64,384]{3,2,1,0:T(8,128)(2,1)S(1)} %maximum_bitcast_fusion), channel_id=1, source_target_pairs={{0,4},{1,5},{2,6},{3,7},{4,0},{5,1},{6,2},{7,3},{8,12},{9,13},{10,... | collective-permute-start | bytes 294920 | tf_op jit(solution)/shard_map/ppermute | solution.py:235
  26.3 4.0 %collective-permute-done.7 = bf16[1,2,64,384]{3,2,1,0:T(8,128)(2,1)S(1)} collective-permute-done((bf16[1,2,64,384]{3,2,1,0:T(8,128)(2,1)S(1)}, bf16[1,2,64,384]{3,2,1,0:T(8,128)(2,1)S(1)}, u32[]{:S(2)}, u32[]{:S(2)}) %collective-permute-start.7) | collective-permute-done | bytes 98336 | tf_op jit(solution)/shard_map/ppermute | solution.py:235
  30.3 2.0 %collective-permute-done.2.refs_8_ = bf16[256,512]{1,0:T(8,128)(2,1)S(1)} collective-permute-done((bf16[256,512]{1,0:T(8,128)(2,1)S(1)}, bf16[256,512]{1,0:T(8,128)(2,1)S(1)}, u32[]{:S(2)}, u32[]{:S(2)}) %collective-permute-start.2) | collective-permute-done | bytes 262176 | tf_op jit(solution)/shard_map/ppermute | solution.py:235
  32.9 1.3 %collective-permute-start.8 = (bf16[256,512]{1,0:T(8,128)(2,1)S(1)}, bf16[256,512]{1,0:T(8,128)(2,1)S(1)}, u32[]{:S(2)}, u32[]{:S(2)}) collective-permute-start(bf16[256,512]{1,0:T(8,128)(2,1)S(1)} %collective-permute-done.2.refs_8_), channel_id=1, source_target_pairs={{0,16},{8,24},{16,0},{24,8},{1,17},{9,25},{17,1},{25,9},{2,18},{10... | collective-permute-start | bytes 786440 | tf_op jit(solution)/shard_map/ppermute | solution.py:238
  34.2 1.4 %collective-permute-start.11 = (bf16[2,2,64,384]{3,2,1,0:T(8,128)(2,1)S(1)}, bf16[2,2,64,384]{3,2,1,0:T(8,128)(2,1)S(1)}, u32[]{:S(2)}, u32[]{:S(2)}) collective-permute-start(bf16[2,2,64,384]{3,2,1,0:T(8,128)(2,1)S(1)} %pad_maximum_fusion.3), channel_id=1, source_target_pairs={{0,2},{1,3},{2,0},{3,1},{4,6},{5,7},{6,4},{7,5},{8,10},{9,11},{10,... | collective-permute-start | bytes 589832 | tf_op jit(solution)/shard_map/ppermute | solution.py:235
  35.6 5.5 %collective-permute-done.8.refs_11_ = bf16[256,512]{1,0:T(8,128)(2,1)S(1)} collective-permute-done((bf16[256,512]{1,0:T(8,128)(2,1)S(1)}, bf16[256,512]{1,0:T(8,128)(2,1)S(1)}, u32[]{:S(2)}, u32[]{:S(2)}) %collective-permute-start.8) | collective-permute-done | bytes 262176 | tf_op jit(solution)/shard_map/ppermute | solution.py:238
  41.2 2.0 %shard_map.112 = (bf16[512,256]{1,0:T(8,128)(2,1)S(1)}, bf16[512,256]{1,0:T(8,128)(2,1)S(1)}, bf16[512,128]{1,0:T(8,128)(2,1)S(1)}, bf16[2048,512]{1,0:T(8,128)(2,1)S(1)}) custom-call(bf16[256,2048]{1,0:T(8,128)(2,1)S(1)} %get-tuple-element.62.refs_0_, bf16[256,2048]{1,0:T(8,128)(2,1)S(1)} %collective-permute-done.9.refs_1_, ...), custom_call_target="tpu_custom_call" | custom-call | flops 1342177280 | bytes 9109504 | tf_op jit(solution)/shard_map/pallas_call | solution.py:26
  43.3 1.5 %shard_map.113 = (f32[128,2048]{1,0:T(8,128)S(1)}, f32[128,2048]{1,0:T(8,128)S(1)}, bf16[128,2048]{1,0:T(8,128)(2,1)S(1)}, bf16[128,2048]{1,0:T(8,128)(2,1)S(1)}) custom-call(bf16[512,256]{1,0:T(8,128)(2,1)S(1)} %get-tuple-element.77.dgu_ref, bf16[2048,512]{1,0:T(8,128)(2,1)S(1)} %get-tuple-element.78.full_ref), custom_call_target="tpu_custom_call" | custom-call | flops 536870912 | bytes 5505024 | tf_op jit(solution)/shard_map/pallas_call | solution.py:26
  45.3 2.3 %collective-permute-start.16 = (bf16[4,2,64,384]{3,2,1,0:T(8,128)(2,1)S(1)}, bf16[4,2,64,384]{3,2,1,0:T(8,128)(2,1)S(1)}, u32[]{:S(2)}, u32[]{:S(2)}) collective-permute-start(bf16[4,2,64,384]{3,2,1,0:T(8,128)(2,1)S(1)} %pad_maximum_fusion.1.refs_3_), channel_id=1, source_target_pairs={{0,8},{8,0},{16,24},{24,16},{1,9},{9,1},{17,25},{25,17},{2,10},{10... | collective-permute-start | bytes 1179656 | tf_op jit(solution)/shard_map/ppermute | solution.py:238
  48.2 2.0 %collective-permute-start.17 = (bf16[3,64,128]{2,1,0:T(8,128)(2,1)S(1)}, bf16[3,64,128]{2,1,0:T(8,128)(2,1)S(1)}, u32[]{:S(2)}, u32[]{:S(2)}) collective-permute-start(bf16[3,64,128]{2,1,0:T(8,128)(2,1)S(1)} %get-tuple-element.94), channel_id=1, source_target_pairs={{0,6},{1,7},{2,4},{3,5},{4,2},{5,3},{6,0},{7,1},{8,14},{9,15},{10,... | collective-permute-start | bytes 147464 | tf_op jit(solution)/shard_map/ppermute | solution.py:235
  50.2 2.4 %collective-permute-start.19 = (bf16[3,64,128]{2,1,0:T(8,128)(2,1)S(1)}, bf16[3,64,128]{2,1,0:T(8,128)(2,1)S(1)}, u32[]{:S(2)}, u32[]{:S(2)}) collective-permute-start(bf16[3,64,128]{2,1,0:T(8,128)(2,1)S(1)} %get-tuple-element.96), channel_id=1, source_target_pairs={{0,2},{1,3},{2,0},{3,1},{4,6},{5,7},{6,4},{7,5},{8,10},{9,11},{10,... | collective-permute-start | bytes 147464 | tf_op jit(solution)/shard_map/ppermute | solution.py:235
  52.6 1.2 %collective-permute-start.15 = (bf16[128,2048]{1,0:T(8,128)(2,1)S(1)}, bf16[128,2048]{1,0:T(8,128)(2,1)S(1)}, u32[]{:S(2)}, u32[]{:S(2)}) collective-permute-start(bf16[128,2048]{1,0:T(8,128)(2,1)S(1)} %add_convert_fusion.1), channel_id=1, source_target_pairs={{0,8},{8,0},{16,24},{24,16},{1,9},{9,1},{17,25},{25,17},{2,10},{10... | collective-permute-start | bytes 1572872 | tf_op jit(solution)/shard_map/ppermute | solution.py:238
  53.8 3.8 %collective-permute-done.16.refs_4_ = bf16[4,2,64,384]{3,2,1,0:T(8,128)(2,1)S(1)} collective-permute-done((bf16[4,2,64,384]{3,2,1,0:T(8,128)(2,1)S(1)}, bf16[4,2,64,384]{3,2,1,0:T(8,128)(2,1)S(1)}, u32[]{:S(2)}, u32[]{:S(2)}) %collective-permute-start.16) | collective-permute-done | bytes 393248 | tf_op jit(solution)/shard_map/ppermute | solution.py:238
  57.6 1.5 %collective-permute-start.20 = (bf16[3,64,128]{2,1,0:T(8,128)(2,1)S(1)}, bf16[3,64,128]{2,1,0:T(8,128)(2,1)S(1)}, u32[]{:S(2)}, u32[]{:S(2)}) collective-permute-start(bf16[3,64,128]{2,1,0:T(8,128)(2,1)S(1)} %add_convert_fusion.3), channel_id=1, source_target_pairs={{0,16},{8,24},{16,0},{24,8},{1,17},{9,25},{17,1},{25,9},{2,18},{10... | collective-permute-start | bytes 147464 | tf_op jit(solution)/shard_map/ppermute | solution.py:238
  59.1 2.6 %collective-permute-done.20 = bf16[3,64,128]{2,1,0:T(8,128)(2,1)S(1)} collective-permute-done((bf16[3,64,128]{2,1,0:T(8,128)(2,1)S(1)}, bf16[3,64,128]{2,1,0:T(8,128)(2,1)S(1)}, u32[]{:S(2)}, u32[]{:S(2)}) %collective-permute-start.20) | collective-permute-done | bytes 49184 | tf_op jit(solution)/shard_map/ppermute | solution.py:238
  61.8 2.4 %collective-permute-start.21 = (bf16[3,64,128]{2,1,0:T(8,128)(2,1)S(1)}, bf16[3,64,128]{2,1,0:T(8,128)(2,1)S(1)}, u32[]{:S(2)}, u32[]{:S(2)}) collective-permute-start(bf16[3,64,128]{2,1,0:T(8,128)(2,1)S(1)} %add_convert_fusion.2), channel_id=1, source_target_pairs={{0,6},{1,7},{2,4},{3,5},{4,2},{5,3},{6,0},{7,1},{8,14},{9,15},{10,... | collective-permute-start | bytes 147464 | tf_op jit(solution)/shard_map/ppermute | solution.py:235
  64.5 1.8 %collective-permute-start.23 = (bf16[3,64,128]{2,1,0:T(8,128)(2,1)S(1)}, bf16[3,64,128]{2,1,0:T(8,128)(2,1)S(1)}, u32[]{:S(2)}, u32[]{:S(2)}) collective-permute-start(bf16[3,64,128]{2,1,0:T(8,128)(2,1)S(1)} %add_convert_fusion.2), channel_id=1, source_target_pairs={{0,2},{1,3},{2,0},{3,1},{4,6},{5,7},{6,4},{7,5},{8,10},{9,11},{10,... | collective-permute-start | bytes 147464 | tf_op jit(solution)/shard_map/ppermute | solution.py:235
  66.3 1.5 %collective-permute-done.21 = bf16[3,64,128]{2,1,0:T(8,128)(2,1)S(1)} collective-permute-done((bf16[3,64,128]{2,1,0:T(8,128)(2,1)S(1)}, bf16[3,64,128]{2,1,0:T(8,128)(2,1)S(1)}, u32[]{:S(2)}, u32[]{:S(2)}) %collective-permute-start.21) | collective-permute-done | bytes 49184 | tf_op jit(solution)/shard_map/ppermute | solution.py:235
  67.8 1.4 %collective-permute-done.22 = bf16[3,64,128]{2,1,0:T(8,128)(2,1)S(1)} collective-permute-done((bf16[3,64,128]{2,1,0:T(8,128)(2,1)S(1)}, bf16[3,64,128]{2,1,0:T(8,128)(2,1)S(1)}, u32[]{:S(2)}, u32[]{:S(2)}) %collective-permute-start.22) | collective-permute-done | bytes 49184 | tf_op jit(solution)/shard_map/ppermute | solution.py:235
  69.2 1.8 %collective-permute-start.24 = (bf16[4,3,64,128]{3,2,1,0:T(8,128)(2,1)S(1)}, bf16[4,3,64,128]{3,2,1,0:T(8,128)(2,1)S(1)}, u32[]{:S(2)}, u32[]{:S(2)}) collective-permute-start(bf16[4,3,64,128]{3,2,1,0:T(8,128)(2,1)S(1)} %get-tuple-element.109.refs_0_), channel_id=1, source_target_pairs={{0,8},{8,0},{16,24},{24,16},{1,9},{9,1},{17,25},{25,17},{2,10},{10... | collective-permute-start | bytes 589832 | tf_op jit(solution)/shard_map/ppermute | solution.py:238
  71.2 3.7 %collective-permute-done.24.refs_1_ = bf16[4,3,64,128]{3,2,1,0:T(8,128)(2,1)S(1)} collective-permute-done((bf16[4,3,64,128]{3,2,1,0:T(8,128)(2,1)S(1)}, bf16[4,3,64,128]{3,2,1,0:T(8,128)(2,1)S(1)}, u32[]{:S(2)}, u32[]{:S(2)}) %collective-permute-start.24) | collective-permute-done | bytes 196640 | tf_op jit(solution)/shard_map/ppermute | solution.py:238
  75.1 1.0 %add_convert_fusion = bf16[128,2048]{1,0:T(8,128)(2,1)} fusion(bf16[128,2048]{1,0:T(8,128)(2,1)S(1)} %collective-permute-done.15, f32[128,2048]{1,0:T(8,128)S(1)} %get-tuple-element.79, bf16[128,2048]{1,0:T(8,128)(2,1)S(1)} %collective-permute-done.12), kind=kLoop, calls=%fused_computation | loop fusion | flops 1310720 | bytes 2621440 | tf_op jit(solution)/shard_map/convert_element_type | solution.py:364
  76.8 2.7 %shard_map.115 = (f32[3,32,512]{2,1,0:T(8,128)}, f32[3,32,512]{2,1,0:T(8,128)}, f32[3,256,512]{2,1,0:T(8,128)}) custom-call(bf16[4,3,64,128]{3,2,1,0:T(8,128)(2,1)S(1)} %get-tuple-element.109.refs_0_, bf16[4,3,64,128]{3,2,1,0:T(8,128)(2,1)S(1)} %collective-permute-done.24.refs_1_, bf16[2,4,3,64,128]{4,3,2,1,0:T(8,128)(2,1)S(1)} %collective-permute-done.25.refs_2_, ...), custom_call_target="tpu_custom_call" | custom-call | flops 402653184 | bytes 4980736 | tf_op jit(solution)/shard_map/pallas_call | solution.py:26
  (44 shorter events, 3.1 us)
Async XLA Ops:
  2.4 12.0 %collective-permute-start = (bf16[256,512]{1,0:T(8,128)(2,1)S(1)}, bf16[256,512]{1,0:T(8,128)(2,1)S(1)}, u32[]{:S(2)}, u32[]{:S(2)}) collective-permute-start(bf16[256,512]{1,0:T(8,128)(2,1)S(1)} %get-tuple-element.56), channel_id=1, source_target_pairs={{0,2},{1,3},{2,0},{3,1},{4,6},{5,7},{6,4},{7,5},{8,10},{9,11},{10,... | collective-permute-start | bytes 786440 | tf_op jit(solution)/shard_map/ppermute | solution.py:246
  5.5 26.8 %collective-permute-start.6 = (bf16[256,2048]{1,0:T(8,128)(2,1)S(1)}, bf16[256,2048]{1,0:T(8,128)(2,1)S(1)}, u32[]{:S(2)}, u32[]{:S(2)}) collective-permute-start(bf16[256,2048]{1,0:T(8,128)(2,1)S(1)} %get-tuple-element.62.refs_0_), channel_id=1, source_target_pairs={{0,8},{8,0},{16,24},{24,16},{1,9},{9,1},{17,25},{25,17},{2,10},{10... | collective-permute-start | bytes 3145736 | tf_op jit(solution)/shard_map/ppermute | solution.py:238
  7.0 16.2 %collective-permute-start.4 = (bf16[320,512]{1,0:T(8,128)(2,1)S(1)}, bf16[320,512]{1,0:T(8,128)(2,1)S(1)}, u32[]{:S(2)}, u32[]{:S(2)}) collective-permute-start(bf16[320,512]{1,0:T(8,128)(2,1)S(1)} %get-tuple-element.57), channel_id=1, source_target_pairs={{0,1},{1,0},{2,3},{3,2},{4,5},{5,4},{6,7},{7,6},{8,9},{9,8},{10,11... | collective-permute-start | bytes 983048 | tf_op jit(solution)/shard_map/ppermute | solution.py:235
  7.0 15.3 %collective-permute-start.1 = (bf16[256,512]{1,0:T(8,128)(2,1)S(1)}, bf16[256,512]{1,0:T(8,128)(2,1)S(1)}, u32[]{:S(2)}, u32[]{:S(2)}) collective-permute-start(bf16[256,512]{1,0:T(8,128)(2,1)S(1)} %get-tuple-element.56), channel_id=1, source_target_pairs={{0,4},{1,5},{2,6},{3,7},{4,0},{5,1},{6,2},{7,3},{8,12},{9,13},{10,... | collective-permute-start | bytes 786440 | tf_op jit(solution)/shard_map/ppermute | solution.py:246
  14.4 10.2 %collective-permute-start.3 = (bf16[256,512]{1,0:T(8,128)(2,1)S(1)}, bf16[256,512]{1,0:T(8,128)(2,1)S(1)}, u32[]{:S(2)}, u32[]{:S(2)}) collective-permute-start(bf16[256,512]{1,0:T(8,128)(2,1)S(1)} %collective-permute-done.refs_6_), channel_id=1, source_target_pairs={{0,16},{8,24},{16,0},{24,8},{1,17},{9,25},{17,1},{25,9},{2,18},{10... | collective-permute-start | bytes 786440 | tf_op jit(solution)/shard_map/ppermute | solution.py:238
  22.3 10.0 %collective-permute-start.2 = (bf16[256,512]{1,0:T(8,128)(2,1)S(1)}, bf16[256,512]{1,0:T(8,128)(2,1)S(1)}, u32[]{:S(2)}, u32[]{:S(2)}) collective-permute-start(bf16[256,512]{1,0:T(8,128)(2,1)S(1)} %collective-permute-done.1.refs_7_), channel_id=1, source_target_pairs={{0,2},{1,3},{2,0},{3,1},{4,6},{5,7},{6,4},{7,5},{8,10},{9,11},{10,... | collective-permute-start | bytes 786440 | tf_op jit(solution)/shard_map/ppermute | solution.py:235
  22.3 10.0 %collective-permute-start.5 = (bf16[256,512]{1,0:T(8,128)(2,1)S(1)}, bf16[256,512]{1,0:T(8,128)(2,1)S(1)}, u32[]{:S(2)}, u32[]{:S(2)}) collective-permute-start(bf16[256,512]{1,0:T(8,128)(2,1)S(1)} %collective-permute-done.1.refs_7_), channel_id=1, source_target_pairs={{0,16},{8,24},{16,0},{24,8},{1,17},{9,25},{17,1},{25,9},{2,18},{10... | collective-permute-start | bytes 786440 | tf_op jit(solution)/shard_map/ppermute | solution.py:238
  24.6 5.7 %collective-permute-start.7 = (bf16[1,2,64,384]{3,2,1,0:T(8,128)(2,1)S(1)}, bf16[1,2,64,384]{3,2,1,0:T(8,128)(2,1)S(1)}, u32[]{:S(2)}, u32[]{:S(2)}) collective-permute-start(bf16[1,2,64,384]{3,2,1,0:T(8,128)(2,1)S(1)} %maximum_bitcast_fusion), channel_id=1, source_target_pairs={{0,4},{1,5},{2,6},{3,7},{4,0},{5,1},{6,2},{7,3},{8,12},{9,13},{10,... | collective-permute-start | bytes 294920 | tf_op jit(solution)/shard_map/ppermute | solution.py:235
  32.4 8.8 %collective-permute-start.9 = (bf16[256,2048]{1,0:T(8,128)(2,1)S(1)}, bf16[256,2048]{1,0:T(8,128)(2,1)S(1)}, u32[]{:S(2)}, u32[]{:S(2)}) collective-permute-start(bf16[256,2048]{1,0:T(8,128)(2,1)S(1)} %get-tuple-element.62.refs_0_), channel_id=1, source_target_pairs={{0,1},{1,0},{2,3},{3,2},{4,5},{5,4},{6,7},{7,6},{8,9},{9,8},{10,11... | collective-permute-start | bytes 3145736 | tf_op jit(solution)/shard_map/ppermute | solution.py:235
  32.4 8.8 %collective-permute-start.10 = (bf16[256,2048]{1,0:T(8,128)(2,1)S(1)}, bf16[256,2048]{1,0:T(8,128)(2,1)S(1)}, u32[]{:S(2)}, u32[]{:S(2)}) collective-permute-start(bf16[256,2048]{1,0:T(8,128)(2,1)S(1)} %collective-permute-done.6.refs_2_), channel_id=1, source_target_pairs={{0,1},{1,0},{2,3},{3,2},{4,5},{5,4},{6,7},{7,6},{8,9},{9,8},{10,11... | collective-permute-start | bytes 3145736 | tf_op jit(solution)/shard_map/ppermute | solution.py:235
  32.9 8.3 %collective-permute-start.8 = (bf16[256,512]{1,0:T(8,128)(2,1)S(1)}, bf16[256,512]{1,0:T(8,128)(2,1)S(1)}, u32[]{:S(2)}, u32[]{:S(2)}) collective-permute-start(bf16[256,512]{1,0:T(8,128)(2,1)S(1)} %collective-permute-done.2.refs_8_), channel_id=1, source_target_pairs={{0,16},{8,24},{16,0},{24,8},{1,17},{9,25},{17,1},{25,9},{2,18},{10... | collective-permute-start | bytes 786440 | tf_op jit(solution)/shard_map/ppermute | solution.py:238
  34.2 9.0 %collective-permute-start.11 = (bf16[2,2,64,384]{3,2,1,0:T(8,128)(2,1)S(1)}, bf16[2,2,64,384]{3,2,1,0:T(8,128)(2,1)S(1)}, u32[]{:S(2)}, u32[]{:S(2)}) collective-permute-start(bf16[2,2,64,384]{3,2,1,0:T(8,128)(2,1)S(1)} %pad_maximum_fusion.3), channel_id=1, source_target_pairs={{0,2},{1,3},{2,0},{3,1},{4,6},{5,7},{6,4},{7,5},{8,10},{9,11},{10,... | collective-permute-start | bytes 589832 | tf_op jit(solution)/shard_map/ppermute | solution.py:235
  43.1 1.6 %collective-permute-start.13 = (bf16[512,256]{1,0:T(8,128)(2,1)S(1)}, bf16[512,256]{1,0:T(8,128)(2,1)S(1)}, u32[]{:S(2)}, u32[]{:S(2)}) collective-permute-start(bf16[512,256]{1,0:T(8,128)(2,1)S(1)} %get-tuple-element.81.mine_ref), channel_id=1, source_target_pairs={{0,1},{1,0},{2,3},{3,2},{4,5},{5,4},{6,7},{7,6},{8,9},{9,8},{10,11... | collective-permute-start | bytes 786440 | tf_op jit(solution)/shard_map/ppermute | solution.py:235
  44.8 3.3 %collective-permute-start.14 = (bf16[128,2048]{1,0:T(8,128)(2,1)S(1)}, bf16[128,2048]{1,0:T(8,128)(2,1)S(1)}, u32[]{:S(2)}, u32[]{:S(2)}) collective-permute-start(bf16[128,2048]{1,0:T(8,128)(2,1)S(1)} %get-tuple-element.90), channel_id=1, source_target_pairs={{0,1},{1,0},{2,3},{3,2},{4,5},{5,4},{6,7},{7,6},{8,9},{9,8},{10,11... | collective-permute-start | bytes 1572872 | tf_op jit(solution)/shard_map/ppermute | solution.py:235
  45.3 12.2 %collective-permute-start.16 = (bf16[4,2,64,384]{3,2,1,0:T(8,128)(2,1)S(1)}, bf16[4,2,64,384]{3,2,1,0:T(8,128)(2,1)S(1)}, u32[]{:S(2)}, u32[]{:S(2)}) collective-permute-start(bf16[4,2,64,384]{3,2,1,0:T(8,128)(2,1)S(1)} %pad_maximum_fusion.1.refs_3_), channel_id=1, source_target_pairs={{0,8},{8,0},{16,24},{24,16},{1,9},{9,1},{17,25},{25,17},{2,10},{10... | collective-permute-start | bytes 1179656 | tf_op jit(solution)/shard_map/ppermute | solution.py:238
  48.2 9.4 %collective-permute-start.17 = (bf16[3,64,128]{2,1,0:T(8,128)(2,1)S(1)}, bf16[3,64,128]{2,1,0:T(8,128)(2,1)S(1)}, u32[]{:S(2)}, u32[]{:S(2)}) collective-permute-start(bf16[3,64,128]{2,1,0:T(8,128)(2,1)S(1)} %get-tuple-element.94), channel_id=1, source_target_pairs={{0,6},{1,7},{2,4},{3,5},{4,2},{5,3},{6,0},{7,1},{8,14},{9,15},{10,... | collective-permute-start | bytes 147464 | tf_op jit(solution)/shard_map/ppermute | solution.py:235
  50.2 7.4 %collective-permute-start.18 = (bf16[3,64,128]{2,1,0:T(8,128)(2,1)S(1)}, bf16[3,64,128]{2,1,0:T(8,128)(2,1)S(1)}, u32[]{:S(2)}, u32[]{:S(2)}) collective-permute-start(bf16[3,64,128]{2,1,0:T(8,128)(2,1)S(1)} %get-tuple-element.95), channel_id=1, source_target_pairs={{0,4},{1,5},{2,6},{3,7},{4,0},{5,1},{6,2},{7,3},{8,12},{9,13},{10,... | collective-permute-start | bytes 147464 | tf_op jit(solution)/shard_map/ppermute | solution.py:235
  50.2 7.4 %collective-permute-start.19 = (bf16[3,64,128]{2,1,0:T(8,128)(2,1)S(1)}, bf16[3,64,128]{2,1,0:T(8,128)(2,1)S(1)}, u32[]{:S(2)}, u32[]{:S(2)}) collective-permute-start(bf16[3,64,128]{2,1,0:T(8,128)(2,1)S(1)} %get-tuple-element.96), channel_id=1, source_target_pairs={{0,2},{1,3},{2,0},{3,1},{4,6},{5,7},{6,4},{7,5},{8,10},{9,11},{10,... | collective-permute-start | bytes 147464 | tf_op jit(solution)/shard_map/ppermute | solution.py:235
  52.6 16.5 %collective-permute-start.15 = (bf16[128,2048]{1,0:T(8,128)(2,1)S(1)}, bf16[128,2048]{1,0:T(8,128)(2,1)S(1)}, u32[]{:S(2)}, u32[]{:S(2)}) collective-permute-start(bf16[128,2048]{1,0:T(8,128)(2,1)S(1)} %add_convert_fusion.1), channel_id=1, source_target_pairs={{0,8},{8,0},{16,24},{24,16},{1,9},{9,1},{17,25},{25,17},{2,10},{10... | collective-permute-start | bytes 1572872 | tf_op jit(solution)/shard_map/ppermute | solution.py:238
  57.6 4.2 %collective-permute-start.20 = (bf16[3,64,128]{2,1,0:T(8,128)(2,1)S(1)}, bf16[3,64,128]{2,1,0:T(8,128)(2,1)S(1)}, u32[]{:S(2)}, u32[]{:S(2)}) collective-permute-start(bf16[3,64,128]{2,1,0:T(8,128)(2,1)S(1)} %add_convert_fusion.3), channel_id=1, source_target_pairs={{0,16},{8,24},{16,0},{24,8},{1,17},{9,25},{17,1},{25,9},{2,18},{10... | collective-permute-start | bytes 147464 | tf_op jit(solution)/shard_map/ppermute | solution.py:238
  61.8 6.0 %collective-permute-start.21 = (bf16[3,64,128]{2,1,0:T(8,128)(2,1)S(1)}, bf16[3,64,128]{2,1,0:T(8,128)(2,1)S(1)}, u32[]{:S(2)}, u32[]{:S(2)}) collective-permute-start(bf16[3,64,128]{2,1,0:T(8,128)(2,1)S(1)} %add_convert_fusion.2), channel_id=1, source_target_pairs={{0,6},{1,7},{2,4},{3,5},{4,2},{5,3},{6,0},{7,1},{8,14},{9,15},{10,... | collective-permute-start | bytes 147464 | tf_op jit(solution)/shard_map/ppermute | solution.py:235
  64.2 5.0 %collective-permute-start.22 = (bf16[3,64,128]{2,1,0:T(8,128)(2,1)S(1)}, bf16[3,64,128]{2,1,0:T(8,128)(2,1)S(1)}, u32[]{:S(2)}, u32[]{:S(2)}) collective-permute-start(bf16[3,64,128]{2,1,0:T(8,128)(2,1)S(1)} %add_convert_fusion.2), channel_id=1, source_target_pairs={{0,4},{1,5},{2,6},{3,7},{4,0},{5,1},{6,2},{7,3},{8,12},{9,13},{10,... | collective-permute-start | bytes 147464 | tf_op jit(solution)/shard_map/ppermute | solution.py:235
  64.5 4.7 %collective-permute-start.23 = (bf16[3,64,128]{2,1,0:T(8,128)(2,1)S(1)}, bf16[3,64,128]{2,1,0:T(8,128)(2,1)S(1)}, u32[]{:S(2)}, u32[]{:S(2)}) collective-permute-start(bf16[3,64,128]{2,1,0:T(8,128)(2,1)S(1)} %add_convert_fusion.2), channel_id=1, source_target_pairs={{0,2},{1,3},{2,0},{3,1},{4,6},{5,7},{6,4},{7,5},{8,10},{9,11},{10,... | collective-permute-start | bytes 147464 | tf_op jit(solution)/shard_map/ppermute | solution.py:235
  66.3 8.8 %collective-permute-start.12 = (bf16[128,2048]{1,0:T(8,128)(2,1)S(1)}, bf16[128,2048]{1,0:T(8,128)(2,1)S(1)}, u32[]{:S(2)}, u32[]{:S(2)}) collective-permute-start(bf16[128,2048]{1,0:T(8,128)(2,1)S(1)} %get-tuple-element.80), channel_id=1, source_target_pairs={{0,1},{1,0},{2,3},{3,2},{4,5},{5,4},{6,7},{7,6},{8,9},{9,8},{10,11... | collective-permute-start | bytes 1572872 | tf_op jit(solution)/shard_map/ppermute | solution.py:235
  69.2 5.7 %collective-permute-start.24 = (bf16[4,3,64,128]{3,2,1,0:T(8,128)(2,1)S(1)}, bf16[4,3,64,128]{3,2,1,0:T(8,128)(2,1)S(1)}, u32[]{:S(2)}, u32[]{:S(2)}) collective-permute-start(bf16[4,3,64,128]{3,2,1,0:T(8,128)(2,1)S(1)} %get-tuple-element.109.refs_0_), channel_id=1, source_target_pairs={{0,8},{8,0},{16,24},{24,16},{1,9},{9,1},{17,25},{25,17},{2,10},{10... | collective-permute-start | bytes 589832 | tf_op jit(solution)/shard_map/ppermute | solution.py:238
  71.1 5.6 %copy-start = (f32[256,256]{1,0:T(8,128)S(1)}, f32[256,256]{1,0:T(8,128)}, u32[]{:S(2)}) copy-start(f32[256,256]{1,0:T(8,128)} %refs_6_.3) | copy-start | bytes 786436
  71.1 5.6 %copy-start.1 = (f32[3,32,512]{2,1,0:T(8,128)S(1)}, f32[3,32,512]{2,1,0:T(8,128)}, u32[]{:S(2)}) copy-start(f32[3,32,512]{2,1,0:T(8,128)} %refs_7_.3) | copy-start | bytes 589828
  71.2 5.6 %copy-start.2 = (f32[3,32,512]{2,1,0:T(8,128)S(1)}, f32[3,32,512]{2,1,0:T(8,128)}, u32[]{:S(2)}) copy-start(f32[3,32,512]{2,1,0:T(8,128)} %refs_8_.1) | copy-start | bytes 589828
  71.2 4.9 %collective-permute-start.26 = (bf16[2,4,2,64,384]{4,3,2,1,0:T(8,128)(2,1)S(1)}, bf16[2,4,2,64,384]{4,3,2,1,0:T(8,128)(2,1)S(1)}, u32[]{:S(2)}, u32[]{:S(2)}) collective-permute-start(bf16[2,4,2,64,384]{4,3,2,1,0:T(8,128)(2,1)S(1)} %pad_maximum_fusion), channel_id=1, source_target_pairs={{0,1},{1,0},{2,3},{3,2},{4,5},{5,4},{6,7},{7,6},{8,9},{9,8},{10,11... | collective-permute-start | bytes 2359304 | tf_op jit(solution)/shard_map/ppermute | solution.py:235
  75.0 1.8 %collective-permute-start.25 = (bf16[2,4,3,64,128]{4,3,2,1,0:T(8,128)(2,1)S(1)}, bf16[2,4,3,64,128]{4,3,2,1,0:T(8,128)(2,1)S(1)}, u32[]{:S(2)}, u32[]{:S(2)}) collective-permute-start(bf16[2,4,3,64,128]{4,3,2,1,0:T(8,128)(2,1)S(1)} %pad_maximum_fusion.2), channel_id=1, source_target_pairs={{0,1},{1,0},{2,3},{3,2},{4,5},{5,4},{6,7},{7,6},{8,9},{9,8},{10,11... | collective-permute-start | bytes 1179656 | tf_op jit(solution)/shard_map/ppermute | solution.py:235

commit v6 on v5

--- a/solution.py
+++ b/solution.py
@@ -163,9 +163,9 @@
 
 
 def last_kernel(chips, limit, *refs):
-    lows, core_low, moms, core_moms = refs[:2], refs[2], refs[3:5], refs[5]
-    basis_ref, first_ref, second_ref, *out_hbms = refs[6:12]
-    full, stepped, new_first_ref, new_second_ref, products, sems = refs[12:]
+    lows, core_lows, moms, core_moms = refs[:2], refs[2:4], refs[4:6], refs[6]
+    basis_ref, first_ref, second_ref, *out_hbms = refs[7:13]
+    full, stepped, new_first_ref, new_second_ref, products, sems = refs[13:]
     side, _, chip, core, member = places()
     height, unit = lows[0].shape[2:]
     squares = None
@@ -174,7 +174,7 @@
             column = ((side ^ dx) * 2 + (core ^ dc)) * unit
             columns = pl.ds(pl.multiple_of(column, unit), unit)
             for k in range(chips):
-                low = (core_low[dx, k] if dc else lows[dx][k]).astype(F32)
+                low = (core_lows if dc else lows)[dx][k].astype(F32)
                 square = jnp.sum((low * low).reshape(-1, 8, unit), axis=0)
                 squares = square if squares is None else squares + square
                 rows = pl.ds(pl.multiple_of((chip ^ k) * height, height), height)
@@ -342,8 +342,7 @@
     near_part = (keep_1 + near_part.astype(F32)).astype(BF)
     lows, near_part = ordered((lows, near_part))
     arrived = [by_member(lows[k], 2 * k) for k in reversed(range(1, chips))]
-    moms_x, arrived = ordered((moms_x, arrived))
-    core_moms = by_member(jnp.stack([moms, moms_x]), 1)
+    arrived = ordered(arrived)
     grad_side = by_group(near_part, 1)
     share = lows[0]
     for low in arrived:
@@ -352,17 +351,19 @@
     while bit < groups:
         sent = share.astype(BF)
         came = by_group(sent, bit)
+        moms_x, came = ordered((moms_x, came))
         share = sent.astype(F32) + came.astype(F32)
         bit *= 2
     share = share.astype(BF)
 
+    core_moms = by_member(jnp.stack([moms, moms_x]), 1)
     low_mine = [by_member(share, 2 * k) for k in reversed(range(1, chips))]
     grad_side, low_mine = ordered((grad_side, low_mine))
     low_mine = jnp.stack([share] + low_mine[::-1])
     low_side = by_group(low_mine, 1)
     mine_part = keep_0 + by_member(send_0, 1).astype(F32)
     input_grad = (mine_part + grad_side.astype(F32)).astype(BF)
-    low_core = by_member(jnp.stack([low_mine, low_side]), 1)
+    low_core = [by_member(low_mine, 1), by_member(low_side, 1)]
     new_first, new_second, updates = call(
         functools.partial(last_kernel, chips, limit),
         [(first_moment.shape, F32), (second_moment.shape, F32), ((parts, depth, hidden_size), F32)],
@@ -377,7 +378,7 @@
         4 * 3 * depth * rank * hidden_size,
         low_mine,
         low_side,
-        low_core,
+        *low_core,
         moms,
         moms_x,
         core_moms,

time: 79.6 us -> 79.1 us (level)
    ppermute x8, waiting for transfers between devices: 17 us -> 15 us  [by_group(): return lax.ppermute(value, 'group', [(i, i ^ bits) for i in range(groups)])]
    ppermute x17 -> x18, waiting for transfers between devices: 9.68 us -> 11.3 us  [by_member(): lax.ppermute(value, 'member', [(i, i ^ bits) for i in range(members)])]
    ppermute x17 -> x18, starting transfers between devices: 13.3 us -> 13.2 us  [by_member(): lax.ppermute(value, 'member', [(i, i ^ bits) for i in range(members)])]
  transfers between devices with their start and end apart: 27 -> 28, of which waited for: 12 -> 15; matrix products, arithmetic and copies ran while one was open for 2% -> 2% of each run, Pallas kernels for 5% -> 5%
where the time goes in v6:
time: 79.1 us; the launch traced here: 78.9 us
  waiting for transfers between devices  35.6 us (45%)
  starting transfers between devices  32.8 us (41%)
  Pallas kernels  8.35 us (11%)
  other arithmetic  1.34 us (2%)
    ppermute x8, waiting for transfers between devices, by_group(): return lax.ppermute(value, 'group', [(i, i ^ bits) for i in range(groups)])  15 us
    ppermute x8, starting transfers between devices, by_group(): return lax.ppermute(value, 'group', [(i, i ^ bits) for i in range(groups)])  14 us
    ppermute x18, starting transfers between devices, by_member(): lax.ppermute(value, 'member', [(i, i ^ bits) for i in range(members)])  13.2 us
    ppermute x18, waiting for transfers between devices, by_member(): lax.ppermute(value, 'member', [(i, i ^ bits) for i in range(members)])  11.3 us
    ppermute x2, waiting for transfers between devices, by_chip(): return lax.ppermute(value, ('group', 'member'), pairs)  9.25 us
    pallas_call x5, Pallas kernels, call(): pl.pallas_call(body, out_shape=[(pltpu.VMEM if pinned else jax.ShapeDtype...  8.35 us
    ppermute x2, starting transfers between devices, by_chip(): return lax.ppermute(value, ('group', 'member'), pairs)  5.68 us
  transfers between devices with their start and end apart: 28, of which 15 were waited for; matrix products, arithmetic and copies ran while one was open for 2% of the time, Pallas kernels for 5%

profile of v6, /device:TPU:0, one launch (start us, length us, event | category | flops | bytes accessed | tf_op | source)
XLA Modules:
  0.0 78.9 jit_solution(9777245836037560609)
XLA Ops:
  0.6 1.8 %shard_map.111 = (bf16[256,512]{1,0:T(8,128)(2,1)S(1)}, bf16[256,512]{1,0:T(8,128)(2,1)S(1)}, bf16[320,512]{1,0:T(8,128)(2,1)S(1)}, bf16[64,384]{1,0:T(8,128)(2,1)S(1)}, bf16[256,2048]{1,0:T(8,128)(2,1)S(1)}) custom-call(bf16[256,512]{1,0:T(8,128)(2,1)} %refs_0_.1, bf16[256,512]{1,0:T(8,128)(2,1)} %refs_1_.1, bf16[256,512]{1,0:T(8,128)(2,1)} %refs_2_.1, ...), custom_call_target="tpu_custom_call" | custom-call | bytes 4440064 | tf_op jit(solution)/shard_map/pallas_call | solution.py:26
  2.4 3.1 %collective-permute-start = (bf16[256,512]{1,0:T(8,128)(2,1)S(1)}, bf16[256,512]{1,0:T(8,128)(2,1)S(1)}, u32[]{:S(2)}, u32[]{:S(2)}) collective-permute-start(bf16[256,512]{1,0:T(8,128)(2,1)S(1)} %get-tuple-element.57), channel_id=1, source_target_pairs={{0,2},{1,3},{2,0},{3,1},{4,6},{5,7},{6,4},{7,5},{8,10},{9,11},{10,... | collective-permute-start | bytes 786440 | tf_op jit(solution)/shard_map/ppermute | solution.py:246
  5.5 1.5 %collective-permute-start.6 = (bf16[256,2048]{1,0:T(8,128)(2,1)S(1)}, bf16[256,2048]{1,0:T(8,128)(2,1)S(1)}, u32[]{:S(2)}, u32[]{:S(2)}) collective-permute-start(bf16[256,2048]{1,0:T(8,128)(2,1)S(1)} %get-tuple-element.63.refs_0_), channel_id=1, source_target_pairs={{0,8},{8,0},{16,24},{24,16},{1,9},{9,1},{17,25},{25,17},{2,10},{10... | collective-permute-start | bytes 3145736 | tf_op jit(solution)/shard_map/ppermute | solution.py:238
  7.0 2.6 %collective-permute-start.1 = (bf16[256,512]{1,0:T(8,128)(2,1)S(1)}, bf16[256,512]{1,0:T(8,128)(2,1)S(1)}, u32[]{:S(2)}, u32[]{:S(2)}) collective-permute-start(bf16[256,512]{1,0:T(8,128)(2,1)S(1)} %get-tuple-element.57), channel_id=1, source_target_pairs={{0,4},{1,5},{2,6},{3,7},{4,0},{5,1},{6,2},{7,3},{8,12},{9,13},{10,... | collective-permute-start | bytes 786440 | tf_op jit(solution)/shard_map/ppermute | solution.py:246
  9.6 4.8 %collective-permute-done.refs_6_ = bf16[256,512]{1,0:T(8,128)(2,1)S(1)} collective-permute-done((bf16[256,512]{1,0:T(8,128)(2,1)S(1)}, bf16[256,512]{1,0:T(8,128)(2,1)S(1)}, u32[]{:S(2)}, u32[]{:S(2)}) %collective-permute-start) | collective-permute-done | bytes 262176 | tf_op jit(solution)/shard_map/ppermute | solution.py:246
  14.4 3.4 %collective-permute-start.3 = (bf16[256,512]{1,0:T(8,128)(2,1)S(1)}, bf16[256,512]{1,0:T(8,128)(2,1)S(1)}, u32[]{:S(2)}, u32[]{:S(2)}) collective-permute-start(bf16[256,512]{1,0:T(8,128)(2,1)S(1)} %collective-permute-done.refs_6_), channel_id=1, source_target_pairs={{0,16},{8,24},{16,0},{24,8},{1,17},{9,25},{17,1},{25,9},{2,18},{10... | collective-permute-start | bytes 786440 | tf_op jit(solution)/shard_map/ppermute | solution.py:238
  17.8 4.5 %collective-permute-done.1.refs_7_ = bf16[256,512]{1,0:T(8,128)(2,1)S(1)} collective-permute-done((bf16[256,512]{1,0:T(8,128)(2,1)S(1)}, bf16[256,512]{1,0:T(8,128)(2,1)S(1)}, u32[]{:S(2)}, u32[]{:S(2)}) %collective-permute-start.1) | collective-permute-done | bytes 262176 | tf_op jit(solution)/shard_map/ppermute | solution.py:246
  22.3 0.9 %collective-permute-start.5 = (bf16[256,512]{1,0:T(8,128)(2,1)S(1)}, bf16[256,512]{1,0:T(8,128)(2,1)S(1)}, u32[]{:S(2)}, u32[]{:S(2)}) collective-permute-start(bf16[256,512]{1,0:T(8,128)(2,1)S(1)} %collective-permute-done.1.refs_7_), channel_id=1, source_target_pairs={{0,16},{8,24},{16,0},{24,8},{1,17},{9,25},{17,1},{25,9},{2,18},{10... | collective-permute-start | bytes 786440 | tf_op jit(solution)/shard_map/ppermute | solution.py:238
  23.3 1.3 %collective-permute-done.3.refs_9_ = bf16[256,512]{1,0:T(8,128)(2,1)S(1)} collective-permute-done((bf16[256,512]{1,0:T(8,128)(2,1)S(1)}, bf16[256,512]{1,0:T(8,128)(2,1)S(1)}, u32[]{:S(2)}, u32[]{:S(2)}) %collective-permute-start.3) | collective-permute-done | bytes 262176 | tf_op jit(solution)/shard_map/ppermute | solution.py:238
  24.6 1.7 %collective-permute-start.7 = (bf16[1,2,64,384]{3,2,1,0:T(8,128)(2,1)S(1)}, bf16[1,2,64,384]{3,2,1,0:T(8,128)(2,1)S(1)}, u32[]{:S(2)}, u32[]{:S(2)}) collective-permute-start(bf16[1,2,64,384]{3,2,1,0:T(8,128)(2,1)S(1)} %maximum_bitcast_fusion), channel_id=1, source_target_pairs={{0,4},{1,5},{2,6},{3,7},{4,0},{5,1},{6,2},{7,3},{8,12},{9,13},{10,... | collective-permute-start | bytes 294920 | tf_op jit(solution)/shard_map/ppermute | solution.py:235
  26.3 4.0 %collective-permute-done.7 = bf16[1,2,64,384]{3,2,1,0:T(8,128)(2,1)S(1)} collective-permute-done((bf16[1,2,64,384]{3,2,1,0:T(8,128)(2,1)S(1)}, bf16[1,2,64,384]{3,2,1,0:T(8,128)(2,1)S(1)}, u32[]{:S(2)}, u32[]{:S(2)}) %collective-permute-start.7) | collective-permute-done | bytes 98336 | tf_op jit(solution)/shard_map/ppermute | solution.py:235
  30.3 2.0 %collective-permute-done.2.refs_8_ = bf16[256,512]{1,0:T(8,128)(2,1)S(1)} collective-permute-done((bf16[256,512]{1,0:T(8,128)(2,1)S(1)}, bf16[256,512]{1,0:T(8,128)(2,1)S(1)}, u32[]{:S(2)}, u32[]{:S(2)}) %collective-permute-start.2) | collective-permute-done | bytes 262176 | tf_op jit(solution)/shard_map/ppermute | solution.py:235
  32.9 1.3 %collective-permute-start.8 = (bf16[256,512]{1,0:T(8,128)(2,1)S(1)}, bf16[256,512]{1,0:T(8,128)(2,1)S(1)}, u32[]{:S(2)}, u32[]{:S(2)}) collective-permute-start(bf16[256,512]{1,0:T(8,128)(2,1)S(1)} %collective-permute-done.2.refs_8_), channel_id=1, source_target_pairs={{0,16},{8,24},{16,0},{24,8},{1,17},{9,25},{17,1},{25,9},{2,18},{10... | collective-permute-start | bytes 786440 | tf_op jit(solution)/shard_map/ppermute | solution.py:238
  34.2 1.4 %collective-permute-start.11 = (bf16[2,2,64,384]{3,2,1,0:T(8,128)(2,1)S(1)}, bf16[2,2,64,384]{3,2,1,0:T(8,128)(2,1)S(1)}, u32[]{:S(2)}, u32[]{:S(2)}) collective-permute-start(bf16[2,2,64,384]{3,2,1,0:T(8,128)(2,1)S(1)} %pad_maximum_fusion.2), channel_id=1, source_target_pairs={{0,2},{1,3},{2,0},{3,1},{4,6},{5,7},{6,4},{7,5},{8,10},{9,11},{10,... | collective-permute-start | bytes 589832 | tf_op jit(solution)/shard_map/ppermute | solution.py:235
  35.6 5.5 %collective-permute-done.8.refs_11_ = bf16[256,512]{1,0:T(8,128)(2,1)S(1)} collective-permute-done((bf16[256,512]{1,0:T(8,128)(2,1)S(1)}, bf16[256,512]{1,0:T(8,128)(2,1)S(1)}, u32[]{:S(2)}, u32[]{:S(2)}) %collective-permute-start.8) | collective-permute-done | bytes 262176 | tf_op jit(solution)/shard_map/ppermute | solution.py:238
  41.2 2.0 %shard_map.112 = (bf16[512,256]{1,0:T(8,128)(2,1)S(1)}, bf16[512,256]{1,0:T(8,128)(2,1)S(1)}, bf16[512,128]{1,0:T(8,128)(2,1)S(1)}, bf16[2048,512]{1,0:T(8,128)(2,1)S(1)}) custom-call(bf16[256,2048]{1,0:T(8,128)(2,1)S(1)} %get-tuple-element.63.refs_0_, bf16[256,2048]{1,0:T(8,128)(2,1)S(1)} %collective-permute-done.9.refs_1_, ...), custom_call_target="tpu_custom_call" | custom-call | flops 1342177280 | bytes 9109504 | tf_op jit(solution)/shard_map/pallas_call | solution.py:26
  43.3 1.5 %shard_map.113 = (f32[128,2048]{1,0:T(8,128)S(1)}, f32[128,2048]{1,0:T(8,128)S(1)}, bf16[128,2048]{1,0:T(8,128)(2,1)S(1)}, bf16[128,2048]{1,0:T(8,128)(2,1)S(1)}) custom-call(bf16[512,256]{1,0:T(8,128)(2,1)S(1)} %get-tuple-element.78.dgu_ref, bf16[2048,512]{1,0:T(8,128)(2,1)S(1)} %get-tuple-element.79.full_ref), custom_call_target="tpu_custom_call" | custom-call | flops 536870912 | bytes 5505024 | tf_op jit(solution)/shard_map/pallas_call | solution.py:26
  45.3 2.3 %collective-permute-start.19 = (bf16[4,2,64,384]{3,2,1,0:T(8,128)(2,1)S(1)}, bf16[4,2,64,384]{3,2,1,0:T(8,128)(2,1)S(1)}, u32[]{:S(2)}, u32[]{:S(2)}) collective-permute-start(bf16[4,2,64,384]{3,2,1,0:T(8,128)(2,1)S(1)} %pad_maximum_fusion.1.refs_4_), channel_id=1, source_target_pairs={{0,8},{8,0},{16,24},{24,16},{1,9},{9,1},{17,25},{25,17},{2,10},{10... | collective-permute-start | bytes 1179656 | tf_op jit(solution)/shard_map/ppermute | solution.py:238
  48.2 2.0 %collective-permute-start.16 = (bf16[3,64,128]{2,1,0:T(8,128)(2,1)S(1)}, bf16[3,64,128]{2,1,0:T(8,128)(2,1)S(1)}, u32[]{:S(2)}, u32[]{:S(2)}) collective-permute-start(bf16[3,64,128]{2,1,0:T(8,128)(2,1)S(1)} %get-tuple-element.94), channel_id=1, source_target_pairs={{0,6},{1,7},{2,4},{3,5},{4,2},{5,3},{6,0},{7,1},{8,14},{9,15},{10,... | collective-permute-start | bytes 147464 | tf_op jit(solution)/shard_map/ppermute | solution.py:235
  50.2 2.4 %collective-permute-start.18 = (bf16[3,64,128]{2,1,0:T(8,128)(2,1)S(1)}, bf16[3,64,128]{2,1,0:T(8,128)(2,1)S(1)}, u32[]{:S(2)}, u32[]{:S(2)}) collective-permute-start(bf16[3,64,128]{2,1,0:T(8,128)(2,1)S(1)} %get-tuple-element.96), channel_id=1, source_target_pairs={{0,2},{1,3},{2,0},{3,1},{4,6},{5,7},{6,4},{7,5},{8,10},{9,11},{10,... | collective-permute-start | bytes 147464 | tf_op jit(solution)/shard_map/ppermute | solution.py:235
  52.6 1.2 %collective-permute-start.15 = (bf16[128,2048]{1,0:T(8,128)(2,1)S(1)}, bf16[128,2048]{1,0:T(8,128)(2,1)S(1)}, u32[]{:S(2)}, u32[]{:S(2)}) collective-permute-start(bf16[128,2048]{1,0:T(8,128)(2,1)S(1)} %add_convert_fusion.1), channel_id=1, source_target_pairs={{0,8},{8,0},{16,24},{24,16},{1,9},{9,1},{17,25},{25,17},{2,10},{10... | collective-permute-start | bytes 1572872 | tf_op jit(solution)/shard_map/ppermute | solution.py:238
  54.1 1.5 %collective-permute-done.17 = bf16[3,64,128]{2,1,0:T(8,128)(2,1)S(1)} collective-permute-done((bf16[3,64,128]{2,1,0:T(8,128)(2,1)S(1)}, bf16[3,64,128]{2,1,0:T(8,128)(2,1)S(1)}, u32[]{:S(2)}, u32[]{:S(2)}) %collective-permute-start.17) | collective-permute-done | bytes 49184 | tf_op jit(solution)/shard_map/ppermute | solution.py:235
  55.7 1.5 %collective-permute-start.20 = (bf16[3,64,128]{2,1,0:T(8,128)(2,1)S(1)}, bf16[3,64,128]{2,1,0:T(8,128)(2,1)S(1)}, u32[]{:S(2)}, u32[]{:S(2)}) collective-permute-start(bf16[3,64,128]{2,1,0:T(8,128)(2,1)S(1)} %add_convert_fusion.3), channel_id=1, source_target_pairs={{0,16},{8,24},{16,0},{24,8},{1,17},{9,25},{17,1},{25,9},{2,18},{10... | collective-permute-start | bytes 147464 | tf_op jit(solution)/shard_map/ppermute | solution.py:238
  57.6 2.2 %collective-permute-done.20 = bf16[3,64,128]{2,1,0:T(8,128)(2,1)S(1)} collective-permute-done((bf16[3,64,128]{2,1,0:T(8,128)(2,1)S(1)}, bf16[3,64,128]{2,1,0:T(8,128)(2,1)S(1)}, u32[]{:S(2)}, u32[]{:S(2)}) %collective-permute-start.20) | collective-permute-done | bytes 49184 | tf_op jit(solution)/shard_map/ppermute | solution.py:238
  59.8 2.0 %collective-permute-start.21 = (bf16[3,64,128]{2,1,0:T(8,128)(2,1)S(1)}, bf16[3,64,128]{2,1,0:T(8,128)(2,1)S(1)}, u32[]{:S(2)}, u32[]{:S(2)}) collective-permute-start(bf16[3,64,128]{2,1,0:T(8,128)(2,1)S(1)} %add_convert_fusion.2), channel_id=1, source_target_pairs={{0,6},{1,7},{2,4},{3,5},{4,2},{5,3},{6,0},{7,1},{8,14},{9,15},{10,... | collective-permute-start | bytes 147464 | tf_op jit(solution)/shard_map/ppermute | solution.py:235
  62.5 1.8 %collective-permute-start.23 = (bf16[3,64,128]{2,1,0:T(8,128)(2,1)S(1)}, bf16[3,64,128]{2,1,0:T(8,128)(2,1)S(1)}, u32[]{:S(2)}, u32[]{:S(2)}) collective-permute-start(bf16[3,64,128]{2,1,0:T(8,128)(2,1)S(1)} %add_convert_fusion.2), channel_id=1, source_target_pairs={{0,2},{1,3},{2,0},{3,1},{4,6},{5,7},{6,4},{7,5},{8,10},{9,11},{10,... | collective-permute-start | bytes 147464 | tf_op jit(solution)/shard_map/ppermute | solution.py:235
  64.4 1.9 %collective-permute-done.21 = bf16[3,64,128]{2,1,0:T(8,128)(2,1)S(1)} collective-permute-done((bf16[3,64,128]{2,1,0:T(8,128)(2,1)S(1)}, bf16[3,64,128]{2,1,0:T(8,128)(2,1)S(1)}, u32[]{:S(2)}, u32[]{:S(2)}) %collective-permute-start.21) | collective-permute-done | bytes 49184 | tf_op jit(solution)/shard_map/ppermute | solution.py:235
  66.3 1.1 %collective-permute-done.22 = bf16[3,64,128]{2,1,0:T(8,128)(2,1)S(1)} collective-permute-done((bf16[3,64,128]{2,1,0:T(8,128)(2,1)S(1)}, bf16[3,64,128]{2,1,0:T(8,128)(2,1)S(1)}, u32[]{:S(2)}, u32[]{:S(2)}) %collective-permute-start.22) | collective-permute-done | bytes 49184 | tf_op jit(solution)/shard_map/ppermute | solution.py:235
  68.3 1.8 %collective-permute-start.24 = (bf16[4,3,64,128]{3,2,1,0:T(8,128)(2,1)S(1)}, bf16[4,3,64,128]{3,2,1,0:T(8,128)(2,1)S(1)}, u32[]{:S(2)}, u32[]{:S(2)}) collective-permute-start(bf16[4,3,64,128]{3,2,1,0:T(8,128)(2,1)S(1)} %pad_maximum_fusion.3.refs_0_), channel_id=1, source_target_pairs={{0,8},{8,0},{16,24},{24,16},{1,9},{9,1},{17,25},{25,17},{2,10},{10... | collective-permute-start | bytes 589832 | tf_op jit(solution)/shard_map/ppermute | solution.py:238
  70.1 4.6 %collective-permute-done.24.refs_1_ = bf16[4,3,64,128]{3,2,1,0:T(8,128)(2,1)S(1)} collective-permute-done((bf16[4,3,64,128]{3,2,1,0:T(8,128)(2,1)S(1)}, bf16[4,3,64,128]{3,2,1,0:T(8,128)(2,1)S(1)}, u32[]{:S(2)}, u32[]{:S(2)}) %collective-permute-start.24) | collective-permute-done | bytes 196640 | tf_op jit(solution)/shard_map/ppermute | solution.py:238
  74.7 1.0 %add_convert_fusion = bf16[128,2048]{1,0:T(8,128)(2,1)} fusion(bf16[128,2048]{1,0:T(8,128)(2,1)S(1)} %collective-permute-done.15, f32[128,2048]{1,0:T(8,128)S(1)} %get-tuple-element.80, bf16[128,2048]{1,0:T(8,128)(2,1)S(1)} %collective-permute-done.12), kind=kLoop, calls=%fused_computation | loop fusion | flops 1310720 | bytes 2621440 | tf_op jit(solution)/shard_map/convert_element_type | solution.py:365
  76.2 2.7 %shard_map.115 = (f32[3,32,512]{2,1,0:T(8,128)}, f32[3,32,512]{2,1,0:T(8,128)}, f32[3,256,512]{2,1,0:T(8,128)}) custom-call(bf16[4,3,64,128]{3,2,1,0:T(8,128)(2,1)S(1)} %pad_maximum_fusion.3.refs_0_, bf16[4,3,64,128]{3,2,1,0:T(8,128)(2,1)S(1)} %collective-permute-done.24.refs_1_, bf16[4,3,64,128]{3,2,1,0:T(8,128)(2,1)S(1)} %collective-permute-done.25.refs_2_, ...), custom_call_target="tpu_custom_call" | custom-call | flops 402653184 | bytes 4980736 | tf_op jit(solution)/shard_map/pallas_call | solution.py:26
  (45 shorter events, 4.6 us)
Async XLA Ops:
  2.4 12.0 %collective-permute-start = (bf16[256,512]{1,0:T(8,128)(2,1)S(1)}, bf16[256,512]{1,0:T(8,128)(2,1)S(1)}, u32[]{:S(2)}, u32[]{:S(2)}) collective-permute-start(bf16[256,512]{1,0:T(8,128)(2,1)S(1)} %get-tuple-element.57), channel_id=1, source_target_pairs={{0,2},{1,3},{2,0},{3,1},{4,6},{5,7},{6,4},{7,5},{8,10},{9,11},{10,... | collective-permute-start | bytes 786440 | tf_op jit(solution)/shard_map/ppermute | solution.py:246
  5.5 26.8 %collective-permute-start.6 = (bf16[256,2048]{1,0:T(8,128)(2,1)S(1)}, bf16[256,2048]{1,0:T(8,128)(2,1)S(1)}, u32[]{:S(2)}, u32[]{:S(2)}) collective-permute-start(bf16[256,2048]{1,0:T(8,128)(2,1)S(1)} %get-tuple-element.63.refs_0_), channel_id=1, source_target_pairs={{0,8},{8,0},{16,24},{24,16},{1,9},{9,1},{17,25},{25,17},{2,10},{10... | collective-permute-start | bytes 3145736 | tf_op jit(solution)/shard_map/ppermute | solution.py:238
  7.0 16.2 %collective-permute-start.4 = (bf16[320,512]{1,0:T(8,128)(2,1)S(1)}, bf16[320,512]{1,0:T(8,128)(2,1)S(1)}, u32[]{:S(2)}, u32[]{:S(2)}) collective-permute-start(bf16[320,512]{1,0:T(8,128)(2,1)S(1)} %get-tuple-element.58), channel_id=1, source_target_pairs={{0,1},{1,0},{2,3},{3,2},{4,5},{5,4},{6,7},{7,6},{8,9},{9,8},{10,11... | collective-permute-start | bytes 983048 | tf_op jit(solution)/shard_map/ppermute | solution.py:235
  7.0 15.3 %collective-permute-start.1 = (bf16[256,512]{1,0:T(8,128)(2,1)S(1)}, bf16[256,512]{1,0:T(8,128)(2,1)S(1)}, u32[]{:S(2)}, u32[]{:S(2)}) collective-permute-start(bf16[256,512]{1,0:T(8,128)(2,1)S(1)} %get-tuple-element.57), channel_id=1, source_target_pairs={{0,4},{1,5},{2,6},{3,7},{4,0},{5,1},{6,2},{7,3},{8,12},{9,13},{10,... | collective-permute-start | bytes 786440 | tf_op jit(solution)/shard_map/ppermute | solution.py:246
  14.4 10.2 %collective-permute-start.3 = (bf16[256,512]{1,0:T(8,128)(2,1)S(1)}, bf16[256,512]{1,0:T(8,128)(2,1)S(1)}, u32[]{:S(2)}, u32[]{:S(2)}) collective-permute-start(bf16[256,512]{1,0:T(8,128)(2,1)S(1)} %collective-permute-done.refs_6_), channel_id=1, source_target_pairs={{0,16},{8,24},{16,0},{24,8},{1,17},{9,25},{17,1},{25,9},{2,18},{10... | collective-permute-start | bytes 786440 | tf_op jit(solution)/shard_map/ppermute | solution.py:238
  22.3 10.0 %collective-permute-start.2 = (bf16[256,512]{1,0:T(8,128)(2,1)S(1)}, bf16[256,512]{1,0:T(8,128)(2,1)S(1)}, u32[]{:S(2)}, u32[]{:S(2)}) collective-permute-start(bf16[256,512]{1,0:T(8,128)(2,1)S(1)} %collective-permute-done.1.refs_7_), channel_id=1, source_target_pairs={{0,2},{1,3},{2,0},{3,1},{4,6},{5,7},{6,4},{7,5},{8,10},{9,11},{10,... | collective-permute-start | bytes 786440 | tf_op jit(solution)/shard_map/ppermute | solution.py:235
  22.3 10.0 %collective-permute-start.5 = (bf16[256,512]{1,0:T(8,128)(2,1)S(1)}, bf16[256,512]{1,0:T(8,128)(2,1)S(1)}, u32[]{:S(2)}, u32[]{:S(2)}) collective-permute-start(bf16[256,512]{1,0:T(8,128)(2,1)S(1)} %collective-permute-done.1.refs_7_), channel_id=1, source_target_pairs={{0,16},{8,24},{16,0},{24,8},{1,17},{9,25},{17,1},{25,9},{2,18},{10... | collective-permute-start | bytes 786440 | tf_op jit(solution)/shard_map/ppermute | solution.py:238
  24.6 5.7 %collective-permute-start.7 = (bf16[1,2,64,384]{3,2,1,0:T(8,128)(2,1)S(1)}, bf16[1,2,64,384]{3,2,1,0:T(8,128)(2,1)S(1)}, u32[]{:S(2)}, u32[]{:S(2)}) collective-permute-start(bf16[1,2,64,384]{3,2,1,0:T(8,128)(2,1)S(1)} %maximum_bitcast_fusion), channel_id=1, source_target_pairs={{0,4},{1,5},{2,6},{3,7},{4,0},{5,1},{6,2},{7,3},{8,12},{9,13},{10,... | collective-permute-start | bytes 294920 | tf_op jit(solution)/shard_map/ppermute | solution.py:235
  32.4 8.8 %collective-permute-start.9 = (bf16[256,2048]{1,0:T(8,128)(2,1)S(1)}, bf16[256,2048]{1,0:T(8,128)(2,1)S(1)}, u32[]{:S(2)}, u32[]{:S(2)}) collective-permute-start(bf16[256,2048]{1,0:T(8,128)(2,1)S(1)} %get-tuple-element.63.refs_0_), channel_id=1, source_target_pairs={{0,1},{1,0},{2,3},{3,2},{4,5},{5,4},{6,7},{7,6},{8,9},{9,8},{10,11... | collective-permute-start | bytes 3145736 | tf_op jit(solution)/shard_map/ppermute | solution.py:235
  32.4 8.8 %collective-permute-start.10 = (bf16[256,2048]{1,0:T(8,128)(2,1)S(1)}, bf16[256,2048]{1,0:T(8,128)(2,1)S(1)}, u32[]{:S(2)}, u32[]{:S(2)}) collective-permute-start(bf16[256,2048]{1,0:T(8,128)(2,1)S(1)} %collective-permute-done.6.refs_2_), channel_id=1, source_target_pairs={{0,1},{1,0},{2,3},{3,2},{4,5},{5,4},{6,7},{7,6},{8,9},{9,8},{10,11... | collective-permute-start | bytes 3145736 | tf_op jit(solution)/shard_map/ppermute | solution.py:235
  32.9 8.3 %collective-permute-start.8 = (bf16[256,512]{1,0:T(8,128)(2,1)S(1)}, bf16[256,512]{1,0:T(8,128)(2,1)S(1)}, u32[]{:S(2)}, u32[]{:S(2)}) collective-permute-start(bf16[256,512]{1,0:T(8,128)(2,1)S(1)} %collective-permute-done.2.refs_8_), channel_id=1, source_target_pairs={{0,16},{8,24},{16,0},{24,8},{1,17},{9,25},{17,1},{25,9},{2,18},{10... | collective-permute-start | bytes 786440 | tf_op jit(solution)/shard_map/ppermute | solution.py:238
  34.2 9.0 %collective-permute-start.11 = (bf16[2,2,64,384]{3,2,1,0:T(8,128)(2,1)S(1)}, bf16[2,2,64,384]{3,2,1,0:T(8,128)(2,1)S(1)}, u32[]{:S(2)}, u32[]{:S(2)}) collective-permute-start(bf16[2,2,64,384]{3,2,1,0:T(8,128)(2,1)S(1)} %pad_maximum_fusion.2), channel_id=1, source_target_pairs={{0,2},{1,3},{2,0},{3,1},{4,6},{5,7},{6,4},{7,5},{8,10},{9,11},{10,... | collective-permute-start | bytes 589832 | tf_op jit(solution)/shard_map/ppermute | solution.py:235
  43.1 1.6 %collective-permute-start.13 = (bf16[512,256]{1,0:T(8,128)(2,1)S(1)}, bf16[512,256]{1,0:T(8,128)(2,1)S(1)}, u32[]{:S(2)}, u32[]{:S(2)}) collective-permute-start(bf16[512,256]{1,0:T(8,128)(2,1)S(1)} %get-tuple-element.82.mine_ref), channel_id=1, source_target_pairs={{0,1},{1,0},{2,3},{3,2},{4,5},{5,4},{6,7},{7,6},{8,9},{9,8},{10,11... | collective-permute-start | bytes 786440 | tf_op jit(solution)/shard_map/ppermute | solution.py:235
  44.8 3.3 %collective-permute-start.14 = (bf16[128,2048]{1,0:T(8,128)(2,1)S(1)}, bf16[128,2048]{1,0:T(8,128)(2,1)S(1)}, u32[]{:S(2)}, u32[]{:S(2)}) collective-permute-start(bf16[128,2048]{1,0:T(8,128)(2,1)S(1)} %get-tuple-element.91), channel_id=1, source_target_pairs={{0,1},{1,0},{2,3},{3,2},{4,5},{5,4},{6,7},{7,6},{8,9},{9,8},{10,11... | collective-permute-start | bytes 1572872 | tf_op jit(solution)/shard_map/ppermute | solution.py:235
  45.3 12.2 %collective-permute-start.19 = (bf16[4,2,64,384]{3,2,1,0:T(8,128)(2,1)S(1)}, bf16[4,2,64,384]{3,2,1,0:T(8,128)(2,1)S(1)}, u32[]{:S(2)}, u32[]{:S(2)}) collective-permute-start(bf16[4,2,64,384]{3,2,1,0:T(8,128)(2,1)S(1)} %pad_maximum_fusion.1.refs_4_), channel_id=1, source_target_pairs={{0,8},{8,0},{16,24},{24,16},{1,9},{9,1},{17,25},{25,17},{2,10},{10... | collective-permute-start | bytes 1179656 | tf_op jit(solution)/shard_map/ppermute | solution.py:238
  48.2 6.0 %collective-permute-start.16 = (bf16[3,64,128]{2,1,0:T(8,128)(2,1)S(1)}, bf16[3,64,128]{2,1,0:T(8,128)(2,1)S(1)}, u32[]{:S(2)}, u32[]{:S(2)}) collective-permute-start(bf16[3,64,128]{2,1,0:T(8,128)(2,1)S(1)} %get-tuple-element.94), channel_id=1, source_target_pairs={{0,6},{1,7},{2,4},{3,5},{4,2},{5,3},{6,0},{7,1},{8,14},{9,15},{10,... | collective-permute-start | bytes 147464 | tf_op jit(solution)/shard_map/ppermute | solution.py:235
  50.2 5.4 %collective-permute-start.17 = (bf16[3,64,128]{2,1,0:T(8,128)(2,1)S(1)}, bf16[3,64,128]{2,1,0:T(8,128)(2,1)S(1)}, u32[]{:S(2)}, u32[]{:S(2)}) collective-permute-start(bf16[3,64,128]{2,1,0:T(8,128)(2,1)S(1)} %get-tuple-element.95), channel_id=1, source_target_pairs={{0,4},{1,5},{2,6},{3,7},{4,0},{5,1},{6,2},{7,3},{8,12},{9,13},{10,... | collective-permute-start | bytes 147464 | tf_op jit(solution)/shard_map/ppermute | solution.py:235
  50.2 5.4 %collective-permute-start.18 = (bf16[3,64,128]{2,1,0:T(8,128)(2,1)S(1)}, bf16[3,64,128]{2,1,0:T(8,128)(2,1)S(1)}, u32[]{:S(2)}, u32[]{:S(2)}) collective-permute-start(bf16[3,64,128]{2,1,0:T(8,128)(2,1)S(1)} %get-tuple-element.96), channel_id=1, source_target_pairs={{0,2},{1,3},{2,0},{3,1},{4,6},{5,7},{6,4},{7,5},{8,10},{9,11},{10,... | collective-permute-start | bytes 147464 | tf_op jit(solution)/shard_map/ppermute | solution.py:235
  52.6 15.6 %collective-permute-start.15 = (bf16[128,2048]{1,0:T(8,128)(2,1)S(1)}, bf16[128,2048]{1,0:T(8,128)(2,1)S(1)}, u32[]{:S(2)}, u32[]{:S(2)}) collective-permute-start(bf16[128,2048]{1,0:T(8,128)(2,1)S(1)} %add_convert_fusion.1), channel_id=1, source_target_pairs={{0,8},{8,0},{16,24},{24,16},{1,9},{9,1},{17,25},{25,17},{2,10},{10... | collective-permute-start | bytes 1572872 | tf_op jit(solution)/shard_map/ppermute | solution.py:238
  55.7 4.2 %collective-permute-start.20 = (bf16[3,64,128]{2,1,0:T(8,128)(2,1)S(1)}, bf16[3,64,128]{2,1,0:T(8,128)(2,1)S(1)}, u32[]{:S(2)}, u32[]{:S(2)}) collective-permute-start(bf16[3,64,128]{2,1,0:T(8,128)(2,1)S(1)} %add_convert_fusion.3), channel_id=1, source_target_pairs={{0,16},{8,24},{16,0},{24,8},{1,17},{9,25},{17,1},{25,9},{2,18},{10... | collective-permute-start | bytes 147464 | tf_op jit(solution)/shard_map/ppermute | solution.py:238
  57.2 17.6 %collective-permute-start.12 = (bf16[128,2048]{1,0:T(8,128)(2,1)S(1)}, bf16[128,2048]{1,0:T(8,128)(2,1)S(1)}, u32[]{:S(2)}, u32[]{:S(2)}) collective-permute-start(bf16[128,2048]{1,0:T(8,128)(2,1)S(1)} %get-tuple-element.81), channel_id=1, source_target_pairs={{0,1},{1,0},{2,3},{3,2},{4,5},{5,4},{6,7},{7,6},{8,9},{9,8},{10,11... | collective-permute-start | bytes 1572872 | tf_op jit(solution)/shard_map/ppermute | solution.py:235
  59.8 6.4 %collective-permute-start.21 = (bf16[3,64,128]{2,1,0:T(8,128)(2,1)S(1)}, bf16[3,64,128]{2,1,0:T(8,128)(2,1)S(1)}, u32[]{:S(2)}, u32[]{:S(2)}) collective-permute-start(bf16[3,64,128]{2,1,0:T(8,128)(2,1)S(1)} %add_convert_fusion.2), channel_id=1, source_target_pairs={{0,6},{1,7},{2,4},{3,5},{4,2},{5,3},{6,0},{7,1},{8,14},{9,15},{10,... | collective-permute-start | bytes 147464 | tf_op jit(solution)/shard_map/ppermute | solution.py:235
  61.9 5.5 %collective-permute-start.22 = (bf16[3,64,128]{2,1,0:T(8,128)(2,1)S(1)}, bf16[3,64,128]{2,1,0:T(8,128)(2,1)S(1)}, u32[]{:S(2)}, u32[]{:S(2)}) collective-permute-start(bf16[3,64,128]{2,1,0:T(8,128)(2,1)S(1)} %add_convert_fusion.2), channel_id=1, source_target_pairs={{0,4},{1,5},{2,6},{3,7},{4,0},{5,1},{6,2},{7,3},{8,12},{9,13},{10,... | collective-permute-start | bytes 147464 | tf_op jit(solution)/shard_map/ppermute | solution.py:235
  62.5 4.9 %collective-permute-start.23 = (bf16[3,64,128]{2,1,0:T(8,128)(2,1)S(1)}, bf16[3,64,128]{2,1,0:T(8,128)(2,1)S(1)}, u32[]{:S(2)}, u32[]{:S(2)}) collective-permute-start(bf16[3,64,128]{2,1,0:T(8,128)(2,1)S(1)} %add_convert_fusion.2), channel_id=1, source_target_pairs={{0,2},{1,3},{2,0},{3,1},{4,6},{5,7},{6,4},{7,5},{8,10},{9,11},{10,... | collective-permute-start | bytes 147464 | tf_op jit(solution)/shard_map/ppermute | solution.py:235
  64.3 11.9 %copy-start = (f32[256,256]{1,0:T(8,128)S(1)}, f32[256,256]{1,0:T(8,128)}, u32[]{:S(2)}) copy-start(f32[256,256]{1,0:T(8,128)} %refs_7_.3) | copy-start | bytes 786436
  64.3 11.9 %copy-start.1 = (f32[3,32,512]{2,1,0:T(8,128)S(1)}, f32[3,32,512]{2,1,0:T(8,128)}, u32[]{:S(2)}) copy-start(f32[3,32,512]{2,1,0:T(8,128)} %refs_8_.1) | copy-start | bytes 589828
  64.3 11.9 %copy-start.2 = (f32[3,32,512]{2,1,0:T(8,128)S(1)}, f32[3,32,512]{2,1,0:T(8,128)}, u32[]{:S(2)}) copy-start(f32[3,32,512]{2,1,0:T(8,128)} %refs_9_.1) | copy-start | bytes 589828
  66.3 9.4 %collective-permute-start.27 = (bf16[2,4,2,64,384]{4,3,2,1,0:T(8,128)(2,1)S(1)}, bf16[2,4,2,64,384]{4,3,2,1,0:T(8,128)(2,1)S(1)}, u32[]{:S(2)}, u32[]{:S(2)}) collective-permute-start(bf16[2,4,2,64,384]{4,3,2,1,0:T(8,128)(2,1)S(1)} %pad_maximum_fusion), channel_id=1, source_target_pairs={{0,1},{1,0},{2,3},{3,2},{4,5},{5,4},{6,7},{7,6},{8,9},{9,8},{10,11... | collective-permute-start | bytes 2359304 | tf_op jit(solution)/shard_map/ppermute | solution.py:235
  68.3 6.4 %collective-permute-start.24 = (bf16[4,3,64,128]{3,2,1,0:T(8,128)(2,1)S(1)}, bf16[4,3,64,128]{3,2,1,0:T(8,128)(2,1)S(1)}, u32[]{:S(2)}, u32[]{:S(2)}) collective-permute-start(bf16[4,3,64,128]{3,2,1,0:T(8,128)(2,1)S(1)} %pad_maximum_fusion.3.refs_0_), channel_id=1, source_target_pairs={{0,8},{8,0},{16,24},{24,16},{1,9},{9,1},{17,25},{25,17},{2,10},{10... | collective-permute-start | bytes 589832 | tf_op jit(solution)/shard_map/ppermute | solution.py:238
  70.1 5.6 %collective-permute-start.25 = (bf16[4,3,64,128]{3,2,1,0:T(8,128)(2,1)S(1)}, bf16[4,3,64,128]{3,2,1,0:T(8,128)(2,1)S(1)}, u32[]{:S(2)}, u32[]{:S(2)}) collective-permute-start(bf16[4,3,64,128]{3,2,1,0:T(8,128)(2,1)S(1)} %pad_maximum_fusion.3.refs_0_), channel_id=1, source_target_pairs={{0,1},{1,0},{2,3},{3,2},{4,5},{5,4},{6,7},{7,6},{8,9},{9,8},{10,11... | collective-permute-start | bytes 589832 | tf_op jit(solution)/shard_map/ppermute | solution.py:235
  74.7 1.4 %collective-permute-start.26 = (bf16[4,3,64,128]{3,2,1,0:T(8,128)(2,1)S(1)}, bf16[4,3,64,128]{3,2,1,0:T(8,128)(2,1)S(1)}, u32[]{:S(2)}, u32[]{:S(2)}) collective-permute-start(bf16[4,3,64,128]{3,2,1,0:T(8,128)(2,1)S(1)} %collective-permute-done.24.refs_1_), channel_id=1, source_target_pairs={{0,1},{1,0},{2,3},{3,2},{4,5},{5,4},{6,7},{7,6},{8,9},{9,8},{10,11... | collective-permute-start | bytes 589832 | tf_op jit(solution)/shard_map/ppermute | solution.py:235
